TPU v7x, 256 devices: a whole 4x4x8 slice. The times are simulated.
256 devices in a mesh: panel: 2 (over core), gx: 32 (over x, z), gy: 4 (over y).
Axes of the slice: x: 4, y: 4, z: 8, core: 2. Of those that a mesh axis runs over, the one named last changes fastest.
Arguments:
- model_state: float32 [2, 2048, 40, 512], P('panel', 'gx', None, 'gy'), may hold values from -6 to 6
- depart_frac: float32 [2, 2048, 512], P('panel', 'gx', 'gy'), may hold values from 0 to 1
- depart_cell: int32 [2, 2048, 512], P('panel', 'gx', 'gy'), may hold values from 1 to 125
- row_source: int32 [2, 8192], P('panel', ('gx', 'gy')), may hold values from 0 to 255, as said below
- send_block: int32 [2, 128, 128, 2], P('panel', ('gx', 'gy')), may hold values from -1 to 63, as said below
- strip_from: int32 [2, 128, 512], P('panel', ('gx', 'gy')), may hold values from 0 to 8191
- strip_into: int32 [2, 128, 512], P('panel', ('gx', 'gy')), may hold values from 0 to 8191, as said below
- helmholtz_coef: float32 [40], replicated, may hold values from 0.25 to 4
- vertical_mix: float32 [40, 40], replicated, may hold values from -1 to 1
Outputs:
- balanced: float32 [2, 2048, 40, 512], P('panel', 'gx', None, 'gy')
Inputs may be any that keep to these rules, and one draw needn't show every extreme that they name: `row_source`: slot k (below 2) of source tile s is named s * 2 + k; the 64 rows of one tile name distinct slots, and every tile takes all 2 slots of itself. `send_block`: A block index, or -1 for an empty slot; exactly the slots named in row_source are filled. `strip_into`: the 512 cells of one tile are distinct.
All inputs are finite; a program needn't handle non-finite values.
Results may differ from a plain program's by a relative error of at most 0.000067.
Values sent between devices are 32-bit elements; how exact they have to be, the bound alone decides.
No kernel may reach another device: no remote copies, remote signals or barrier semaphores. Data moves between devices by JAX's collectives and lax.ppermute only.
A program may use at most 64 MiB of HBM per device.

v0:
```python
import jax
import jax.numpy as jnp
from jax import lax
from jax.sharding import PartitionSpec as P

SWEEPS = 8


def swapped(block, axis, bit):
    count = lax.axis_size(axis)
    route = []
    for low in range(count):
        high = low | 1 << bit
        if high != low and high < count:
            route += [(low, high), (high, low)]
    return lax.ppermute(block, axis, route)


def with_halo(block, sides, width):
    for axis, dim in sides:
        count = lax.axis_size(axis)
        forward = [(i, i + 1) for i in range(count - 1)]
        backward = [(target, source) for source, target in forward]
        low = lax.ppermute(
            lax.slice_in_dim(block, block.shape[dim] - width, None, axis=dim), axis, forward
        )
        high = lax.ppermute(lax.slice_in_dim(block, 0, width, axis=dim), axis, backward)
        block = jnp.concatenate([low, block, high], axis=dim)
    return block


def cubic_matrix(cell_index, fraction, cells):
    weight_a = -fraction * (fraction - 1.0) * (fraction - 2.0) / 6.0
    weight_b = (fraction + 1.0) * (fraction - 1.0) * (fraction - 2.0) / 2.0
    weight_c = -(fraction + 1.0) * fraction * (fraction - 2.0) / 2.0
    weight_d = (fraction + 1.0) * fraction * (fraction - 1.0) / 6.0
    source_cell = jnp.arange(cells, dtype=jnp.int32)[None, :, None]
    target = cell_index[:, None, :]
    banded = jnp.where(source_cell == target - 1, weight_a[:, None, :], 0.0)
    banded = banded + jnp.where(source_cell == target, weight_b[:, None, :], 0.0)
    banded = banded + jnp.where(source_cell == target + 1, weight_c[:, None, :], 0.0)
    banded = banded + jnp.where(source_cell == target + 2, weight_d[:, None, :], 0.0)
    return banded


def local(
    model_state,
    depart_frac,
    depart_cell,
    row_source,
    send_block,
    strip_from,
    strip_into,
    helmholtz_coef,
    vertical_mix,
):
    own_tile = model_state[0]
    cells = own_tile.shape[2]
    wanted = send_block[0, 0]
    present = wanted >= 0
    outgoing = jnp.where(present[:, :, None, None], own_tile[jnp.maximum(wanted, 0)], 0.0)
    coupled = jnp.einsum("xgy,gf->xfy", own_tile, vertical_mix, precision=lax.Precision.HIGHEST)
    arrived = lax.all_to_all(outgoing, ("gx", "gy"), split_axis=0, concat_axis=0, tiled=True)
    slot_rows = arrived.reshape((-1,) + own_tile.shape[1:])
    fetched = slot_rows[row_source[0]]
    banded = cubic_matrix(depart_cell[0], depart_frac[0], cells)
    interp = jnp.einsum("xgj,xjc->xgc", fetched, banded, precision=lax.Precision.HIGHEST)
    arrival = interp + 0.5 * coupled
    from_cells = strip_from[0, 0]
    strip_vals = arrival[from_cells // cells, :, from_cells % cells]
    received = swapped(strip_vals, "panel", 0)
    into_cells = strip_into[0, 0]
    merged = arrival.at[into_cells // cells, :, into_cells % cells].set(received)
    coeff = helmholtz_coef[None, :, None]
    diagonal = 1.0 + 4.0 * coeff
    balanced = merged
    for sweep_no in range(SWEEPS):
        padded = with_halo(balanced, (("gx", 0), ("gy", 2)), 1)
        neighbours = (
            padded[2:, :, 1:-1] + padded[:-2, :, 1:-1] + padded[1:-1, :, 2:] + padded[1:-1, :, :-2]
        )
        balanced = (merged + coeff * neighbours) / diagonal
    return balanced[None]


def solution(mesh):
    in_specs = (
        P("panel", "gx", None, "gy"),
        P("panel", "gx", "gy"),
        P("panel", "gx", "gy"),
        P("panel", ("gx", "gy")),
        P("panel", ("gx", "gy"), None, None),
        P("panel", ("gx", "gy"), None),
        P("panel", ("gx", "gy"), None),
        P(),
        P(),
    )
    out_specs = P("panel", "gx", None, "gy")
    return jax.shard_map(local, mesh=mesh, in_specs=in_specs, out_specs=out_specs, check_vma=False)
```

profile of v0, /device:TPU:2, one launch (start us, length us, event | category | flops | bytes accessed | tf_op | source)
XLA Modules:
  0.0 430.7 jit_solution(12381820388533806388)
XLA Ops:
  5.3 4.3 %broadcast_select_fusion = f32[128,2,40,128]{3,2,1,0:T(8,128)} fusion(f32[128,2,40,128]{3,2,1,0:T(8,128)} %bitcast.83, pred[128,2]{1,0:T(8,128)(4,1)S(1)} %copy.131), kind=kLoop, calls=%fused_computation.125 | loop fusion | flops 1310720 | bytes 10486016 | tf_op jit(solution)/shard_map/jit(_where)/select_n | solution.py:61
  9.7 16.1 %all-to-all-start = ((f32[128,2,40,128]{3,2,1,0:T(8,128)}), f32[128,2,40,128]{3,2,1,0:T(8,128)}, u32[]{:S(2)}, u32[]{:S(2)}) async-start(f32[128,2,40,128]{3,2,1,0:T(8,128)} %broadcast_select_fusion), calls=%async_computation | async-start | bytes 10485760 | tf_op jit(solution)/shard_map/all_to_all | solution.py:63
  25.9 119.1 %all-to-all-done = f32[128,2,40,128]{3,2,1,0:T(8,128)} async-done(((f32[128,2,40,128]{3,2,1,0:T(8,128)}), f32[128,2,40,128]{3,2,1,0:T(8,128)}, u32[]{:S(2)}, u32[]{:S(2)}) %all-to-all-start) | async-done | bytes 5242912 | tf_op jit(solution)/shard_map/all_to_all | solution.py:63
  148.1 5.5 %fusion.49 = f32[64,40,128]{2,1,0:T(8,128)S(1)} fusion(f32[64,40,128]{2,1,0:T(8,128)S(1)} %gather_fusion.1, f32[64,128]{1,0:T(8,128)S(1)} %get-tuple-element.43, s32[64,128]{1,0:T(8,128)S(1)} %get-tuple-element.39, f32[64,128]{1,0:T(8,128)S(1)} %get-tuple-element.42, s32[64,128]{1,0:T(8,128)S(1)} %get-tuple-element.38, ...), kind=kOutput, calls=%fused_computation.113 | convolution fusion | flops 514850816 | bytes 2883584 | tf_op jit(solution)/shard_map/xgj,xjc->xgc/dot_general | solution.py:67
  157.7 5.5 %gather_fusion.2 = f32[512,40]{1,0:T(8,128)S(1)} fusion(f32[64,40,128]{1,2,0:T(8,128)} %copy.135, s32[512]{0:T(512)S(1)} %bitcast.81), kind=kCustom, calls=%fused_computation.2 | custom fusion | bytes 167936 | tf_op jit(solution)/shard_map/gather | solution.py:70
  165.0 51.4 %scatter_fusion = f32[64,40,128]{1,2,0:T(8,128)} fusion(f32[64,40,128]{1,2,0:T(8,128)} %copy.135, s32[512]{0:T(512)S(1)} %bitcast.82, f32[512,40]{1,0:T(8,128)S(1)} %collective-permute-done), kind=kCustom, calls=%fused_computation.3 | custom fusion | bytes 249856 | tf_op jit(solution)/shard_map/scatter | solution.py:73
  219.6 5.7 %collective-permute-start.1 = (f32[1,40,128]{1,2,0:T(8,128)S(1)}, f32[1,40,128]{1,2,0:T(8,128)S(1)}, u32[]{:S(2)}, u32[]{:S(2)}) collective-permute-start(f32[1,40,128]{1,2,0:T(8,128)S(1)} %get-tuple-element.35), channel_id=1, source_target_pairs={{4,0},{8,4},{12,8},{16,12},{20,16},{24,20},{28,24},{32,28},{36,32}... | collective-permute-start | bytes 61448 | tf_op jit(solution)/shard_map/ppermute | solution.py:27
  229.8 4.5 %collective-permute-start.4 = (f32[66,40,1]{1,2,0:T(1,128)S(1)}, f32[66,40,1]{1,2,0:T(1,128)S(1)}, u32[]{:S(2)}, u32[]{:S(2)}) collective-permute-start(f32[66,40,1]{1,2,0:T(1,128)S(1)} %get-tuple-element.20), channel_id=1, source_target_pairs={{0,1},{1,2},{2,3},{4,5},{5,6},{6,7},{8,9},{9,10},{10,11},{12,13},{... | collective-permute-start | bytes 31688 | tf_op jit(solution)/shard_map/ppermute | solution.py:24
  235.9 6.3 %fusion.46 = f32[64,40,128]{1,2,0:T(8,128)S(1)} fusion(f32[64,40,128]{1,2,0:T(8,128)S(1)} %copy-done.2, f32[66,40,128]{1,2,0:T(8,128)S(1)} %constant_dynamic-update-slice_fusion, f32[66,40,1]{1,2,0:T(1,128)S(1)} %collective-permute-done.4, f32[66,40,1]{1,2,0:T(1,128)S(1)} %collective-permute-done.3, f32[1,40,128]{1,2,0:T(8,128)S(1)} %collective-permute-done.2, ...), kind=kLoop, calls=%fused_computation.107 | loop fusion | flops 3276800 | bytes 4035520 | tf_op jit(solution)/shard_map/div | solution.py:82
  242.3 5.1 %collective-permute-start.5 = (f32[1,40,128]{1,2,0:T(8,128)S(1)}, f32[1,40,128]{1,2,0:T(8,128)S(1)}, u32[]{:S(2)}, u32[]{:S(2)}) collective-permute-start(f32[1,40,128]{1,2,0:T(8,128)S(1)} %get-tuple-element.34), channel_id=1, source_target_pairs={{4,0},{8,4},{12,8},{16,12},{20,16},{24,20},{28,24},{32,28},{36,32}... | collective-permute-start | bytes 61448 | tf_op jit(solution)/shard_map/ppermute | solution.py:27
  249.3 6.3 %collective-permute-done.6 = f32[1,40,128]{1,2,0:T(8,128)S(1)} collective-permute-done((f32[1,40,128]{1,2,0:T(8,128)S(1)}, f32[1,40,128]{1,2,0:T(8,128)S(1)}, u32[]{:S(2)}, u32[]{:S(2)}) %collective-permute-start.6) | collective-permute-done | bytes 20512 | tf_op jit(solution)/shard_map/ppermute | solution.py:24
  257.0 4.9 %collective-permute-start.8 = (f32[66,40,1]{1,2,0:T(1,128)S(1)}, f32[66,40,1]{1,2,0:T(1,128)S(1)}, u32[]{:S(2)}, u32[]{:S(2)}) collective-permute-start(f32[66,40,1]{1,2,0:T(1,128)S(1)} %get-tuple-element.18), channel_id=1, source_target_pairs={{0,1},{1,2},{2,3},{4,5},{5,6},{6,7},{8,9},{9,10},{10,11},{12,13},{... | collective-permute-start | bytes 31688 | tf_op jit(solution)/shard_map/ppermute | solution.py:24
  263.4 7.3 %fusion.40 = f32[64,40,128]{1,2,0:T(8,128)S(1)} fusion(f32[64,40,128]{1,2,0:T(8,128)S(1)} %copy-done.2, f32[66,40,1]{1,2,0:T(1,128)S(1)} %collective-permute-done.8, f32[1,40,128]{1,2,0:T(8,128)S(1)} %collective-permute-done.5, f32[64,40,128]{1,2,0:T(8,128)S(1)} %fusion.46, f32[1,40,128]{1,2,0:T(8,128)S(1)} %collective-permute-done.6, ...), kind=kLoop, calls=%fused_computation.93 | loop fusion | flops 4587520 | bytes 3994560 | tf_op jit(solution)/shard_map/div | solution.py:82
  272.7 6.0 %collective-permute-start.9 = (f32[1,40,128]{1,2,0:T(8,128)S(1)}, f32[1,40,128]{1,2,0:T(8,128)S(1)}, u32[]{:S(2)}, u32[]{:S(2)}) collective-permute-start(f32[1,40,128]{1,2,0:T(8,128)S(1)} %get-tuple-element.32), channel_id=1, source_target_pairs={{4,0},{8,4},{12,8},{16,12},{20,16},{24,20},{28,24},{32,28},{36,32}... | collective-permute-start | bytes 61448 | tf_op jit(solution)/shard_map/ppermute | solution.py:27
  282.0 4.9 %collective-permute-start.12 = (f32[66,40,1]{1,2,0:T(1,128)S(1)}, f32[66,40,1]{1,2,0:T(1,128)S(1)}, u32[]{:S(2)}, u32[]{:S(2)}) collective-permute-start(f32[66,40,1]{1,2,0:T(1,128)S(1)} %get-tuple-element.16), channel_id=1, source_target_pairs={{0,1},{1,2},{2,3},{4,5},{5,6},{6,7},{8,9},{9,10},{10,11},{12,13},{... | collective-permute-start | bytes 31688 | tf_op jit(solution)/shard_map/ppermute | solution.py:24
  288.5 7.3 %fusion.34 = f32[64,40,128]{1,2,0:T(8,128)S(1)} fusion(f32[64,40,128]{1,2,0:T(8,128)S(1)} %copy-done.2, f32[66,40,1]{1,2,0:T(1,128)S(1)} %collective-permute-done.12, f32[1,40,128]{1,2,0:T(8,128)S(1)} %collective-permute-done.9, f32[64,40,128]{1,2,0:T(8,128)S(1)} %fusion.40, f32[1,40,128]{1,2,0:T(8,128)S(1)} %collective-permute-done.10, ...), kind=kLoop, calls=%fused_computation.79 | loop fusion | flops 4587520 | bytes 3994560 | tf_op jit(solution)/shard_map/div | solution.py:82
  295.8 6.4 %collective-permute-start.13 = (f32[1,40,128]{1,2,0:T(8,128)S(1)}, f32[1,40,128]{1,2,0:T(8,128)S(1)}, u32[]{:S(2)}, u32[]{:S(2)}) collective-permute-start(f32[1,40,128]{1,2,0:T(8,128)S(1)} %get-tuple-element.30), channel_id=1, source_target_pairs={{4,0},{8,4},{12,8},{16,12},{20,16},{24,20},{28,24},{32,28},{36,32}... | collective-permute-start | bytes 61448 | tf_op jit(solution)/shard_map/ppermute | solution.py:27
  304.1 6.3 %collective-permute-done.14 = f32[1,40,128]{1,2,0:T(8,128)S(1)} collective-permute-done((f32[1,40,128]{1,2,0:T(8,128)S(1)}, f32[1,40,128]{1,2,0:T(8,128)S(1)}, u32[]{:S(2)}, u32[]{:S(2)}) %collective-permute-start.14) | collective-permute-done | bytes 20512 | tf_op jit(solution)/shard_map/ppermute | solution.py:24
  311.8 4.9 %collective-permute-start.16 = (f32[66,40,1]{1,2,0:T(1,128)S(1)}, f32[66,40,1]{1,2,0:T(1,128)S(1)}, u32[]{:S(2)}, u32[]{:S(2)}) collective-permute-start(f32[66,40,1]{1,2,0:T(1,128)S(1)} %get-tuple-element.14), channel_id=1, source_target_pairs={{0,1},{1,2},{2,3},{4,5},{5,6},{6,7},{8,9},{9,10},{10,11},{12,13},{... | collective-permute-start | bytes 31688 | tf_op jit(solution)/shard_map/ppermute | solution.py:24
  318.3 7.3 %fusion.28 = f32[64,40,128]{1,2,0:T(8,128)S(1)} fusion(f32[64,40,128]{1,2,0:T(8,128)S(1)} %copy-done.2, f32[66,40,1]{1,2,0:T(1,128)S(1)} %collective-permute-done.16, f32[1,40,128]{1,2,0:T(8,128)S(1)} %collective-permute-done.13, f32[64,40,128]{1,2,0:T(8,128)S(1)} %fusion.34, f32[1,40,128]{1,2,0:T(8,128)S(1)} %collective-permute-done.14, ...), kind=kLoop, calls=%fused_computation.65 | loop fusion | flops 4587520 | bytes 3994560 | tf_op jit(solution)/shard_map/div | solution.py:82
  331.8 4.0 collective-permute-done.18
  337.2 5.1 %collective-permute-start.20 = (f32[66,40,1]{1,2,0:T(1,128)S(1)}, f32[66,40,1]{1,2,0:T(1,128)S(1)}, u32[]{:S(2)}, u32[]{:S(2)}) collective-permute-start(f32[66,40,1]{1,2,0:T(1,128)S(1)} %get-tuple-element.12), channel_id=1, source_target_pairs={{0,1},{1,2},{2,3},{4,5},{5,6},{6,7},{8,9},{9,10},{10,11},{12,13},{... | collective-permute-start | bytes 31688 | tf_op jit(solution)/shard_map/ppermute | solution.py:24
  343.6 7.3 %fusion.22 = f32[64,40,128]{1,2,0:T(8,128)S(1)} fusion(f32[64,40,128]{1,2,0:T(8,128)S(1)} %copy-done.2, f32[66,40,1]{1,2,0:T(1,128)S(1)} %collective-permute-done.20, f32[1,40,128]{1,2,0:T(8,128)S(1)} %collective-permute-done.17, f32[64,40,128]{1,2,0:T(8,128)S(1)} %fusion.28, f32[1,40,128]{1,2,0:T(8,128)S(1)} %collective-permute-done.18, ...), kind=kLoop, calls=%fused_computation.51 | loop fusion | flops 4587520 | bytes 3994560 | tf_op jit(solution)/shard_map/div | solution.py:82
  357.2 4.0 collective-permute-done.22
  362.6 4.9 %collective-permute-start.24 = (f32[66,40,1]{1,2,0:T(1,128)S(1)}, f32[66,40,1]{1,2,0:T(1,128)S(1)}, u32[]{:S(2)}, u32[]{:S(2)}) collective-permute-start(f32[66,40,1]{1,2,0:T(1,128)S(1)} %get-tuple-element.10), channel_id=1, source_target_pairs={{0,1},{1,2},{2,3},{4,5},{5,6},{6,7},{8,9},{9,10},{10,11},{12,13},{... | collective-permute-start | bytes 31688 | tf_op jit(solution)/shard_map/ppermute | solution.py:24
  369.0 7.3 %fusion.16 = f32[64,40,128]{1,2,0:T(8,128)S(1)} fusion(f32[64,40,128]{1,2,0:T(8,128)S(1)} %copy-done.2, f32[66,40,1]{1,2,0:T(1,128)S(1)} %collective-permute-done.24, f32[1,40,128]{1,2,0:T(8,128)S(1)} %collective-permute-done.21, f32[64,40,128]{1,2,0:T(8,128)S(1)} %fusion.22, f32[1,40,128]{1,2,0:T(8,128)S(1)} %collective-permute-done.22, ...), kind=kLoop, calls=%fused_computation.37 | loop fusion | flops 4587520 | bytes 3994560 | tf_op jit(solution)/shard_map/div | solution.py:82
  382.5 4.0 collective-permute-done.26
  387.9 4.9 %collective-permute-start.28 = (f32[66,40,1]{1,2,0:T(1,128)S(1)}, f32[66,40,1]{1,2,0:T(1,128)S(1)}, u32[]{:S(2)}, u32[]{:S(2)}) collective-permute-start(f32[66,40,1]{1,2,0:T(1,128)S(1)} %get-tuple-element.8), channel_id=1, source_target_pairs={{0,1},{1,2},{2,3},{4,5},{5,6},{6,7},{8,9},{9,10},{10,11},{12,13},{... | collective-permute-start | bytes 31688 | tf_op jit(solution)/shard_map/ppermute | solution.py:24
  394.4 7.3 %fusion.10 = f32[64,40,128]{1,2,0:T(8,128)S(1)} fusion(f32[64,40,128]{1,2,0:T(8,128)S(1)} %copy-done.2, f32[66,40,1]{1,2,0:T(1,128)S(1)} %collective-permute-done.28, f32[1,40,128]{1,2,0:T(8,128)S(1)} %collective-permute-done.25, f32[64,40,128]{1,2,0:T(8,128)S(1)} %fusion.16, f32[1,40,128]{1,2,0:T(8,128)S(1)} %collective-permute-done.26, ...), kind=kLoop, calls=%fused_computation.23 | loop fusion | flops 4587520 | bytes 3994560 | tf_op jit(solution)/shard_map/div | solution.py:82
  407.9 4.0 collective-permute-done.30
  413.3 4.9 %collective-permute-start.32 = (f32[66,40,1]{1,2,0:T(1,128)S(1)}, f32[66,40,1]{1,2,0:T(1,128)S(1)}, u32[]{:S(2)}, u32[]{:S(2)}) collective-permute-start(f32[66,40,1]{1,2,0:T(1,128)S(1)} %get-tuple-element.6), channel_id=1, source_target_pairs={{0,1},{1,2},{2,3},{4,5},{5,6},{6,7},{8,9},{9,10},{10,11},{12,13},{... | collective-permute-start | bytes 31688 | tf_op jit(solution)/shard_map/ppermute | solution.py:24
  419.7 7.3 %fusion.4 = f32[1,64,40,128]{2,3,1,0:T(8,128)} fusion(f32[64,40,128]{1,2,0:T(8,128)S(1)} %copy-done.2, f32[66,40,1]{1,2,0:T(1,128)S(1)} %collective-permute-done.32, f32[1,40,128]{1,2,0:T(8,128)S(1)} %collective-permute-done.29, f32[64,40,128]{1,2,0:T(8,128)S(1)} %fusion.10, f32[1,40,128]{1,2,0:T(8,128)S(1)} %collective-permute-done.30, ...), kind=kLoop, calls=%fused_computation.9 | loop fusion | flops 4587520 | bytes 3994560 | tf_op jit(solution)/shard_map/broadcast_in_dim | solution.py:83
  (105 shorter events, 79.8 us)
Async XLA Ops:
  9.7 135.3 %all-to-all-start = ((f32[128,2,40,128]{3,2,1,0:T(8,128)}), f32[128,2,40,128]{3,2,1,0:T(8,128)}, u32[]{:S(2)}, u32[]{:S(2)}) async-start(f32[128,2,40,128]{3,2,1,0:T(8,128)} %broadcast_select_fusion), calls=%async_computation | async-start | bytes 10485760 | tf_op jit(solution)/shard_map/all_to_all | solution.py:63
  217.3 8.3 %collective-permute-start.2 = (f32[1,40,128]{1,2,0:T(8,128)S(1)}, f32[1,40,128]{1,2,0:T(8,128)S(1)}, u32[]{:S(2)}, u32[]{:S(2)}) collective-permute-start(f32[1,40,128]{1,2,0:T(8,128)S(1)} %get-tuple-element.36), channel_id=1, source_target_pairs={{0,4},{4,8},{8,12},{12,16},{16,20},{20,24},{24,28},{28,32},{32,36}... | collective-permute-start | bytes 61448 | tf_op jit(solution)/shard_map/ppermute | solution.py:24
  219.6 8.8 %collective-permute-start.1 = (f32[1,40,128]{1,2,0:T(8,128)S(1)}, f32[1,40,128]{1,2,0:T(8,128)S(1)}, u32[]{:S(2)}, u32[]{:S(2)}) collective-permute-start(f32[1,40,128]{1,2,0:T(8,128)S(1)} %get-tuple-element.35), channel_id=1, source_target_pairs={{4,0},{8,4},{12,8},{16,12},{20,16},{24,20},{28,24},{32,28},{36,32}... | collective-permute-start | bytes 61448 | tf_op jit(solution)/shard_map/ppermute | solution.py:27
  229.8 6.1 %collective-permute-start.4 = (f32[66,40,1]{1,2,0:T(1,128)S(1)}, f32[66,40,1]{1,2,0:T(1,128)S(1)}, u32[]{:S(2)}, u32[]{:S(2)}) collective-permute-start(f32[66,40,1]{1,2,0:T(1,128)S(1)} %get-tuple-element.20), channel_id=1, source_target_pairs={{0,1},{1,2},{2,3},{4,5},{5,6},{6,7},{8,9},{9,10},{10,11},{12,13},{... | collective-permute-start | bytes 31688 | tf_op jit(solution)/shard_map/ppermute | solution.py:24
  242.3 7.0 %collective-permute-start.5 = (f32[1,40,128]{1,2,0:T(8,128)S(1)}, f32[1,40,128]{1,2,0:T(8,128)S(1)}, u32[]{:S(2)}, u32[]{:S(2)}) collective-permute-start(f32[1,40,128]{1,2,0:T(8,128)S(1)} %get-tuple-element.34), channel_id=1, source_target_pairs={{4,0},{8,4},{12,8},{16,12},{20,16},{24,20},{28,24},{32,28},{36,32}... | collective-permute-start | bytes 61448 | tf_op jit(solution)/shard_map/ppermute | solution.py:27
  247.4 8.3 %collective-permute-start.6 = (f32[1,40,128]{1,2,0:T(8,128)S(1)}, f32[1,40,128]{1,2,0:T(8,128)S(1)}, u32[]{:S(2)}, u32[]{:S(2)}) collective-permute-start(f32[1,40,128]{1,2,0:T(8,128)S(1)} %get-tuple-element.33), channel_id=1, source_target_pairs={{0,4},{4,8},{8,12},{12,16},{16,20},{20,24},{24,28},{28,32},{32,36}... | collective-permute-start | bytes 61448 | tf_op jit(solution)/shard_map/ppermute | solution.py:24
  255.7 6.2 %collective-permute-start.7 = (f32[66,40,1]{1,2,0:T(1,128)S(1)}, f32[66,40,1]{1,2,0:T(1,128)S(1)}, u32[]{:S(2)}, u32[]{:S(2)}) collective-permute-start(f32[66,40,1]{1,2,0:T(1,128)S(1)} %get-tuple-element.17), channel_id=1, source_target_pairs={{1,0},{2,1},{3,2},{5,4},{6,5},{7,6},{9,8},{10,9},{11,10},{13,12},{... | collective-permute-start | bytes 31688 | tf_op jit(solution)/shard_map/ppermute | solution.py:27
  257.0 6.4 %collective-permute-start.8 = (f32[66,40,1]{1,2,0:T(1,128)S(1)}, f32[66,40,1]{1,2,0:T(1,128)S(1)}, u32[]{:S(2)}, u32[]{:S(2)}) collective-permute-start(f32[66,40,1]{1,2,0:T(1,128)S(1)} %get-tuple-element.18), channel_id=1, source_target_pairs={{0,1},{1,2},{2,3},{4,5},{5,6},{6,7},{8,9},{9,10},{10,11},{12,13},{... | collective-permute-start | bytes 31688 | tf_op jit(solution)/shard_map/ppermute | solution.py:24
  270.8 8.3 %collective-permute-start.10 = (f32[1,40,128]{1,2,0:T(8,128)S(1)}, f32[1,40,128]{1,2,0:T(8,128)S(1)}, u32[]{:S(2)}, u32[]{:S(2)}) collective-permute-start(f32[1,40,128]{1,2,0:T(8,128)S(1)} %get-tuple-element.31), channel_id=1, source_target_pairs={{0,4},{4,8},{8,12},{12,16},{16,20},{20,24},{24,28},{28,32},{32,36}... | collective-permute-start | bytes 61448 | tf_op jit(solution)/shard_map/ppermute | solution.py:24
  272.7 7.9 %collective-permute-start.9 = (f32[1,40,128]{1,2,0:T(8,128)S(1)}, f32[1,40,128]{1,2,0:T(8,128)S(1)}, u32[]{:S(2)}, u32[]{:S(2)}) collective-permute-start(f32[1,40,128]{1,2,0:T(8,128)S(1)} %get-tuple-element.32), channel_id=1, source_target_pairs={{4,0},{8,4},{12,8},{16,12},{20,16},{24,20},{28,24},{32,28},{36,32}... | collective-permute-start | bytes 61448 | tf_op jit(solution)/shard_map/ppermute | solution.py:27
  280.7 6.2 %collective-permute-start.11 = (f32[66,40,1]{1,2,0:T(1,128)S(1)}, f32[66,40,1]{1,2,0:T(1,128)S(1)}, u32[]{:S(2)}, u32[]{:S(2)}) collective-permute-start(f32[66,40,1]{1,2,0:T(1,128)S(1)} %get-tuple-element.15), channel_id=1, source_target_pairs={{1,0},{2,1},{3,2},{5,4},{6,5},{7,6},{9,8},{10,9},{11,10},{13,12},{... | collective-permute-start | bytes 31688 | tf_op jit(solution)/shard_map/ppermute | solution.py:27
  282.0 6.4 %collective-permute-start.12 = (f32[66,40,1]{1,2,0:T(1,128)S(1)}, f32[66,40,1]{1,2,0:T(1,128)S(1)}, u32[]{:S(2)}, u32[]{:S(2)}) collective-permute-start(f32[66,40,1]{1,2,0:T(1,128)S(1)} %get-tuple-element.16), channel_id=1, source_target_pairs={{0,1},{1,2},{2,3},{4,5},{5,6},{6,7},{8,9},{9,10},{10,11},{12,13},{... | collective-permute-start | bytes 31688 | tf_op jit(solution)/shard_map/ppermute | solution.py:24
  295.8 8.3 %collective-permute-start.13 = (f32[1,40,128]{1,2,0:T(8,128)S(1)}, f32[1,40,128]{1,2,0:T(8,128)S(1)}, u32[]{:S(2)}, u32[]{:S(2)}) collective-permute-start(f32[1,40,128]{1,2,0:T(8,128)S(1)} %get-tuple-element.30), channel_id=1, source_target_pairs={{4,0},{8,4},{12,8},{16,12},{20,16},{24,20},{28,24},{32,28},{36,32}... | collective-permute-start | bytes 61448 | tf_op jit(solution)/shard_map/ppermute | solution.py:27
  302.2 8.3 %collective-permute-start.14 = (f32[1,40,128]{1,2,0:T(8,128)S(1)}, f32[1,40,128]{1,2,0:T(8,128)S(1)}, u32[]{:S(2)}, u32[]{:S(2)}) collective-permute-start(f32[1,40,128]{1,2,0:T(8,128)S(1)} %get-tuple-element.29), channel_id=1, source_target_pairs={{0,4},{4,8},{8,12},{12,16},{16,20},{20,24},{24,28},{28,32},{32,36}... | collective-permute-start | bytes 61448 | tf_op jit(solution)/shard_map/ppermute | solution.py:24
  310.5 6.2 %collective-permute-start.15 = (f32[66,40,1]{1,2,0:T(1,128)S(1)}, f32[66,40,1]{1,2,0:T(1,128)S(1)}, u32[]{:S(2)}, u32[]{:S(2)}) collective-permute-start(f32[66,40,1]{1,2,0:T(1,128)S(1)} %get-tuple-element.13), channel_id=1, source_target_pairs={{1,0},{2,1},{3,2},{5,4},{6,5},{7,6},{9,8},{10,9},{11,10},{13,12},{... | collective-permute-start | bytes 31688 | tf_op jit(solution)/shard_map/ppermute | solution.py:27
  311.8 6.4 %collective-permute-start.16 = (f32[66,40,1]{1,2,0:T(1,128)S(1)}, f32[66,40,1]{1,2,0:T(1,128)S(1)}, u32[]{:S(2)}, u32[]{:S(2)}) collective-permute-start(f32[66,40,1]{1,2,0:T(1,128)S(1)} %get-tuple-element.14), channel_id=1, source_target_pairs={{0,1},{1,2},{2,3},{4,5},{5,6},{6,7},{8,9},{9,10},{10,11},{12,13},{... | collective-permute-start | bytes 31688 | tf_op jit(solution)/shard_map/ppermute | solution.py:24
  325.6 6.2 %collective-permute-start.17 = (f32[1,40,128]{1,2,0:T(8,128)S(1)}, f32[1,40,128]{1,2,0:T(8,128)S(1)}, u32[]{:S(2)}, u32[]{:S(2)}) collective-permute-start(f32[1,40,128]{1,2,0:T(8,128)S(1)} %get-tuple-element.28), channel_id=1, source_target_pairs={{4,0},{8,4},{12,8},{16,12},{20,16},{24,20},{28,24},{32,28},{36,32}... | collective-permute-start | bytes 61448 | tf_op jit(solution)/shard_map/ppermute | solution.py:27
  327.6 8.3 %collective-permute-start.18 = (f32[1,40,128]{1,2,0:T(8,128)S(1)}, f32[1,40,128]{1,2,0:T(8,128)S(1)}, u32[]{:S(2)}, u32[]{:S(2)}) collective-permute-start(f32[1,40,128]{1,2,0:T(8,128)S(1)} %get-tuple-element.27), channel_id=1, source_target_pairs={{0,4},{4,8},{8,12},{12,16},{16,20},{20,24},{24,28},{28,32},{32,36}... | collective-permute-start | bytes 61448 | tf_op jit(solution)/shard_map/ppermute | solution.py:24
  335.9 6.4 %collective-permute-start.19 = (f32[66,40,1]{1,2,0:T(1,128)S(1)}, f32[66,40,1]{1,2,0:T(1,128)S(1)}, u32[]{:S(2)}, u32[]{:S(2)}) collective-permute-start(f32[66,40,1]{1,2,0:T(1,128)S(1)} %get-tuple-element.11), channel_id=1, source_target_pairs={{1,0},{2,1},{3,2},{5,4},{6,5},{7,6},{9,8},{10,9},{11,10},{13,12},{... | collective-permute-start | bytes 31688 | tf_op jit(solution)/shard_map/ppermute | solution.py:27
  337.2 6.4 %collective-permute-start.20 = (f32[66,40,1]{1,2,0:T(1,128)S(1)}, f32[66,40,1]{1,2,0:T(1,128)S(1)}, u32[]{:S(2)}, u32[]{:S(2)}) collective-permute-start(f32[66,40,1]{1,2,0:T(1,128)S(1)} %get-tuple-element.12), channel_id=1, source_target_pairs={{0,1},{1,2},{2,3},{4,5},{5,6},{6,7},{8,9},{9,10},{10,11},{12,13},{... | collective-permute-start | bytes 31688 | tf_op jit(solution)/shard_map/ppermute | solution.py:24
  351.0 6.2 %collective-permute-start.21 = (f32[1,40,128]{1,2,0:T(8,128)S(1)}, f32[1,40,128]{1,2,0:T(8,128)S(1)}, u32[]{:S(2)}, u32[]{:S(2)}) collective-permute-start(f32[1,40,128]{1,2,0:T(8,128)S(1)} %get-tuple-element.26), channel_id=1, source_target_pairs={{4,0},{8,4},{12,8},{16,12},{20,16},{24,20},{28,24},{32,28},{36,32}... | collective-permute-start | bytes 61448 | tf_op jit(solution)/shard_map/ppermute | solution.py:27
  352.9 8.3 %collective-permute-start.22 = (f32[1,40,128]{1,2,0:T(8,128)S(1)}, f32[1,40,128]{1,2,0:T(8,128)S(1)}, u32[]{:S(2)}, u32[]{:S(2)}) collective-permute-start(f32[1,40,128]{1,2,0:T(8,128)S(1)} %get-tuple-element.25), channel_id=1, source_target_pairs={{0,4},{4,8},{8,12},{12,16},{16,20},{20,24},{24,28},{28,32},{32,36}... | collective-permute-start | bytes 61448 | tf_op jit(solution)/shard_map/ppermute | solution.py:24
  361.3 6.2 %collective-permute-start.23 = (f32[66,40,1]{1,2,0:T(1,128)S(1)}, f32[66,40,1]{1,2,0:T(1,128)S(1)}, u32[]{:S(2)}, u32[]{:S(2)}) collective-permute-start(f32[66,40,1]{1,2,0:T(1,128)S(1)} %get-tuple-element.9), channel_id=1, source_target_pairs={{1,0},{2,1},{3,2},{5,4},{6,5},{7,6},{9,8},{10,9},{11,10},{13,12},{... | collective-permute-start | bytes 31688 | tf_op jit(solution)/shard_map/ppermute | solution.py:27
  362.6 6.4 %collective-permute-start.24 = (f32[66,40,1]{1,2,0:T(1,128)S(1)}, f32[66,40,1]{1,2,0:T(1,128)S(1)}, u32[]{:S(2)}, u32[]{:S(2)}) collective-permute-start(f32[66,40,1]{1,2,0:T(1,128)S(1)} %get-tuple-element.10), channel_id=1, source_target_pairs={{0,1},{1,2},{2,3},{4,5},{5,6},{6,7},{8,9},{9,10},{10,11},{12,13},{... | collective-permute-start | bytes 31688 | tf_op jit(solution)/shard_map/ppermute | solution.py:24
  376.4 6.2 %collective-permute-start.25 = (f32[1,40,128]{1,2,0:T(8,128)S(1)}, f32[1,40,128]{1,2,0:T(8,128)S(1)}, u32[]{:S(2)}, u32[]{:S(2)}) collective-permute-start(f32[1,40,128]{1,2,0:T(8,128)S(1)} %get-tuple-element.24), channel_id=1, source_target_pairs={{4,0},{8,4},{12,8},{16,12},{20,16},{24,20},{28,24},{32,28},{36,32}... | collective-permute-start | bytes 61448 | tf_op jit(solution)/shard_map/ppermute | solution.py:27
  378.3 8.3 %collective-permute-start.26 = (f32[1,40,128]{1,2,0:T(8,128)S(1)}, f32[1,40,128]{1,2,0:T(8,128)S(1)}, u32[]{:S(2)}, u32[]{:S(2)}) collective-permute-start(f32[1,40,128]{1,2,0:T(8,128)S(1)} %get-tuple-element.23), channel_id=1, source_target_pairs={{0,4},{4,8},{8,12},{12,16},{16,20},{20,24},{24,28},{28,32},{32,36}... | collective-permute-start | bytes 61448 | tf_op jit(solution)/shard_map/ppermute | solution.py:24
  386.6 6.2 %collective-permute-start.27 = (f32[66,40,1]{1,2,0:T(1,128)S(1)}, f32[66,40,1]{1,2,0:T(1,128)S(1)}, u32[]{:S(2)}, u32[]{:S(2)}) collective-permute-start(f32[66,40,1]{1,2,0:T(1,128)S(1)} %get-tuple-element.7), channel_id=1, source_target_pairs={{1,0},{2,1},{3,2},{5,4},{6,5},{7,6},{9,8},{10,9},{11,10},{13,12},{... | collective-permute-start | bytes 31688 | tf_op jit(solution)/shard_map/ppermute | solution.py:27
  387.9 6.4 %collective-permute-start.28 = (f32[66,40,1]{1,2,0:T(1,128)S(1)}, f32[66,40,1]{1,2,0:T(1,128)S(1)}, u32[]{:S(2)}, u32[]{:S(2)}) collective-permute-start(f32[66,40,1]{1,2,0:T(1,128)S(1)} %get-tuple-element.8), channel_id=1, source_target_pairs={{0,1},{1,2},{2,3},{4,5},{5,6},{6,7},{8,9},{9,10},{10,11},{12,13},{... | collective-permute-start | bytes 31688 | tf_op jit(solution)/shard_map/ppermute | solution.py:24
  401.7 6.2 %collective-permute-start.29 = (f32[1,40,128]{1,2,0:T(8,128)S(1)}, f32[1,40,128]{1,2,0:T(8,128)S(1)}, u32[]{:S(2)}, u32[]{:S(2)}) collective-permute-start(f32[1,40,128]{1,2,0:T(8,128)S(1)} %get-tuple-element.22), channel_id=1, source_target_pairs={{4,0},{8,4},{12,8},{16,12},{20,16},{24,20},{28,24},{32,28},{36,32}... | collective-permute-start | bytes 61448 | tf_op jit(solution)/shard_map/ppermute | solution.py:27
  403.7 8.3 %collective-permute-start.30 = (f32[1,40,128]{1,2,0:T(8,128)S(1)}, f32[1,40,128]{1,2,0:T(8,128)S(1)}, u32[]{:S(2)}, u32[]{:S(2)}) collective-permute-start(f32[1,40,128]{1,2,0:T(8,128)S(1)} %get-tuple-element.21), channel_id=1, source_target_pairs={{0,4},{4,8},{8,12},{12,16},{16,20},{20,24},{24,28},{28,32},{32,36}... | collective-permute-start | bytes 61448 | tf_op jit(solution)/shard_map/ppermute | solution.py:24
  412.0 6.2 %collective-permute-start.31 = (f32[66,40,1]{1,2,0:T(1,128)S(1)}, f32[66,40,1]{1,2,0:T(1,128)S(1)}, u32[]{:S(2)}, u32[]{:S(2)}) collective-permute-start(f32[66,40,1]{1,2,0:T(1,128)S(1)} %get-tuple-element.5), channel_id=1, source_target_pairs={{1,0},{2,1},{3,2},{5,4},{6,5},{7,6},{9,8},{10,9},{11,10},{13,12},{... | collective-permute-start | bytes 31688 | tf_op jit(solution)/shard_map/ppermute | solution.py:27
  413.3 6.4 %collective-permute-start.32 = (f32[66,40,1]{1,2,0:T(1,128)S(1)}, f32[66,40,1]{1,2,0:T(1,128)S(1)}, u32[]{:S(2)}, u32[]{:S(2)}) collective-permute-start(f32[66,40,1]{1,2,0:T(1,128)S(1)} %get-tuple-element.6), channel_id=1, source_target_pairs={{0,1},{1,2},{2,3},{4,5},{5,6},{6,7},{8,9},{9,10},{10,11},{12,13},{... | collective-permute-start | bytes 31688 | tf_op jit(solution)/shard_map/ppermute | solution.py:24
  (12 other events, 118.4 us)
where the time goes:
time: 435 us; the launch traced here: 431 us
  waiting for transfers between devices  165 us (38%)
  starting transfers between devices  120 us (28%)
  local copies, waits for them, and re-layouts  74.1 us (17%)
  other arithmetic  63.9 us (15%)
  matrix products  6.82 us (2%)
    all_to_all x1, waiting for transfers between devices, local(): lax.all_to_all(outgoing, ('gx', 'gy'), split_axis=0, concat_axis=0, tiled...  119 us
    ppermute x16, starting transfers between devices, with_halo(): lax.ppermute(lax.slice_in_dim(block, block.shape[dim] - width, None, axis...  62.5 us
    scatter x1, local copies, waits for them, and re-layouts, local(): arrival.at[into_cells // cells, :, into_cells % cells].set(received)  51.4 us
    div x7, other arithmetic, local(): balanced = (merged + coeff * neighbours) / diagonal  50.3 us
    ppermute x16, waiting for transfers between devices, with_halo(): lax.ppermute(lax.slice_in_dim(block, block.shape[dim] - width, None, axis...  41.8 us
    ppermute x16, starting transfers between devices, with_halo(): lax.ppermute(lax.slice_in_dim(block, 0, width, axis=dim), axis, backward)  41.2 us
    all_to_all x1, starting transfers between devices, local(): lax.all_to_all(outgoing, ('gx', 'gy'), split_axis=0, concat_axis=0, tiled...  16.1 us
  transfers between devices with their start and end apart: 34, of which 23 were waited for; matrix products, arithmetic and copies ran while one was open for 1% of the time, Pallas kernels for 0%

commit v1 on v0

v1 whole, which is shorter than its diff:
```python
import functools

import jax
import jax.numpy as jnp
from jax import lax
from jax.experimental import pallas as pl
from jax.experimental.pallas import tpu as pltpu
from jax.sharding import PartitionSpec as P

SWEEPS = 8
WIDTH = 8
SUB = 8
F32 = jnp.float32
VMEM_LIMIT = 48 * 1024 * 1024


def whole(space=pltpu.VMEM):
    return pl.BlockSpec(memory_space=space)


def params():
    return pltpu.CompilerParams(vmem_limit_bytes=VMEM_LIMIT)


def cost(flops, moved):
    return pl.CostEstimate(flops=flops, bytes_accessed=moved, transcendentals=0)


def pack_kernel(wanted, tile, out, sem):
    slots, tiles = wanted.shape

    def send(d, sent):
        for k in range(slots):
            block = wanted[k, d]
            filled = block >= 0

            @pl.when(filled)
            def _():
                pltpu.make_async_copy(tile.at[block], out.at[d, k], sem).start()

            sent = sent + jnp.where(filled, 1, 0)
        return sent

    sent = lax.fori_loop(0, tiles, send, 0)

    def wait(_, carry):
        pltpu.make_async_copy(tile.at[0], out.at[0, 0], sem).wait()
        return carry

    lax.fori_loop(0, sent, wait, 0)


def pack_blocks(wanted, tile):
    slots, tiles = wanted.shape
    return pl.pallas_call(
        pack_kernel,
        out_shape=jax.ShapeDtypeStruct((tiles, slots) + tile.shape[1:], F32),
        in_specs=[whole(pltpu.SMEM), whole()],
        out_specs=whole(pl.ANY),
        scratch_shapes=[pltpu.SemaphoreType.DMA],
        compiler_params=params(),
        name="pack_blocks",
    )(wanted, tile)


def couple_kernel(tile, mix_t, out):
    mix = mix_t[...] * 0.5

    def row(r, carry):
        out[r] = jnp.dot(mix, tile[r], precision=lax.Precision.HIGHEST, preferred_element_type=F32)
        return carry

    lax.fori_loop(0, tile.shape[0], row, 0, unroll=4)


def couple(tile, mix_t):
    return pl.pallas_call(
        couple_kernel,
        out_shape=jax.ShapeDtypeStruct(tile.shape, F32),
        in_specs=[whole(), whole()],
        out_specs=whole(),
        compiler_params=params(),
        cost_estimate=cost(2 * tile.size * tile.shape[1] * 6, 8 * tile.size),
        name="couple",
    )(tile, mix_t)


def arrive_kernel(rows, strip, slots, coupled, cell, frac, out, picked, fetched, sem):
    count, chan, cells = out.shape

    def fetch(r, carry):
        pltpu.make_async_copy(slots.at[rows[0, r]], fetched.at[r], sem).start()
        return carry

    lax.fori_loop(0, count, fetch, 0)
    pltpu.make_async_copy(slots.at[pl.ds(0, count)], fetched, sem).wait()

    def row(r, carry):
        t = frac[pl.ds(r, 1), :]
        m = jnp.broadcast_to(cell[pl.ds(r, 1), :], (SUB, cells))
        weights = (
            -t * (t - 1.0) * (t - 2.0) / 6.0,
            (t + 1.0) * (t - 1.0) * (t - 2.0) / 2.0,
            -(t + 1.0) * t * (t - 2.0) / 2.0,
            (t + 1.0) * t * (t - 1.0) / 6.0,
        )
        weights = [jnp.broadcast_to(w, (SUB, cells)) for w in weights]
        for c in range(0, chan, SUB):
            block = fetched[r, c : c + SUB, :]
            total = coupled[r, c : c + SUB, :]
            for tap, weight in zip((-1, 0, 1, 2), weights):
                total = total + weight * jnp.take_along_axis(
                    block, m + tap, axis=1, mode="promise_in_bounds"
                )
            out[r, c : c + SUB, :] = total
        return carry

    lax.fori_loop(0, count, row, 0, unroll=2)

    lane = lax.broadcasted_iota(jnp.int32, (chan, cells), 1)
    for part in range(picked.shape[1] // cells):

        def pick(j, held):
            place = strip[0, part * cells + j]
            moved = pltpu.roll(out[place // cells], (j - place % cells) & (cells - 1), 1)
            return jnp.where(lane == j, moved, held)

        held = lax.fori_loop(0, cells, pick, jnp.zeros((chan, cells), F32), unroll=8)
        picked[:, part * cells : (part + 1) * cells] = held


def arrive(rows, strip, slots, coupled, cell, frac):
    return pl.pallas_call(
        arrive_kernel,
        out_shape=(
            jax.ShapeDtypeStruct(coupled.shape, F32),
            jax.ShapeDtypeStruct((coupled.shape[1], strip.shape[1]), F32),
        ),
        in_specs=[whole(pltpu.SMEM), whole(pltpu.SMEM), whole(pl.ANY), whole(), whole(), whole()],
        out_specs=(whole(), whole()),
        scratch_shapes=[pltpu.VMEM(coupled.shape, F32), pltpu.SemaphoreType.DMA],
        compiler_params=params(),
        name="arrive",
    )(rows, strip, slots, coupled, cell, frac)


def merge_kernel(strip, arrival, received, out, low, high):
    count, chan, cells = out.shape
    out[...] = arrival[...]
    lane = lax.broadcasted_iota(jnp.int32, (chan, cells), 1)
    for part in range(received.shape[1] // cells):

        def put(j, carry):
            place = strip[0, part * cells + j]
            at = place % cells
            moved = pltpu.roll(
                received[:, part * cells : (part + 1) * cells], (at - j) & (cells - 1), 1
            )
            pltpu.store(out.at[place // cells], moved, mask=lane == at)
            return carry

        lax.fori_loop(0, cells, put, 0, unroll=8)
    per = cells // WIDTH
    for g in range(count // per):

        def edge(i, held):
            row = out[g * per + i]
            here = (lane // WIDTH) == i
            first = pltpu.roll(row, i * WIDTH, 1)
            last = pltpu.roll(row, (i + 1) * WIDTH & (cells - 1), 1)
            return jnp.where(here, first, held[0]), jnp.where(here, last, held[1])

        empty = jnp.zeros((chan, cells), F32)
        low[g], high[g] = lax.fori_loop(0, per, edge, (empty, empty), unroll=4)


def merge(strip, arrival, received):
    count, chan, cells = arrival.shape
    edge = jax.ShapeDtypeStruct((count * WIDTH // cells, chan, cells), F32)
    return pl.pallas_call(
        merge_kernel,
        out_shape=(jax.ShapeDtypeStruct(arrival.shape, F32), edge, edge),
        in_specs=[whole(pltpu.SMEM), whole(), whole()],
        out_specs=(whole(), whole(), whole()),
        compiler_params=params(),
        name="merge",
    )(strip, arrival, received)


def edge_rows_kernel(merged, left, right, first, last):
    count, chan, cells = merged.shape
    lane = lax.broadcasted_iota(jnp.int32, (chan, cells), 1)
    half = cells // 2
    groups = left.shape[0]
    first[:WIDTH] = merged[:WIDTH]
    first[WIDTH] = jnp.where(lane < half, right[0], pltpu.roll(left[0], half, 1))
    last[:WIDTH] = merged[count - WIDTH :]
    last[WIDTH] = jnp.where(lane < half, pltpu.roll(right[groups - 1], half, 1), left[groups - 1])


def edge_rows(merged, left, right):
    count, chan, cells = merged.shape
    rows = jax.ShapeDtypeStruct((WIDTH + 1, chan, cells), F32)
    return pl.pallas_call(
        edge_rows_kernel,
        out_shape=(rows, rows),
        in_specs=[whole(), whole(), whole()],
        out_specs=(whole(), whole()),
        compiler_params=params(),
        name="edge_rows",
    )(merged, left, right)


def relax_kernel(inside, merged, above, below, left, right, coef, out, m0, m1, a0, a1, b0, b1):
    count, chan, cells = merged.shape
    lane = lax.broadcasted_iota(jnp.int32, (chan, cells), 1)
    is_right, is_left = lane < WIDTH, lane >= cells - WIDTH
    h = coef[...]
    inv = 1.0 / (1.0 + 4.0 * h)
    inv_b = jnp.broadcast_to(inv, (chan, cells))
    total = count + 2 * WIDTH
    per = cells // WIDTH
    half = cells // 2

    def load(at, row, beside):
        a0[at] = row
        m0[at] = row * inv_b
        a1[at] = beside
        m1[at] = beside * inv_b

    for at, rows in ((0, above), (WIDTH + count, below)):
        for i in range(WIDTH):
            packed = rows[WIDTH]
            beside = jnp.where(
                is_right,
                pltpu.roll(packed, (-i * WIDTH) % cells, 1),
                jnp.where(is_left, pltpu.roll(packed, (half - (i + 1) * WIDTH) % cells, 1), 0.0),
            )
            load(at + i, rows[i], beside)
    for g in range(left.shape[0]):

        def fill(i, carry):
            to_right = pltpu.roll(right[g], (cells - i * WIDTH) & (cells - 1), 1)
            to_left = pltpu.roll(left[g], cells - (i + 1) * WIDTH, 1)
            beside = jnp.where(is_right, to_right, jnp.where(is_left, to_left, 0.0))
            r = g * per + i
            load(WIDTH + r, merged[r], beside)
            return carry

        lax.fori_loop(0, per, fill, 0, unroll=4)

    lane8 = lax.broadcasted_iota(jnp.int32, (SUB, cells), 1)
    is_first, is_last = lane8 == 0, lane8 == cells - 1
    side = jnp.where(
        lane8 < WIDTH, inside[3], jnp.where(lane8 >= cells - WIDTH, inside[2], 0)
    ).astype(F32)

    def turn(row, beside):
        l0, l1 = pltpu.roll(row, 1, 1), pltpu.roll(beside, 1, 1)
        r0, r1 = pltpu.roll(row, cells - 1, 1), pltpu.roll(beside, cells - 1, 1)
        return (
            jnp.where(is_first, l1, l0) + jnp.where(is_last, r1, r0),
            jnp.where(is_first, l0, l1) + jnp.where(is_last, r0, r1),
        )

    for c in range(0, chan, SUB):
        ch = slice(c, c + SUB)
        gain = jnp.broadcast_to(h[ch] * inv[ch], (SUB, cells))
        gain_side = gain * side
        lo = inside[0].astype(F32)
        hi = inside[1].astype(F32)

        for s in range(SWEEPS):
            src0, src1 = (a0, a1) if s % 2 == 0 else (b0, b1)
            dst0, dst1 = (b0, b1) if s % 2 == 0 else (a0, a1)
            last = s == SWEEPS - 1
            begin, end = s + 1, total - s - 1

            def update(x, held, g0, g1):
                up0, up1, mid0, mid1 = held
                down0, down1 = src0[x + 1, ch], src1[x + 1, ch]
                across0, across1 = turn(mid0, mid1)
                new0 = m0[x, ch] + g0 * (up0 + down0 + across0)
                if last:
                    out[x - WIDTH, ch] = new0
                else:
                    dst0[x, ch] = new0
                    dst1[x, ch] = m1[x, ch] + g1 * (up1 + down1 + across1)
                return mid0, mid1, down0, down1

            held = (
                src0[begin - 1, ch],
                src1[begin - 1, ch],
                src0[begin, ch],
                src1[begin, ch],
            )
            for x in range(begin, WIDTH):
                held = update(x, held, gain * lo, gain_side * lo)
            held = lax.fori_loop(
                WIDTH,
                WIDTH + count,
                lambda x, v: update(x, v, gain, gain_side),
                held,
                unroll=8,
            )
            for x in range(WIDTH + count, end):
                held = update(x, held, gain * hi, gain_side * hi)


def relax(inside, merged, above, below, left, right, coef):
    count, chan, cells = merged.shape
    held = pltpu.VMEM((count + 2 * WIDTH, chan, cells), F32)
    return pl.pallas_call(
        relax_kernel,
        out_shape=jax.ShapeDtypeStruct(merged.shape, F32),
        in_specs=[whole(pltpu.SMEM)] + [whole()] * 6,
        out_specs=whole(),
        scratch_shapes=[held] * 6,
        compiler_params=params(),
        name="relax",
    )(inside, merged, above, below, left, right, coef)


def shifted(block, axis, step):
    count = lax.axis_size(axis)
    route = [(i, i + step) for i in range(count) if 0 <= i + step < count]
    return lax.ppermute(block, axis, route)


def local(
    model_state,
    depart_frac,
    depart_cell,
    row_source,
    send_block,
    strip_from,
    strip_into,
    helmholtz_coef,
    vertical_mix,
):
    tile = model_state[0]
    chan = tile.shape[1]
    outgoing = pack_blocks(send_block[0, 0].T, tile)
    arrived = lax.all_to_all(outgoing, ("gx", "gy"), split_axis=0, concat_axis=0, tiled=True)
    coupled = couple(tile, vertical_mix.T)
    slots = arrived.reshape((-1,) + tile.shape[1:])
    arrival, picked = arrive(
        row_source, strip_from[0], slots, coupled, depart_cell[0], depart_frac[0]
    )
    received = lax.ppermute(picked, "panel", [(0, 1), (1, 0)])
    merged, low, high = merge(strip_into[0], arrival, received)
    right = shifted(low, "gy", -1)
    left = shifted(high, "gy", 1)
    first, last = edge_rows(merged, left, right)
    below = shifted(first, "gx", -1)
    above = shifted(last, "gx", 1)
    gx, gy = lax.axis_index("gx"), lax.axis_index("gy")
    inside = jnp.stack(
        [gx > 0, gx < lax.axis_size("gx") - 1, gy > 0, gy < lax.axis_size("gy") - 1]
    ).astype(jnp.int32)
    balanced = relax(
        inside, merged, above, below, left, right, helmholtz_coef.reshape(chan, 1)
    )
    return balanced[None]


def solution(mesh):
    in_specs = (
        P("panel", "gx", None, "gy"),
        P("panel", "gx", "gy"),
        P("panel", "gx", "gy"),
        P("panel", ("gx", "gy")),
        P("panel", ("gx", "gy"), None, None),
        P("panel", ("gx", "gy"), None),
        P("panel", ("gx", "gy"), None),
        P(),
        P(),
    )
    out_specs = P("panel", "gx", None, "gy")
    return jax.shard_map(local, mesh=mesh, in_specs=in_specs, out_specs=out_specs, check_vma=False)
```

time: 435 us -> 226 us (0.52)
  starting transfers between devices: 120 us -> 27.8 us
  Pallas kernels: 0 us -> 71.9 us
  local copies, waits for them, and re-layouts: 74.1 us -> 2.2 us
  other arithmetic: 63.9 us -> 0.08 us
  waiting for transfers between devices: 165 us -> 124 us
  matrix products: 6.82 us -> 0 us
    ppermute x33 -> x5, starting transfers between devices: 104 us -> 11.7 us  [the longest x4 11.6 us: shifted(): return lax.ppermute(block, axis, route)]
    pallas_call x0 -> x6, Pallas kernels: none -> 71.9 us  [the longest x1 40.3 us: relax(): pl.pallas_call(relax_kernel, out_shape=jax.ShapeDtypeStruct(merged.shape,...]
    scatter x1 -> x0, local copies, waits for them, and re-layouts: 51.4 us -> none  [local(): arrival.at[into_cells // cells, :, into_cells % cells].set(received)]
    div x8 -> x0, other arithmetic: 50.3 us -> none  [the longest x7 50.3 us: local(): balanced = (merged + coeff * neighbours) / diagonal]
    ppermute x33 -> x5, waiting for transfers between devices: 46.1 us -> 9.14 us  [the longest x4 7.88 us: shifted(): return lax.ppermute(block, axis, route)]
    gather x3 -> x0, local copies, waits for them, and re-layouts: 12.1 us -> none  [the longest x1 5.49 us: local(): strip_vals = arrival[from_cells // cells, :, from_cells % cells]]
    broadcast_in_dim x1 -> x0, other arithmetic: 7.31 us -> none  [local(): return balanced[None]]
    dot_general x2 -> x0, matrix products: 6.82 us -> none  [the longest x1 5.53 us: local(): jnp.einsum('xgj,xjc->xgc', fetched, banded, precision=lax.Precision.HIGHEST)]
  transfers between devices with their start and end apart: 34 -> 6, of which waited for: 23 -> 6; matrix products, arithmetic and copies ran while one was open for 1% -> 0% of each run, Pallas kernels for 0% -> 2%
where the time goes in v1:
time: 226 us
  waiting for transfers between devices  124 us (55%)
  Pallas kernels  71.9 us (32%)
  starting transfers between devices  27.8 us (12%)
    all_to_all x1, waiting for transfers between devices, local(): lax.all_to_all(outgoing, ('gx', 'gy'), split_axis=0, concat_axis=0, tiled...  115 us
    pallas_call x1, Pallas kernels, relax(): pl.pallas_call(relax_kernel, out_shape=jax.ShapeDtypeStruct(merged.shape,...  40.3 us
    all_to_all x1, starting transfers between devices, local(): lax.all_to_all(outgoing, ('gx', 'gy'), split_axis=0, concat_axis=0, tiled...  16.1 us
    pallas_call x1, Pallas kernels, arrive(): pl.pallas_call(arrive_kernel, out_shape=(jax.ShapeDtypeStruct(coupled.sha...  14.8 us
    ppermute x4, starting transfers between devices, shifted(): return lax.ppermute(block, axis, route)  11.6 us
    pallas_call x1, Pallas kernels, merge(): pl.pallas_call(merge_kernel, out_shape=(jax.ShapeDtypeStruct(arrival.shap...  9.79 us
    ppermute x4, waiting for transfers between devices, shifted(): return lax.ppermute(block, axis, route)  7.88 us
  transfers between devices with their start and end apart: 6, of which 6 were waited for; matrix products, arithmetic and copies ran while one was open for 0% of the time, Pallas kernels for 2%

profile of v1, /device:TPU:2, one launch (start us, length us, event | category | flops | bytes accessed | tf_op | source)
XLA Modules:
  0.0 226.0 jit_solution(12821459502645400042)
XLA Ops:
  0.0 1.3 copy-done
  1.3 0.7 copy-done.6
  2.0 2.6 %pack_blocks.1 = f32[128,2,40,128]{3,2,1,0:T(8,128)} custom-call(s32[2,128]{1,0:T(2,128)S(1)} %bitcast.23, f32[64,40,128]{2,1,0:T(8,128)S(1)} %bitcast.16), custom_call_target="tpu_custom_call" | custom-call | tf_op jit(solution)/shard_map/pack_blocks/pallas_call | solution.py:55
  4.6 0.0 copy-start.8
  4.6 0.0 copy-start.1
  4.6 16.1 %all-to-all-start = ((f32[128,2,40,128]{3,2,1,0:T(8,128)}), f32[128,2,40,128]{3,2,1,0:T(8,128)}, u32[]{:S(2)}, u32[]{:S(2)}) async-start(f32[128,2,40,128]{3,2,1,0:T(8,128)} %pack_blocks.1), calls=%async_computation | async-start | bytes 10485760 | tf_op jit(solution)/shard_map/all_to_all | solution.py:344
  20.7 0.0 copy-done.8
  20.7 0.1 copy.10
  20.8 0.0 copy-start.3
  20.8 0.0 copy-start.4
  20.8 0.0 copy-start.7
  20.8 4.3 %couple.1.coupled = f32[64,40,128]{2,1,0:T(8,128)S(1)} custom-call(f32[64,40,128]{2,1,0:T(8,128)S(1)} %bitcast.17, f32[40,40]{1,0:T(8,128)S(1)} %bitcast.18), custom_call_target="tpu_custom_call" | custom-call | flops 157286400 | bytes 2621440 | tf_op jit(solution)/shard_map/couple/pallas_call | solution.py:77
  25.1 114.7 %all-to-all-done = f32[128,2,40,128]{3,2,1,0:T(8,128)} async-done(((f32[128,2,40,128]{3,2,1,0:T(8,128)}), f32[128,2,40,128]{3,2,1,0:T(8,128)}, u32[]{:S(2)}, u32[]{:S(2)}) %all-to-all-start) | async-done | bytes 5242912 | tf_op jit(solution)/shard_map/all_to_all | solution.py:344
  139.9 0.0 copy-done.2
  139.9 0.0 copy-done.4
  139.9 0.0 copy-start.5
  139.9 14.8 %arrive.1 = (f32[64,40,128]{2,1,0:T(8,128)S(1)}, f32[40,512]{1,0:T(8,128)S(1)}) custom-call(s32[1,64]{1,0:T(1,128)S(1)} %copy-done.7, s32[1,512]{1,0:T(1,128)S(1)} %bitcast.21, f32[256,40,128]{2,1,0:T(8,128)} %bitcast.9.slots, f32[64,40,128]{2,1,0:T(8,128)S(1)} %couple.1.coupled, s32[64,128]{1,0:T(8,128)S(1)} %bitcast.19, f32[64,128]{1,0:T(8,128)S(1)} %bitcast.20), custom_call_target="tpu_custom_call" | custom-call | tf_op jit(solution)/shard_map/arrive/pallas_call | solution.py:133
  154.7 0.1 collective-permute-start
  154.8 1.3 collective-permute-done.received
  156.1 9.8 %merge.1 = (f32[64,40,128]{2,1,0:T(8,128)S(1)}, f32[4,40,128]{2,1,0:T(8,128)S(1)}, f32[4,40,128]{2,1,0:T(8,128)S(1)}) custom-call(s32[1,512]{1,0:T(1,128)S(1)} %bitcast.22, f32[64,40,128]{2,1,0:T(8,128)S(1)} %get-tuple-element.12.arrival, f32[40,512]{1,0:T(8,128)S(1)} %collective-permute-done.received), custom_call_target="tpu_custom_call" | custom-call | tf_op jit(solution)/shard_map/merge/pallas_call | solution.py:180
  165.9 2.4 %collective-permute-start.1 = (f32[4,40,128]{2,1,0:T(8,128)S(1)}, f32[4,40,128]{2,1,0:T(8,128)S(1)}, u32[]{:S(2)}, u32[]{:S(2)}) collective-permute-start(f32[4,40,128]{2,1,0:T(8,128)S(1)} %get-tuple-element.15), channel_id=1, source_target_pairs={{0,1},{1,2},{2,3},{4,5},{5,6},{6,7},{8,9},{9,10},{10,11},{12,13},{... | collective-permute-start | bytes 245768 | tf_op jit(solution)/shard_map/ppermute | solution.py:327
  168.3 1.3 collective-permute-start.2
  169.6 0.7 collective-permute-done.1.left
  170.3 4.3 %collective-permute-done.2.right = f32[4,40,128]{2,1,0:T(8,128)S(1)} collective-permute-done((f32[4,40,128]{2,1,0:T(8,128)S(1)}, f32[4,40,128]{2,1,0:T(8,128)S(1)}, u32[]{:S(2)}, u32[]{:S(2)}) %collective-permute-start.2) | collective-permute-done | bytes 81952 | tf_op jit(solution)/shard_map/ppermute | solution.py:327
  174.6 0.1 edge_rows.1
  174.7 2.4 %collective-permute-start.3 = (f32[9,40,128]{2,1,0:T(8,128)S(1)}, f32[9,40,128]{2,1,0:T(8,128)S(1)}, u32[]{:S(2)}, u32[]{:S(2)}) collective-permute-start(f32[9,40,128]{2,1,0:T(8,128)S(1)} %get-tuple-element.17), channel_id=1, source_target_pairs={{0,4},{4,8},{8,12},{12,16},{16,20},{20,24},{24,28},{28,32},{32,36}... | collective-permute-start | bytes 552968 | tf_op jit(solution)/shard_map/ppermute | solution.py:327
  177.1 5.6 %collective-permute-start.4 = (f32[9,40,128]{2,1,0:T(8,128)S(1)}, f32[9,40,128]{2,1,0:T(8,128)S(1)}, u32[]{:S(2)}, u32[]{:S(2)}) collective-permute-start(f32[9,40,128]{2,1,0:T(8,128)S(1)} %get-tuple-element.18), channel_id=1, source_target_pairs={{4,0},{8,4},{12,8},{16,12},{20,16},{24,20},{28,24},{32,28},{36,32}... | collective-permute-start | bytes 552968 | tf_op jit(solution)/shard_map/ppermute | solution.py:327
  182.7 0.1 copy.11.coef
  182.8 0.1 add_convert_fusion.inside
  182.8 1.4 collective-permute-done.3.above
  184.2 1.5 collective-permute-done.4.below
  185.7 40.3 %relax.1 = f32[64,40,128]{2,1,0:T(8,128)} custom-call(s32[4]{0:T(128)S(1)} %add_convert_fusion.inside, f32[64,40,128]{2,1,0:T(8,128)S(1)} %get-tuple-element.14.merged, f32[9,40,128]{2,1,0:T(8,128)S(1)} %collective-permute-done.3.above, f32[9,40,128]{2,1,0:T(8,128)S(1)} %collective-permute-done.4.below, f32[4,40,128]{2,1,0:T(8,128)S(1)} %collective-permute-done.1.left, ...), custom_call_target="tpu_custom_call" | custom-call | tf_op jit(solution)/shard_map/relax/pallas_call | solution.py:313
  (9 shorter events, 0.0 us)
Async XLA Ops:
  0.0 1.3 copy-start
  1.3 0.7 copy-start.6
  4.6 16.1 %copy-start.8 = (f32[40,40]{1,0:T(8,128)S(1)}, f32[40,40]{1,0:T(8,128)}, u32[]{:S(2)}) copy-start(f32[40,40]{1,0:T(8,128)} %param.17) | copy-start | bytes 19204
  4.6 16.2 %copy-start.1 = (f32[1,64,40,128]{3,2,1,0:T(8,128)S(1)}, f32[1,64,40,128]{3,2,1,0:T(8,128)}, u32[]{:S(2)}) copy-start(f32[1,64,40,128]{3,2,1,0:T(8,128)} %param.9) | copy-start | bytes 3932164
  4.6 135.3 %all-to-all-start = ((f32[128,2,40,128]{3,2,1,0:T(8,128)}), f32[128,2,40,128]{3,2,1,0:T(8,128)}, u32[]{:S(2)}, u32[]{:S(2)}) async-start(f32[128,2,40,128]{3,2,1,0:T(8,128)} %pack_blocks.1), calls=%async_computation | async-start | bytes 10485760 | tf_op jit(solution)/shard_map/all_to_all | solution.py:344
  20.8 119.1 %copy-start.2 = (s32[1,64,128]{2,1,0:T(8,128)S(1)}, s32[1,64,128]{2,1,0:T(8,128)}, u32[]{:S(2)}) copy-start(s32[1,64,128]{2,1,0:T(8,128)} %param.11) | copy-start | bytes 98308
  20.8 119.1 %copy-start.3 = (f32[1,64,128]{2,1,0:T(8,128)S(1)}, f32[1,64,128]{2,1,0:T(8,128)}, u32[]{:S(2)}) copy-start(f32[1,64,128]{2,1,0:T(8,128)} %param.10) | copy-start | bytes 98308
  20.8 119.1 %copy-start.4 = (s32[1,1,512]{2,1,0:T(1,128)S(1)}, s32[1,1,512]{2,1,0:T(1,128)}, u32[]{:S(2)}) copy-start(s32[1,1,512]{2,1,0:T(1,128)} %param.14) | copy-start | bytes 6148
  20.8 119.1 %copy-start.7 = (s32[1,64]{1,0:T(1,128)S(1)}, s32[1,64]{1,0:T(1,128)}, u32[]{:S(2)}) copy-start(s32[1,64]{1,0:T(1,128)} %rows.1) | copy-start | bytes 772
  139.9 16.1 %copy-start.5 = (s32[1,1,512]{2,1,0:T(1,128)S(1)}, s32[1,1,512]{2,1,0:T(1,128)}, u32[]{:S(2)}) copy-start(s32[1,1,512]{2,1,0:T(1,128)} %param.15) | copy-start | bytes 6148
  154.7 1.4 collective-permute-start
  156.1 26.6 %copy-start.9 = (f32[40]{0:T(128)S(1)}, f32[40]{0:T(128)}, u32[]{:S(2)}) copy-start(f32[40]{0:T(128)} %param.16) | copy-start | bytes 484
  165.9 4.4 %collective-permute-start.1 = (f32[4,40,128]{2,1,0:T(8,128)S(1)}, f32[4,40,128]{2,1,0:T(8,128)S(1)}, u32[]{:S(2)}, u32[]{:S(2)}) collective-permute-start(f32[4,40,128]{2,1,0:T(8,128)S(1)} %get-tuple-element.15), channel_id=1, source_target_pairs={{0,1},{1,2},{2,3},{4,5},{5,6},{6,7},{8,9},{9,10},{10,11},{12,13},{... | collective-permute-start | bytes 245768 | tf_op jit(solution)/shard_map/ppermute | solution.py:327
  168.3 6.3 %collective-permute-start.2 = (f32[4,40,128]{2,1,0:T(8,128)S(1)}, f32[4,40,128]{2,1,0:T(8,128)S(1)}, u32[]{:S(2)}, u32[]{:S(2)}) collective-permute-start(f32[4,40,128]{2,1,0:T(8,128)S(1)} %get-tuple-element.16), channel_id=1, source_target_pairs={{1,0},{2,1},{3,2},{5,4},{6,5},{7,6},{9,8},{10,9},{11,10},{13,12},{... | collective-permute-start | bytes 245768 | tf_op jit(solution)/shard_map/ppermute | solution.py:327
  174.7 9.5 %collective-permute-start.3 = (f32[9,40,128]{2,1,0:T(8,128)S(1)}, f32[9,40,128]{2,1,0:T(8,128)S(1)}, u32[]{:S(2)}, u32[]{:S(2)}) collective-permute-start(f32[9,40,128]{2,1,0:T(8,128)S(1)} %get-tuple-element.17), channel_id=1, source_target_pairs={{0,4},{4,8},{8,12},{12,16},{16,20},{20,24},{24,28},{28,32},{32,36}... | collective-permute-start | bytes 552968 | tf_op jit(solution)/shard_map/ppermute | solution.py:327
  177.1 8.6 %collective-permute-start.4 = (f32[9,40,128]{2,1,0:T(8,128)S(1)}, f32[9,40,128]{2,1,0:T(8,128)S(1)}, u32[]{:S(2)}, u32[]{:S(2)}) collective-permute-start(f32[9,40,128]{2,1,0:T(8,128)S(1)} %get-tuple-element.18), channel_id=1, source_target_pairs={{4,0},{8,4},{12,8},{16,12},{20,16},{24,20},{28,24},{32,28},{36,32}... | collective-permute-start | bytes 552968 | tf_op jit(solution)/shard_map/ppermute | solution.py:327

commit v2 on v1

--- a/solution.py
+++ b/solution.py
@@ -115,7 +115,7 @@
             out[r, c : c + SUB, :] = total
         return carry
 
-    lax.fori_loop(0, count, row, 0, unroll=2)
+    lax.fori_loop(0, count, row, 0, unroll=16)
 
     lane = lax.broadcasted_iota(jnp.int32, (chan, cells), 1)
     for part in range(picked.shape[1] // cells):
@@ -125,7 +125,7 @@
             moved = pltpu.roll(out[place // cells], (j - place % cells) & (cells - 1), 1)
             return jnp.where(lane == j, moved, held)
 
-        held = lax.fori_loop(0, cells, pick, jnp.zeros((chan, cells), F32), unroll=8)
+        held = lax.fori_loop(0, cells, pick, jnp.zeros((chan, cells), F32), unroll=True)
         picked[:, part * cells : (part + 1) * cells] = held
 
 
@@ -159,7 +159,7 @@
             pltpu.store(out.at[place // cells], moved, mask=lane == at)
             return carry
 
-        lax.fori_loop(0, cells, put, 0, unroll=8)
+        lax.fori_loop(0, cells, put, 0, unroll=32)
     per = cells // WIDTH
     for g in range(count // per):
 
@@ -171,7 +171,7 @@
             return jnp.where(here, first, held[0]), jnp.where(here, last, held[1])
 
         empty = jnp.zeros((chan, cells), F32)
-        low[g], high[g] = lax.fori_loop(0, per, edge, (empty, empty), unroll=4)
+        low[g], high[g] = lax.fori_loop(0, per, edge, (empty, empty), unroll=True)
 
 
 def merge(strip, arrival, received):
@@ -211,49 +211,38 @@
     )(merged, left, right)
 
 
-def relax_kernel(inside, merged, above, below, left, right, coef, out, m0, m1, a0, a1, b0, b1):
+def relax_kernel(inside, merged, above, below, left, right, coef, out, a0, a1, b0, b1, start1):
     count, chan, cells = merged.shape
     lane = lax.broadcasted_iota(jnp.int32, (chan, cells), 1)
     is_right, is_left = lane < WIDTH, lane >= cells - WIDTH
     h = coef[...]
     inv = 1.0 / (1.0 + 4.0 * h)
-    inv_b = jnp.broadcast_to(inv, (chan, cells))
     total = count + 2 * WIDTH
     per = cells // WIDTH
     half = cells // 2
 
-    def load(at, row, beside):
-        a0[at] = row
-        m0[at] = row * inv_b
-        a1[at] = beside
-        m1[at] = beside * inv_b
-
     for at, rows in ((0, above), (WIDTH + count, below)):
         for i in range(WIDTH):
             packed = rows[WIDTH]
-            beside = jnp.where(
+            start1[at + i] = jnp.where(
                 is_right,
                 pltpu.roll(packed, (-i * WIDTH) % cells, 1),
                 jnp.where(is_left, pltpu.roll(packed, (half - (i + 1) * WIDTH) % cells, 1), 0.0),
             )
-            load(at + i, rows[i], beside)
-    for g in range(left.shape[0]):
-
-        def fill(i, carry):
-            to_right = pltpu.roll(right[g], (cells - i * WIDTH) & (cells - 1), 1)
-            to_left = pltpu.roll(left[g], cells - (i + 1) * WIDTH, 1)
-            beside = jnp.where(is_right, to_right, jnp.where(is_left, to_left, 0.0))
-            r = g * per + i
-            load(WIDTH + r, merged[r], beside)
-            return carry
-
-        lax.fori_loop(0, per, fill, 0, unroll=4)
+    for r in range(count):
+        g, i = divmod(r, per)
+        start1[WIDTH + r] = jnp.where(
+            is_right,
+            pltpu.roll(right[g], (-i * WIDTH) % cells, 1),
+            jnp.where(is_left, pltpu.roll(left[g], (-(i + 1) * WIDTH) % cells, 1), 0.0),
+        )
 
     lane8 = lax.broadcasted_iota(jnp.int32, (SUB, cells), 1)
     is_first, is_last = lane8 == 0, lane8 == cells - 1
     side = jnp.where(
         lane8 < WIDTH, inside[3], jnp.where(lane8 >= cells - WIDTH, inside[2], 0)
     ).astype(F32)
+    lo, hi = inside[0].astype(F32), inside[1].astype(F32)
 
     def turn(row, beside):
         l0, l1 = pltpu.roll(row, 1, 1), pltpu.roll(beside, 1, 1)
@@ -263,48 +252,40 @@
             jnp.where(is_first, l0, l1) + jnp.where(is_last, r0, r1),
         )
 
+    def first_row(x, ch):
+        if x < WIDTH:
+            return above[x, ch]
+        return merged[x - WIDTH, ch] if x < WIDTH + count else below[x - WIDTH - count, ch]
+
     for c in range(0, chan, SUB):
         ch = slice(c, c + SUB)
+        inv8 = jnp.broadcast_to(inv[ch], (SUB, cells))
         gain = jnp.broadcast_to(h[ch] * inv[ch], (SUB, cells))
         gain_side = gain * side
-        lo = inside[0].astype(F32)
-        hi = inside[1].astype(F32)
 
         for s in range(SWEEPS):
-            src0, src1 = (a0, a1) if s % 2 == 0 else (b0, b1)
-            dst0, dst1 = (b0, b1) if s % 2 == 0 else (a0, a1)
-            last = s == SWEEPS - 1
+            now, later = ((a0, a1), (b0, b1))[:: 1 if s % 2 else -1]
             begin, end = s + 1, total - s - 1
 
-            def update(x, held, g0, g1):
-                up0, up1, mid0, mid1 = held
-                down0, down1 = src0[x + 1, ch], src1[x + 1, ch]
-                across0, across1 = turn(mid0, mid1)
-                new0 = m0[x, ch] + g0 * (up0 + down0 + across0)
-                if last:
-                    out[x - WIDTH, ch] = new0
+            def held(x):
+                if s == 0:
+                    return first_row(x, ch), start1[x, ch]
+                return now[0][x, ch], now[1][x, ch]
+
+            up, mid = held(begin - 1), held(begin)
+            for x in range(begin, end):
+                down = held(x + 1)
+                across = turn(*mid)
+                part = lo if x < WIDTH else hi if x >= WIDTH + count else None
+                g0 = gain if part is None else gain * part
+                new = first_row(x, ch) * inv8 + g0 * (up[0] + down[0] + across[0])
+                if s == SWEEPS - 1:
+                    out[x - WIDTH, ch] = new
                 else:
-                    dst0[x, ch] = new0
-                    dst1[x, ch] = m1[x, ch] + g1 * (up1 + down1 + across1)
-                return mid0, mid1, down0, down1
-
-            held = (
-                src0[begin - 1, ch],
-                src1[begin - 1, ch],
-                src0[begin, ch],
-                src1[begin, ch],
-            )
-            for x in range(begin, WIDTH):
-                held = update(x, held, gain * lo, gain_side * lo)
-            held = lax.fori_loop(
-                WIDTH,
-                WIDTH + count,
-                lambda x, v: update(x, v, gain, gain_side),
-                held,
-                unroll=8,
-            )
-            for x in range(WIDTH + count, end):
-                held = update(x, held, gain * hi, gain_side * hi)
+                    later[0][x, ch] = new
+                    g1 = gain_side if part is None else gain_side * part
+                    later[1][x, ch] = start1[x, ch] * inv8 + g1 * (up[1] + down[1] + across[1])
+                up, mid = mid, down
 
 
 def relax(inside, merged, above, below, left, right, coef):
@@ -315,7 +296,7 @@
         out_shape=jax.ShapeDtypeStruct(merged.shape, F32),
         in_specs=[whole(pltpu.SMEM)] + [whole()] * 6,
         out_specs=whole(),
-        scratch_shapes=[held] * 6,
+        scratch_shapes=[held] * 5,
         compiler_params=params(),
         name="relax",
     )(inside, merged, above, below, left, right, coef)

time: 226 us -> 192 us (0.85)
  Pallas kernels: 71.9 us -> 37.1 us
    pallas_call x1, Pallas kernels: 40.3 us -> 14.4 us  [relax(): pl.pallas_call(relax_kernel, out_shape=jax.ShapeDtypeStruct(merged.shape,...]
    pallas_call x1, Pallas kernels: 14.8 us -> 9.7 us  [arrive(): pl.pallas_call(arrive_kernel, out_shape=(jax.ShapeDtypeStruct(coupled.sha...]
    pallas_call x1, Pallas kernels: 9.79 us -> 6.1 us  [merge(): pl.pallas_call(merge_kernel, out_shape=(jax.ShapeDtypeStruct(arrival.shap...]
where the time goes in v2:
time: 192 us; the launch traced here: 191 us
  waiting for transfers between devices  124 us (65%)
  Pallas kernels  37.1 us (19%)
  starting transfers between devices  28.1 us (15%)
  local copies, waits for them, and re-layouts  2.2 us (1%)
    all_to_all x1, waiting for transfers between devices, local(): lax.all_to_all(outgoing, ('gx', 'gy'), split_axis=0, concat_axis=0, tiled...  115 us
    all_to_all x1, starting transfers between devices, local(): lax.all_to_all(outgoing, ('gx', 'gy'), split_axis=0, concat_axis=0, tiled...  16.1 us
    pallas_call x1, Pallas kernels, relax(): pl.pallas_call(relax_kernel, out_shape=jax.ShapeDtypeStruct(merged.shape,...  14.4 us
    ppermute x4, starting transfers between devices, shifted(): return lax.ppermute(block, axis, route)  11.8 us
    pallas_call x1, Pallas kernels, arrive(): pl.pallas_call(arrive_kernel, out_shape=(jax.ShapeDtypeStruct(coupled.sha...  9.7 us
    ppermute x4, waiting for transfers between devices, shifted(): return lax.ppermute(block, axis, route)  7.7 us
    pallas_call x1, Pallas kernels, merge(): pl.pallas_call(merge_kernel, out_shape=(jax.ShapeDtypeStruct(arrival.shap...  6.1 us
    pallas_call x1, Pallas kernels, couple(): pl.pallas_call(couple_kernel, out_shape=jax.ShapeDtypeStruct(tile.shape,...  4.33 us
  transfers between devices with their start and end apart: 6, of which 6 were waited for; matrix products, arithmetic and copies ran while one was open for 0% of the time, Pallas kernels for 2%

profile of v2, /device:TPU:2, one launch (start us, length us, event | category | flops | bytes accessed | tf_op | source)
XLA Modules:
  0.0 191.4 jit_solution(684941520187773095)
XLA Ops:
  0.0 1.3 copy-done
  1.3 0.7 copy-done.6
  2.0 2.5 %pack_blocks.1 = f32[128,2,40,128]{3,2,1,0:T(8,128)} custom-call(s32[2,128]{1,0:T(2,128)S(1)} %bitcast.23, f32[64,40,128]{2,1,0:T(8,128)S(1)} %bitcast.16), custom_call_target="tpu_custom_call" | custom-call | tf_op jit(solution)/shard_map/pack_blocks/pallas_call | solution.py:55
  4.5 0.0 copy-start.8
  4.5 0.0 copy-start.1
  4.5 16.1 %all-to-all-start = ((f32[128,2,40,128]{3,2,1,0:T(8,128)}), f32[128,2,40,128]{3,2,1,0:T(8,128)}, u32[]{:S(2)}, u32[]{:S(2)}) async-start(f32[128,2,40,128]{3,2,1,0:T(8,128)} %pack_blocks.1), calls=%async_computation | async-start | bytes 10485760 | tf_op jit(solution)/shard_map/all_to_all | solution.py:325
  20.7 0.0 copy-done.8
  20.7 0.1 copy.10
  20.8 0.0 copy-done.1
  20.8 0.0 copy-start.3
  20.8 0.0 copy-start.4
  20.8 0.0 copy-start.7
  20.8 4.3 %couple.1.coupled = f32[64,40,128]{2,1,0:T(8,128)S(1)} custom-call(f32[64,40,128]{2,1,0:T(8,128)S(1)} %bitcast.17, f32[40,40]{1,0:T(8,128)S(1)} %bitcast.18), custom_call_target="tpu_custom_call" | custom-call | flops 157286400 | bytes 2621440 | tf_op jit(solution)/shard_map/couple/pallas_call | solution.py:77
  25.1 114.7 %all-to-all-done = f32[128,2,40,128]{3,2,1,0:T(8,128)} async-done(((f32[128,2,40,128]{3,2,1,0:T(8,128)}), f32[128,2,40,128]{3,2,1,0:T(8,128)}, u32[]{:S(2)}, u32[]{:S(2)}) %all-to-all-start) | async-done | bytes 5242912 | tf_op jit(solution)/shard_map/all_to_all | solution.py:325
  139.9 0.0 copy-done.4
  139.9 0.0 copy-start.5
  139.9 9.7 %arrive.1 = (f32[64,40,128]{2,1,0:T(8,128)S(1)}, f32[40,512]{1,0:T(8,128)S(1)}) custom-call(s32[1,64]{1,0:T(1,128)S(1)} %copy-done.7, s32[1,512]{1,0:T(1,128)S(1)} %bitcast.21, f32[256,40,128]{2,1,0:T(8,128)} %bitcast.9.slots, f32[64,40,128]{2,1,0:T(8,128)S(1)} %couple.1.coupled, s32[64,128]{1,0:T(8,128)S(1)} %bitcast.19, f32[64,128]{1,0:T(8,128)S(1)} %bitcast.20), custom_call_target="tpu_custom_call" | custom-call | tf_op jit(solution)/shard_map/arrive/pallas_call | solution.py:133
  149.6 0.1 collective-permute-start
  149.7 1.3 collective-permute-done.received
  151.0 6.1 %merge.1 = (f32[64,40,128]{2,1,0:T(8,128)S(1)}, f32[4,40,128]{2,1,0:T(8,128)S(1)}, f32[4,40,128]{2,1,0:T(8,128)S(1)}) custom-call(s32[1,512]{1,0:T(1,128)S(1)} %bitcast.22, f32[64,40,128]{2,1,0:T(8,128)S(1)} %get-tuple-element.12.arrival, f32[40,512]{1,0:T(8,128)S(1)} %collective-permute-done.received), custom_call_target="tpu_custom_call" | custom-call | tf_op jit(solution)/shard_map/merge/pallas_call | solution.py:180
  157.1 2.4 %collective-permute-start.1 = (f32[4,40,128]{2,1,0:T(8,128)S(1)}, f32[4,40,128]{2,1,0:T(8,128)S(1)}, u32[]{:S(2)}, u32[]{:S(2)}) collective-permute-start(f32[4,40,128]{2,1,0:T(8,128)S(1)} %get-tuple-element.15), channel_id=1, source_target_pairs={{0,1},{1,2},{2,3},{4,5},{5,6},{6,7},{8,9},{9,10},{10,11},{12,13},{... | collective-permute-start | bytes 245768 | tf_op jit(solution)/shard_map/ppermute | solution.py:308
  159.5 1.3 collective-permute-start.2
  160.8 0.7 collective-permute-done.1.left
  161.6 4.3 %collective-permute-done.2.right = f32[4,40,128]{2,1,0:T(8,128)S(1)} collective-permute-done((f32[4,40,128]{2,1,0:T(8,128)S(1)}, f32[4,40,128]{2,1,0:T(8,128)S(1)}, u32[]{:S(2)}, u32[]{:S(2)}) %collective-permute-start.2) | collective-permute-done | bytes 81952 | tf_op jit(solution)/shard_map/ppermute | solution.py:308
  165.9 0.1 edge_rows.1
  166.0 2.3 %collective-permute-start.3 = (f32[9,40,128]{2,1,0:T(8,128)S(1)}, f32[9,40,128]{2,1,0:T(8,128)S(1)}, u32[]{:S(2)}, u32[]{:S(2)}) collective-permute-start(f32[9,40,128]{2,1,0:T(8,128)S(1)} %get-tuple-element.17), channel_id=1, source_target_pairs={{0,4},{4,8},{8,12},{12,16},{16,20},{20,24},{24,28},{28,32},{32,36}... | collective-permute-start | bytes 552968 | tf_op jit(solution)/shard_map/ppermute | solution.py:308
  168.3 5.8 %collective-permute-start.4 = (f32[9,40,128]{2,1,0:T(8,128)S(1)}, f32[9,40,128]{2,1,0:T(8,128)S(1)}, u32[]{:S(2)}, u32[]{:S(2)}) collective-permute-start(f32[9,40,128]{2,1,0:T(8,128)S(1)} %get-tuple-element.18), channel_id=1, source_target_pairs={{4,0},{8,4},{12,8},{16,12},{20,16},{24,20},{28,24},{32,28},{36,32}... | collective-permute-start | bytes 552968 | tf_op jit(solution)/shard_map/ppermute | solution.py:308
  174.1 0.1 copy.11.coef
  174.2 0.1 add_convert_fusion.inside
  174.3 1.2 collective-permute-done.3.above
  175.5 1.5 collective-permute-done.4.below
  176.9 14.4 %relax.1 = f32[64,40,128]{2,1,0:T(8,128)} custom-call(s32[4]{0:T(128)S(1)} %add_convert_fusion.inside, f32[64,40,128]{2,1,0:T(8,128)S(1)} %get-tuple-element.14.merged, f32[9,40,128]{2,1,0:T(8,128)S(1)} %collective-permute-done.3.above, f32[9,40,128]{2,1,0:T(8,128)S(1)} %collective-permute-done.4.below, f32[4,40,128]{2,1,0:T(8,128)S(1)} %collective-permute-done.1.left, ...), custom_call_target="tpu_custom_call" | custom-call | tf_op jit(solution)/shard_map/relax/pallas_call | solution.py:294
  (9 shorter events, 0.0 us)
Async XLA Ops:
  0.0 1.3 copy-start
  1.3 0.7 copy-start.6
  4.5 16.2 %copy-start.8 = (f32[40,40]{1,0:T(8,128)S(1)}, f32[40,40]{1,0:T(8,128)}, u32[]{:S(2)}) copy-start(f32[40,40]{1,0:T(8,128)} %param.17) | copy-start | bytes 19204
  4.5 16.2 %copy-start.1 = (f32[1,64,40,128]{3,2,1,0:T(8,128)S(1)}, f32[1,64,40,128]{3,2,1,0:T(8,128)}, u32[]{:S(2)}) copy-start(f32[1,64,40,128]{3,2,1,0:T(8,128)} %param.9) | copy-start | bytes 3932164
  4.5 135.4 %all-to-all-start = ((f32[128,2,40,128]{3,2,1,0:T(8,128)}), f32[128,2,40,128]{3,2,1,0:T(8,128)}, u32[]{:S(2)}, u32[]{:S(2)}) async-start(f32[128,2,40,128]{3,2,1,0:T(8,128)} %pack_blocks.1), calls=%async_computation | async-start | bytes 10485760 | tf_op jit(solution)/shard_map/all_to_all | solution.py:325
  20.8 119.1 %copy-start.2 = (s32[1,64,128]{2,1,0:T(8,128)S(1)}, s32[1,64,128]{2,1,0:T(8,128)}, u32[]{:S(2)}) copy-start(s32[1,64,128]{2,1,0:T(8,128)} %param.11) | copy-start | bytes 98308
  20.8 119.1 %copy-start.3 = (f32[1,64,128]{2,1,0:T(8,128)S(1)}, f32[1,64,128]{2,1,0:T(8,128)}, u32[]{:S(2)}) copy-start(f32[1,64,128]{2,1,0:T(8,128)} %param.10) | copy-start | bytes 98308
  20.8 119.1 %copy-start.4 = (s32[1,1,512]{2,1,0:T(1,128)S(1)}, s32[1,1,512]{2,1,0:T(1,128)}, u32[]{:S(2)}) copy-start(s32[1,1,512]{2,1,0:T(1,128)} %param.14) | copy-start | bytes 6148
  20.8 119.1 %copy-start.7 = (s32[1,64]{1,0:T(1,128)S(1)}, s32[1,64]{1,0:T(1,128)}, u32[]{:S(2)}) copy-start(s32[1,64]{1,0:T(1,128)} %rows.1) | copy-start | bytes 772
  139.9 11.1 %copy-start.5 = (s32[1,1,512]{2,1,0:T(1,128)S(1)}, s32[1,1,512]{2,1,0:T(1,128)}, u32[]{:S(2)}) copy-start(s32[1,1,512]{2,1,0:T(1,128)} %param.15) | copy-start | bytes 6148
  149.6 1.4 collective-permute-start
  151.0 23.1 %copy-start.9 = (f32[40]{0:T(128)S(1)}, f32[40]{0:T(128)}, u32[]{:S(2)}) copy-start(f32[40]{0:T(128)} %param.16) | copy-start | bytes 484
  157.1 4.5 %collective-permute-start.1 = (f32[4,40,128]{2,1,0:T(8,128)S(1)}, f32[4,40,128]{2,1,0:T(8,128)S(1)}, u32[]{:S(2)}, u32[]{:S(2)}) collective-permute-start(f32[4,40,128]{2,1,0:T(8,128)S(1)} %get-tuple-element.15), channel_id=1, source_target_pairs={{0,1},{1,2},{2,3},{4,5},{5,6},{6,7},{8,9},{9,10},{10,11},{12,13},{... | collective-permute-start | bytes 245768 | tf_op jit(solution)/shard_map/ppermute | solution.py:308
  159.5 6.3 %collective-permute-start.2 = (f32[4,40,128]{2,1,0:T(8,128)S(1)}, f32[4,40,128]{2,1,0:T(8,128)S(1)}, u32[]{:S(2)}, u32[]{:S(2)}) collective-permute-start(f32[4,40,128]{2,1,0:T(8,128)S(1)} %get-tuple-element.16), channel_id=1, source_target_pairs={{1,0},{2,1},{3,2},{5,4},{6,5},{7,6},{9,8},{10,9},{11,10},{13,12},{... | collective-permute-start | bytes 245768 | tf_op jit(solution)/shard_map/ppermute | solution.py:308
  166.0 9.5 %collective-permute-start.3 = (f32[9,40,128]{2,1,0:T(8,128)S(1)}, f32[9,40,128]{2,1,0:T(8,128)S(1)}, u32[]{:S(2)}, u32[]{:S(2)}) collective-permute-start(f32[9,40,128]{2,1,0:T(8,128)S(1)} %get-tuple-element.17), channel_id=1, source_target_pairs={{0,4},{4,8},{8,12},{12,16},{16,20},{20,24},{24,28},{28,32},{32,36}... | collective-permute-start | bytes 552968 | tf_op jit(solution)/shard_map/ppermute | solution.py:308
  168.3 8.6 %collective-permute-start.4 = (f32[9,40,128]{2,1,0:T(8,128)S(1)}, f32[9,40,128]{2,1,0:T(8,128)S(1)}, u32[]{:S(2)}, u32[]{:S(2)}) collective-permute-start(f32[9,40,128]{2,1,0:T(8,128)S(1)} %get-tuple-element.18), channel_id=1, source_target_pairs={{4,0},{8,4},{12,8},{16,12},{20,16},{24,20},{28,24},{32,28},{36,32}... | collective-permute-start | bytes 552968 | tf_op jit(solution)/shard_map/ppermute | solution.py:308

commit v3 on v2

--- a/solution.py
+++ b/solution.py
@@ -9,9 +9,11 @@
 
 SWEEPS = 8
 WIDTH = 8
+PARTS = 4
 SUB = 8
 F32 = jnp.float32
 VMEM_LIMIT = 48 * 1024 * 1024
+PACK_LIMIT = 63 * 1024 * 1024
 
 
 def whole(space=pltpu.VMEM):
@@ -26,8 +28,13 @@
     return pl.CostEstimate(flops=flops, bytes_accessed=moved, transcendentals=0)
 
 
-def pack_kernel(wanted, tile, out, sem):
+def split(place, cells):
+    return lax.shift_right_logical(place, cells.bit_length() - 1), place & (cells - 1)
+
+
+def pack_kernel(listed, tile, out, wanted, sem):
     slots, tiles = wanted.shape
+    pltpu.sync_copy(listed, wanted)
 
     def send(d, sent):
         for k in range(slots):
@@ -41,7 +48,7 @@
             sent = sent + jnp.where(filled, 1, 0)
         return sent
 
-    sent = lax.fori_loop(0, tiles, send, 0)
+    sent = lax.fori_loop(0, tiles, send, 0, unroll=4)
 
     def wait(_, carry):
         pltpu.make_async_copy(tile.at[0], out.at[0, 0], sem).wait()
@@ -55,10 +62,10 @@
     return pl.pallas_call(
         pack_kernel,
         out_shape=jax.ShapeDtypeStruct((tiles, slots) + tile.shape[1:], F32),
-        in_specs=[whole(pltpu.SMEM), whole()],
+        in_specs=[whole(pltpu.HBM), whole(pltpu.HBM)],
         out_specs=whole(pl.ANY),
-        scratch_shapes=[pltpu.SemaphoreType.DMA],
-        compiler_params=params(),
+        scratch_shapes=[pltpu.SMEM(wanted.shape, jnp.int32), pltpu.SemaphoreType.DMA],
+        compiler_params=pltpu.CompilerParams(vmem_limit_bytes=PACK_LIMIT),
         name="pack_blocks",
     )(wanted, tile)
 
@@ -88,12 +95,16 @@
 def arrive_kernel(rows, strip, slots, coupled, cell, frac, out, picked, fetched, sem):
     count, chan, cells = out.shape
 
-    def fetch(r, carry):
-        pltpu.make_async_copy(slots.at[rows[0, r]], fetched.at[r], sem).start()
+    step = count // PARTS
+
+    def fetch(r, carry, part):
+        pltpu.make_async_copy(slots.at[rows[0, r]], fetched.at[r], sem.at[part]).start()
         return carry
 
-    lax.fori_loop(0, count, fetch, 0)
-    pltpu.make_async_copy(slots.at[pl.ds(0, count)], fetched, sem).wait()
+    for part in range(PARTS):
+        lax.fori_loop(
+            part * step, (part + 1) * step, functools.partial(fetch, part=part), 0, unroll=True
+        )
 
     def row(r, carry):
         t = frac[pl.ds(r, 1), :]
@@ -115,14 +126,18 @@
             out[r, c : c + SUB, :] = total
         return carry
 
-    lax.fori_loop(0, count, row, 0, unroll=16)
+    for part in range(PARTS):
+        here = pl.ds(part * step, step)
+        pltpu.make_async_copy(slots.at[here], fetched.at[here], sem.at[part]).wait()
+        lax.fori_loop(part * step, (part + 1) * step, row, 0, unroll=True)
 
     lane = lax.broadcasted_iota(jnp.int32, (chan, cells), 1)
     for part in range(picked.shape[1] // cells):
 
         def pick(j, held):
             place = strip[0, part * cells + j]
-            moved = pltpu.roll(out[place // cells], (j - place % cells) & (cells - 1), 1)
+            row, at = split(place, cells)
+            moved = pltpu.roll(out[row], (j - at) & (cells - 1), 1)
             return jnp.where(lane == j, moved, held)
 
         held = lax.fori_loop(0, cells, pick, jnp.zeros((chan, cells), F32), unroll=True)
@@ -138,13 +153,13 @@
         ),
         in_specs=[whole(pltpu.SMEM), whole(pltpu.SMEM), whole(pl.ANY), whole(), whole(), whole()],
         out_specs=(whole(), whole()),
-        scratch_shapes=[pltpu.VMEM(coupled.shape, F32), pltpu.SemaphoreType.DMA],
+        scratch_shapes=[pltpu.VMEM(coupled.shape, F32), pltpu.SemaphoreType.DMA((PARTS,))],
         compiler_params=params(),
         name="arrive",
     )(rows, strip, slots, coupled, cell, frac)
 
 
-def merge_kernel(strip, arrival, received, out, low, high):
+def merge_kernel(strip, arrival, received, out, low, high, first, last):
     count, chan, cells = out.shape
     out[...] = arrival[...]
     lane = lax.broadcasted_iota(jnp.int32, (chan, cells), 1)
@@ -152,23 +167,25 @@
 
         def put(j, carry):
             place = strip[0, part * cells + j]
-            at = place % cells
+            row, at = split(place, cells)
             moved = pltpu.roll(
                 received[:, part * cells : (part + 1) * cells], (at - j) & (cells - 1), 1
             )
-            pltpu.store(out.at[place // cells], moved, mask=lane == at)
+            pltpu.store(out.at[row], moved, mask=lane == at)
             return carry
 
         lax.fori_loop(0, cells, put, 0, unroll=32)
+    first[...] = out[:WIDTH]
+    last[...] = out[count - WIDTH :]
     per = cells // WIDTH
     for g in range(count // per):
 
         def edge(i, held):
             row = out[g * per + i]
             here = (lane // WIDTH) == i
-            first = pltpu.roll(row, i * WIDTH, 1)
-            last = pltpu.roll(row, (i + 1) * WIDTH & (cells - 1), 1)
-            return jnp.where(here, first, held[0]), jnp.where(here, last, held[1])
+            left = pltpu.roll(row, i * WIDTH, 1)
+            right = pltpu.roll(row, (i + 1) * WIDTH & (cells - 1), 1)
+            return jnp.where(here, left, held[0]), jnp.where(here, right, held[1])
 
         empty = jnp.zeros((chan, cells), F32)
         low[g], high[g] = lax.fori_loop(0, per, edge, (empty, empty), unroll=True)
@@ -177,41 +194,56 @@
 def merge(strip, arrival, received):
     count, chan, cells = arrival.shape
     edge = jax.ShapeDtypeStruct((count * WIDTH // cells, chan, cells), F32)
+    rows = jax.ShapeDtypeStruct((WIDTH, chan, cells), F32)
     return pl.pallas_call(
         merge_kernel,
-        out_shape=(jax.ShapeDtypeStruct(arrival.shape, F32), edge, edge),
+        out_shape=(jax.ShapeDtypeStruct(arrival.shape, F32), edge, edge, rows, rows),
         in_specs=[whole(pltpu.SMEM), whole(), whole()],
-        out_specs=(whole(), whole(), whole()),
+        out_specs=(whole(),) * 5,
         compiler_params=params(),
         name="merge",
     )(strip, arrival, received)
 
 
-def edge_rows_kernel(merged, left, right, first, last):
-    count, chan, cells = merged.shape
+def corners_kernel(left, right, first, last):
+    groups, chan, cells = left.shape
     lane = lax.broadcasted_iota(jnp.int32, (chan, cells), 1)
     half = cells // 2
-    groups = left.shape[0]
-    first[:WIDTH] = merged[:WIDTH]
-    first[WIDTH] = jnp.where(lane < half, right[0], pltpu.roll(left[0], half, 1))
-    last[:WIDTH] = merged[count - WIDTH :]
-    last[WIDTH] = jnp.where(lane < half, pltpu.roll(right[groups - 1], half, 1), left[groups - 1])
-
-
-def edge_rows(merged, left, right):
-    count, chan, cells = merged.shape
-    rows = jax.ShapeDtypeStruct((WIDTH + 1, chan, cells), F32)
-    return pl.pallas_call(
-        edge_rows_kernel,
-        out_shape=(rows, rows),
-        in_specs=[whole(), whole(), whole()],
+    first[...] = jnp.where(lane < half, right[0], pltpu.roll(left[0], half, 1))
+    last[...] = jnp.where(lane < half, pltpu.roll(right[groups - 1], half, 1), left[groups - 1])
+
+
+def corners(left, right):
+    held = jax.ShapeDtypeStruct(left.shape[1:], F32)
+    return pl.pallas_call(
+        corners_kernel,
+        out_shape=(held, held),
+        in_specs=[whole(), whole()],
         out_specs=(whole(), whole()),
         compiler_params=params(),
-        name="edge_rows",
-    )(merged, left, right)
-
-
-def relax_kernel(inside, merged, above, below, left, right, coef, out, a0, a1, b0, b1, start1):
+        name="corners",
+    )(left, right)
+
+
+def relax_kernel(
+    inside,
+    merged,
+    above,
+    below,
+    above_side,
+    below_side,
+    left,
+    right,
+    coef,
+    result,
+    out,
+    a0,
+    a1,
+    b0,
+    b1,
+    start1,
+    sem,
+):
     count, chan, cells = merged.shape
     lane = lax.broadcasted_iota(jnp.int32, (chan, cells), 1)
     is_right, is_left = lane < WIDTH, lane >= cells - WIDTH
@@ -221,9 +253,9 @@
     per = cells // WIDTH
     half = cells // 2
 
-    for at, rows in ((0, above), (WIDTH + count, below)):
+    for at, rows in ((0, above_side), (WIDTH + count, below_side)):
+        packed = rows[...]
         for i in range(WIDTH):
-            packed = rows[WIDTH]
             start1[at + i] = jnp.where(
                 is_right,
                 pltpu.roll(packed, (-i * WIDTH) % cells, 1),
@@ -286,20 +318,27 @@
                     g1 = gain_side if part is None else gain_side * part
                     later[1][x, ch] = start1[x, ch] * inv8 + g1 * (up[1] + down[1] + across[1])
                 up, mid = mid, down
-
-
-def relax(inside, merged, above, below, left, right, coef):
+        pltpu.make_async_copy(out.at[:, ch], result.at[:, ch], sem.at[c // SUB]).start()
+
+    for c in range(0, chan, SUB):
+        ch = slice(c, c + SUB)
+        pltpu.make_async_copy(out.at[:, ch], result.at[:, ch], sem.at[c // SUB]).wait()
+
+
+def relax(inside, merged, above, below, above_side, below_side, left, right, coef):
     count, chan, cells = merged.shape
     held = pltpu.VMEM((count + 2 * WIDTH, chan, cells), F32)
     return pl.pallas_call(
         relax_kernel,
         out_shape=jax.ShapeDtypeStruct(merged.shape, F32),
-        in_specs=[whole(pltpu.SMEM)] + [whole()] * 6,
-        out_specs=whole(),
-        scratch_shapes=[held] * 5,
+        in_specs=[whole(pltpu.SMEM)] + [whole()] * 8,
+        out_specs=whole(pl.ANY),
+        scratch_shapes=[pltpu.VMEM(merged.shape, F32)]
+        + [held] * 5
+        + [pltpu.SemaphoreType.DMA((chan // SUB,))],
         compiler_params=params(),
         name="relax",
-    )(inside, merged, above, below, left, right, coef)
+    )(inside, merged, above, below, above_side, below_side, left, right, coef)
 
 
 def shifted(block, axis, step):
@@ -329,18 +368,28 @@
         row_source, strip_from[0], slots, coupled, depart_cell[0], depart_frac[0]
     )
     received = lax.ppermute(picked, "panel", [(0, 1), (1, 0)])
-    merged, low, high = merge(strip_into[0], arrival, received)
+    merged, low, high, first, last = merge(strip_into[0], arrival, received)
     right = shifted(low, "gy", -1)
     left = shifted(high, "gy", 1)
-    first, last = edge_rows(merged, left, right)
     below = shifted(first, "gx", -1)
     above = shifted(last, "gx", 1)
+    first_side, last_side = corners(left, right)
+    below_side = shifted(first_side, "gx", -1)
+    above_side = shifted(last_side, "gx", 1)
     gx, gy = lax.axis_index("gx"), lax.axis_index("gy")
     inside = jnp.stack(
         [gx > 0, gx < lax.axis_size("gx") - 1, gy > 0, gy < lax.axis_size("gy") - 1]
     ).astype(jnp.int32)
     balanced = relax(
-        inside, merged, above, below, left, right, helmholtz_coef.reshape(chan, 1)
+        inside,
+        merged,
+        above,
+        below,
+        above_side,
+        below_side,
+        left,
+        right,
+        helmholtz_coef.reshape(chan, 1),
     )
     return balanced[None]
 

time: 192 us -> 235 us (1.22)
  Pallas kernels: 37.1 us -> 68.8 us
  starting transfers between devices: 28.1 us -> 49.5 us
  waiting for transfers between devices: 124 us -> 114 us
    pallas_call x1, Pallas kernels: 2.5 us -> 36.5 us  [pack_blocks(): pl.pallas_call(pack_kernel, out_shape=jax.ShapeDtypeStruct((tiles, slots)...]
    all_to_all x1, starting transfers between devices: 16.1 us -> 29.9 us  [local(): lax.all_to_all(outgoing, ('gx', 'gy'), split_axis=0, concat_axis=0, tiled...]
    ppermute x4 -> x6, starting transfers between devices: 11.8 us -> 19.4 us  [shifted(): return lax.ppermute(block, axis, route)]
    ppermute x4 -> x6, waiting for transfers between devices: 7.7 us -> 1.12 us  [shifted(): return lax.ppermute(block, axis, route)]
    all_to_all x1, waiting for transfers between devices: 115 us -> 111 us  [local(): lax.all_to_all(outgoing, ('gx', 'gy'), split_axis=0, concat_axis=0, tiled...]
  transfers between devices with their start and end apart: 6 -> 8, of which waited for: 6 -> 3; matrix products, arithmetic and copies ran while one was open for 0% -> 0% of each run, Pallas kernels for 2% -> 2%
where the time goes in v3:
time: 235 us; the launch traced here: 233 us
  waiting for transfers between devices  114 us (49%)
  Pallas kernels  68.8 us (29%)
  starting transfers between devices  49.5 us (21%)
    all_to_all x1, waiting for transfers between devices, local(): lax.all_to_all(outgoing, ('gx', 'gy'), split_axis=0, concat_axis=0, tiled...  111 us
    pallas_call x1, Pallas kernels, pack_blocks(): pl.pallas_call(pack_kernel, out_shape=jax.ShapeDtypeStruct((tiles, slots)...  36.5 us
    all_to_all x1, starting transfers between devices, local(): lax.all_to_all(outgoing, ('gx', 'gy'), split_axis=0, concat_axis=0, tiled...  29.9 us
    ppermute x6, starting transfers between devices, shifted(): return lax.ppermute(block, axis, route)  19.4 us
    pallas_call x1, Pallas kernels, relax(): pl.pallas_call(relax_kernel, out_shape=jax.ShapeDtypeStruct(merged.shape,...  14.1 us
    pallas_call x1, Pallas kernels, arrive(): pl.pallas_call(arrive_kernel, out_shape=(jax.ShapeDtypeStruct(coupled.sha...  8.59 us
    pallas_call x1, Pallas kernels, merge(): pl.pallas_call(merge_kernel, out_shape=(jax.ShapeDtypeStruct(arrival.shap...  5.16 us
  transfers between devices with their start and end apart: 8, of which 3 were waited for; matrix products, arithmetic and copies ran while one was open for 0% of the time, Pallas kernels for 2%

profile of v3, /device:TPU:2, one launch (start us, length us, event | category | flops | bytes accessed | tf_op | source)
XLA Modules:
  0.0 232.8 jit_solution(16426149554000105148)
XLA Ops:
  0.0 36.5 %pack_blocks.1 = f32[128,2,40,128]{3,2,1,0:T(8,128)} custom-call(s32[2,128]{1,0:T(2,128)} %bitcast.23, f32[64,40,128]{2,1,0:T(8,128)} %bitcast.16), custom_call_target="tpu_custom_call" | custom-call | tf_op jit(solution)/shard_map/pack_blocks/pallas_call | solution.py:62
  36.6 0.0 copy-start.6
  36.6 0.0 copy-start
  36.6 29.9 %all-to-all-start = ((f32[128,2,40,128]{3,2,1,0:T(8,128)}), f32[128,2,40,128]{3,2,1,0:T(8,128)}, u32[]{:S(2)}, u32[]{:S(2)}) async-start(f32[128,2,40,128]{3,2,1,0:T(8,128)} %pack_blocks.1), calls=%async_computation | async-start | bytes 10485760 | tf_op jit(solution)/shard_map/all_to_all | solution.py:364
  66.5 0.1 copy.10
  66.6 0.0 copy-start.2
  66.6 0.0 copy-start.3
  66.6 0.0 copy-start.5
  66.6 4.3 %couple.1.coupled = f32[64,40,128]{2,1,0:T(8,128)S(1)} custom-call(f32[64,40,128]{2,1,0:T(8,128)S(1)} %bitcast.17, f32[40,40]{1,0:T(8,128)S(1)} %bitcast.18), custom_call_target="tpu_custom_call" | custom-call | flops 157286400 | bytes 2621440 | tf_op jit(solution)/shard_map/couple/pallas_call | solution.py:84
  71.0 111.5 %all-to-all-done = f32[128,2,40,128]{3,2,1,0:T(8,128)} async-done(((f32[128,2,40,128]{3,2,1,0:T(8,128)}), f32[128,2,40,128]{3,2,1,0:T(8,128)}, u32[]{:S(2)}, u32[]{:S(2)}) %all-to-all-start) | async-done | bytes 5242912 | tf_op jit(solution)/shard_map/all_to_all | solution.py:364
  182.5 0.0 copy-start.4
  182.5 8.6 %arrive.1 = (f32[64,40,128]{2,1,0:T(8,128)S(1)}, f32[40,512]{1,0:T(8,128)S(1)}) custom-call(s32[1,64]{1,0:T(1,128)S(1)} %copy-done.5, s32[1,512]{1,0:T(1,128)S(1)} %bitcast.21, f32[256,40,128]{2,1,0:T(8,128)} %bitcast.9.slots, f32[64,40,128]{2,1,0:T(8,128)S(1)} %couple.1.coupled, s32[64,128]{1,0:T(8,128)S(1)} %bitcast.19, f32[64,128]{1,0:T(8,128)S(1)} %bitcast.20), custom_call_target="tpu_custom_call" | custom-call | tf_op jit(solution)/shard_map/arrive/pallas_call | solution.py:148
  191.1 0.0 copy-start.7
  191.1 0.1 collective-permute-start
  191.2 1.3 collective-permute-done.received
  192.5 5.2 %merge.1 = (f32[64,40,128]{2,1,0:T(8,128)S(1)}, f32[4,40,128]{2,1,0:T(8,128)S(1)}, f32[4,40,128]{2,1,0:T(8,128)S(1)}, f32[8,40,128]{2,1,0:T(8,128)S(1)}, f32[8,40,128]{2,1,0:T(8,128)S(1)}) custom-call(s32[1,512]{1,0:T(1,128)S(1)} %bitcast.22, f32[64,40,128]{2,1,0:T(8,128)S(1)} %get-tuple-element.14.arrival, f32[40,512]{1,0:T(8,128)S(1)} %collective-permute-done.received), custom_call_target="tpu_custom_call" | custom-call | tf_op jit(solution)/shard_map/merge/pallas_call | solution.py:198
  197.6 2.1 collective-permute-start.3
  199.7 1.3 collective-permute-start.4
  201.0 3.4 %collective-permute-start.1 = (f32[8,40,128]{2,1,0:T(8,128)S(1)}, f32[8,40,128]{2,1,0:T(8,128)S(1)}, u32[]{:S(2)}, u32[]{:S(2)}) collective-permute-start(f32[8,40,128]{2,1,0:T(8,128)S(1)} %get-tuple-element.17), channel_id=1, source_target_pairs={{0,4},{4,8},{8,12},{12,16},{16,20},{20,24},{24,28},{28,32},{32,36}... | collective-permute-start | bytes 491528 | tf_op jit(solution)/shard_map/ppermute | solution.py:347
  204.4 4.6 %collective-permute-start.2 = (f32[8,40,128]{2,1,0:T(8,128)S(1)}, f32[8,40,128]{2,1,0:T(8,128)S(1)}, u32[]{:S(2)}, u32[]{:S(2)}) collective-permute-start(f32[8,40,128]{2,1,0:T(8,128)S(1)} %get-tuple-element.18), channel_id=1, source_target_pairs={{4,0},{8,4},{12,8},{16,12},{20,16},{24,20},{28,24},{32,28},{36,32}... | collective-permute-start | bytes 491528 | tf_op jit(solution)/shard_map/ppermute | solution.py:347
  209.0 0.0 collective-permute-done.3.left
  209.0 0.0 collective-permute-done.4.right
  209.0 0.1 corners.1
  209.1 1.9 collective-permute-start.5
  211.0 6.2 %collective-permute-start.6 = (f32[40,128]{1,0:T(8,128)S(1)}, f32[40,128]{1,0:T(8,128)S(1)}, u32[]{:S(2)}, u32[]{:S(2)}) collective-permute-start(f32[40,128]{1,0:T(8,128)S(1)} %get-tuple-element.22), channel_id=1, source_target_pairs={{4,0},{8,4},{12,8},{16,12},{20,16},{24,20},{28,24},{32,28},{36,32}... | collective-permute-start | bytes 61448 | tf_op jit(solution)/shard_map/ppermute | solution.py:347
  217.2 0.1 add_convert_fusion.inside
  217.3 0.1 copy.11.coef
  217.4 0.0 collective-permute-done.5.above_side
  217.4 1.1 collective-permute-done.6.below_side
  218.5 0.0 collective-permute-done.1.above
  218.5 0.0 collective-permute-done.2.below
  218.5 14.1 %relax.1 = f32[64,40,128]{2,1,0:T(8,128)} custom-call(s32[4]{0:T(128)S(1)} %add_convert_fusion.inside, f32[64,40,128]{2,1,0:T(8,128)S(1)} %get-tuple-element.16.merged, f32[8,40,128]{2,1,0:T(8,128)S(1)} %collective-permute-done.1.above, f32[8,40,128]{2,1,0:T(8,128)S(1)} %collective-permute-done.2.below, f32[40,128]{1,0:T(8,128)S(1)} %collective-permute-done.5.above_side, ...), custom_call_target="tpu_custom_call" | custom-call | tf_op jit(solution)/shard_map/relax/pallas_call | solution.py:331
  (9 shorter events, 0.0 us)
Async XLA Ops:
  36.6 30.0 %copy-start.6 = (f32[40,40]{1,0:T(8,128)S(1)}, f32[40,40]{1,0:T(8,128)}, u32[]{:S(2)}) copy-start(f32[40,40]{1,0:T(8,128)} %param.17) | copy-start | bytes 19204
  36.6 30.0 %copy-start = (f32[1,64,40,128]{3,2,1,0:T(8,128)S(1)}, f32[1,64,40,128]{3,2,1,0:T(8,128)}, u32[]{:S(2)}) copy-start(f32[1,64,40,128]{3,2,1,0:T(8,128)} %param.9) | copy-start | bytes 3932164
  36.6 145.9 %all-to-all-start = ((f32[128,2,40,128]{3,2,1,0:T(8,128)}), f32[128,2,40,128]{3,2,1,0:T(8,128)}, u32[]{:S(2)}, u32[]{:S(2)}) async-start(f32[128,2,40,128]{3,2,1,0:T(8,128)} %pack_blocks.1), calls=%async_computation | async-start | bytes 10485760 | tf_op jit(solution)/shard_map/all_to_all | solution.py:364
  66.6 115.9 %copy-start.1 = (s32[1,64,128]{2,1,0:T(8,128)S(1)}, s32[1,64,128]{2,1,0:T(8,128)}, u32[]{:S(2)}) copy-start(s32[1,64,128]{2,1,0:T(8,128)} %param.11) | copy-start | bytes 98308
  66.6 115.9 %copy-start.2 = (f32[1,64,128]{2,1,0:T(8,128)S(1)}, f32[1,64,128]{2,1,0:T(8,128)}, u32[]{:S(2)}) copy-start(f32[1,64,128]{2,1,0:T(8,128)} %param.10) | copy-start | bytes 98308
  66.6 115.9 %copy-start.3 = (s32[1,1,512]{2,1,0:T(1,128)S(1)}, s32[1,1,512]{2,1,0:T(1,128)}, u32[]{:S(2)}) copy-start(s32[1,1,512]{2,1,0:T(1,128)} %param.14) | copy-start | bytes 6148
  66.6 115.8 %copy-start.5 = (s32[1,64]{1,0:T(1,128)S(1)}, s32[1,64]{1,0:T(1,128)}, u32[]{:S(2)}) copy-start(s32[1,64]{1,0:T(1,128)} %rows.1) | copy-start | bytes 772
  182.5 10.0 %copy-start.4 = (s32[1,1,512]{2,1,0:T(1,128)S(1)}, s32[1,1,512]{2,1,0:T(1,128)}, u32[]{:S(2)}) copy-start(s32[1,1,512]{2,1,0:T(1,128)} %param.15) | copy-start | bytes 6148
  191.1 26.2 %copy-start.7 = (f32[40]{0:T(128)S(1)}, f32[40]{0:T(128)}, u32[]{:S(2)}) copy-start(f32[40]{0:T(128)} %param.16) | copy-start | bytes 484
  191.1 1.4 collective-permute-start
  197.6 11.4 %collective-permute-start.3 = (f32[4,40,128]{2,1,0:T(8,128)S(1)}, f32[4,40,128]{2,1,0:T(8,128)S(1)}, u32[]{:S(2)}, u32[]{:S(2)}) collective-permute-start(f32[4,40,128]{2,1,0:T(8,128)S(1)} %get-tuple-element.19), channel_id=1, source_target_pairs={{0,1},{1,2},{2,3},{4,5},{5,6},{6,7},{8,9},{9,10},{10,11},{12,13},{... | collective-permute-start | bytes 245768 | tf_op jit(solution)/shard_map/ppermute | solution.py:347
  199.7 9.3 %collective-permute-start.4 = (f32[4,40,128]{2,1,0:T(8,128)S(1)}, f32[4,40,128]{2,1,0:T(8,128)S(1)}, u32[]{:S(2)}, u32[]{:S(2)}) collective-permute-start(f32[4,40,128]{2,1,0:T(8,128)S(1)} %get-tuple-element.20), channel_id=1, source_target_pairs={{1,0},{2,1},{3,2},{5,4},{6,5},{7,6},{9,8},{10,9},{11,10},{13,12},{... | collective-permute-start | bytes 245768 | tf_op jit(solution)/shard_map/ppermute | solution.py:347
  201.0 17.5 %collective-permute-start.1 = (f32[8,40,128]{2,1,0:T(8,128)S(1)}, f32[8,40,128]{2,1,0:T(8,128)S(1)}, u32[]{:S(2)}, u32[]{:S(2)}) collective-permute-start(f32[8,40,128]{2,1,0:T(8,128)S(1)} %get-tuple-element.17), channel_id=1, source_target_pairs={{0,4},{4,8},{8,12},{12,16},{16,20},{20,24},{24,28},{28,32},{32,36}... | collective-permute-start | bytes 491528 | tf_op jit(solution)/shard_map/ppermute | solution.py:347
  204.4 14.1 %collective-permute-start.2 = (f32[8,40,128]{2,1,0:T(8,128)S(1)}, f32[8,40,128]{2,1,0:T(8,128)S(1)}, u32[]{:S(2)}, u32[]{:S(2)}) collective-permute-start(f32[8,40,128]{2,1,0:T(8,128)S(1)} %get-tuple-element.18), channel_id=1, source_target_pairs={{4,0},{8,4},{12,8},{16,12},{20,16},{24,20},{28,24},{32,28},{36,32}... | collective-permute-start | bytes 491528 | tf_op jit(solution)/shard_map/ppermute | solution.py:347
  209.1 8.3 %collective-permute-start.5 = (f32[40,128]{1,0:T(8,128)S(1)}, f32[40,128]{1,0:T(8,128)S(1)}, u32[]{:S(2)}, u32[]{:S(2)}) collective-permute-start(f32[40,128]{1,0:T(8,128)S(1)} %get-tuple-element.21), channel_id=1, source_target_pairs={{0,4},{4,8},{8,12},{12,16},{16,20},{20,24},{24,28},{28,32},{32,36}... | collective-permute-start | bytes 61448 | tf_op jit(solution)/shard_map/ppermute | solution.py:347
  211.0 7.5 %collective-permute-start.6 = (f32[40,128]{1,0:T(8,128)S(1)}, f32[40,128]{1,0:T(8,128)S(1)}, u32[]{:S(2)}, u32[]{:S(2)}) collective-permute-start(f32[40,128]{1,0:T(8,128)S(1)} %get-tuple-element.22), channel_id=1, source_target_pairs={{4,0},{8,4},{12,8},{16,12},{20,16},{24,20},{28,24},{32,28},{36,32}... | collective-permute-start | bytes 61448 | tf_op jit(solution)/shard_map/ppermute | solution.py:347

commit v4 on v3

--- a/solution.py
+++ b/solution.py
@@ -10,10 +10,10 @@
 SWEEPS = 8
 WIDTH = 8
 PARTS = 4
+CHUNK = 16
 SUB = 8
 F32 = jnp.float32
 VMEM_LIMIT = 48 * 1024 * 1024
-PACK_LIMIT = 63 * 1024 * 1024
 
 
 def whole(space=pltpu.VMEM):
@@ -62,10 +62,10 @@
     return pl.pallas_call(
         pack_kernel,
         out_shape=jax.ShapeDtypeStruct((tiles, slots) + tile.shape[1:], F32),
-        in_specs=[whole(pltpu.HBM), whole(pltpu.HBM)],
+        in_specs=[whole(pltpu.HBM), whole()],
         out_specs=whole(pl.ANY),
         scratch_shapes=[pltpu.SMEM(wanted.shape, jnp.int32), pltpu.SemaphoreType.DMA],
-        compiler_params=pltpu.CompilerParams(vmem_limit_bytes=PACK_LIMIT),
+        compiler_params=params(),
         name="pack_blocks",
     )(wanted, tile)
 
@@ -159,7 +159,7 @@
     )(rows, strip, slots, coupled, cell, frac)
 
 
-def merge_kernel(strip, arrival, received, out, low, high, first, last):
+def merge_kernel(strip, arrival, received, out, low, high):
     count, chan, cells = out.shape
     out[...] = arrival[...]
     lane = lax.broadcasted_iota(jnp.int32, (chan, cells), 1)
@@ -175,8 +175,6 @@
             return carry
 
         lax.fori_loop(0, cells, put, 0, unroll=32)
-    first[...] = out[:WIDTH]
-    last[...] = out[count - WIDTH :]
     per = cells // WIDTH
     for g in range(count // per):
 
@@ -194,35 +192,38 @@
 def merge(strip, arrival, received):
     count, chan, cells = arrival.shape
     edge = jax.ShapeDtypeStruct((count * WIDTH // cells, chan, cells), F32)
-    rows = jax.ShapeDtypeStruct((WIDTH, chan, cells), F32)
     return pl.pallas_call(
         merge_kernel,
-        out_shape=(jax.ShapeDtypeStruct(arrival.shape, F32), edge, edge, rows, rows),
+        out_shape=(jax.ShapeDtypeStruct(arrival.shape, F32), edge, edge),
         in_specs=[whole(pltpu.SMEM), whole(), whole()],
-        out_specs=(whole(),) * 5,
+        out_specs=(whole(),) * 3,
         compiler_params=params(),
         name="merge",
     )(strip, arrival, received)
 
 
-def corners_kernel(left, right, first, last):
-    groups, chan, cells = left.shape
+def edge_rows_kernel(merged, left, right, first, last):
+    count, chan, cells = merged.shape
     lane = lax.broadcasted_iota(jnp.int32, (chan, cells), 1)
     half = cells // 2
-    first[...] = jnp.where(lane < half, right[0], pltpu.roll(left[0], half, 1))
-    last[...] = jnp.where(lane < half, pltpu.roll(right[groups - 1], half, 1), left[groups - 1])
-
-
-def corners(left, right):
-    held = jax.ShapeDtypeStruct(left.shape[1:], F32)
-    return pl.pallas_call(
-        corners_kernel,
-        out_shape=(held, held),
-        in_specs=[whole(), whole()],
+    groups = left.shape[0]
+    first[:WIDTH] = merged[:WIDTH]
+    first[WIDTH] = jnp.where(lane < half, right[0], pltpu.roll(left[0], half, 1))
+    last[:WIDTH] = merged[count - WIDTH :]
+    last[WIDTH] = jnp.where(lane < half, pltpu.roll(right[groups - 1], half, 1), left[groups - 1])
+
+
+def edge_rows(merged, left, right):
+    count, chan, cells = merged.shape
+    rows = jax.ShapeDtypeStruct((WIDTH + 1, chan, cells), F32)
+    return pl.pallas_call(
+        edge_rows_kernel,
+        out_shape=(rows, rows),
+        in_specs=[whole(), whole(), whole()],
         out_specs=(whole(), whole()),
         compiler_params=params(),
-        name="corners",
-    )(left, right)
+        name="edge_rows",
+    )(merged, left, right)
 
 
 def relax_kernel(
@@ -230,8 +231,6 @@
     merged,
     above,
     below,
-    above_side,
-    below_side,
     left,
     right,
     coef,
@@ -242,21 +241,25 @@
     b0,
     b1,
     start1,
+    start0,
     sem,
 ):
     count, chan, cells = merged.shape
     lane = lax.broadcasted_iota(jnp.int32, (chan, cells), 1)
-    is_right, is_left = lane < WIDTH, lane >= cells - WIDTH
+    is_right = lane < jnp.where(inside[3] > 0, WIDTH, 0)
+    is_left = lane >= jnp.where(inside[2] > 0, cells - WIDTH, cells)
     h = coef[...]
     inv = 1.0 / (1.0 + 4.0 * h)
     total = count + 2 * WIDTH
     per = cells // WIDTH
     half = cells // 2
 
-    for at, rows in ((0, above_side), (WIDTH + count, below_side)):
-        packed = rows[...]
+    for at, rows, flag in ((0, above, 0), (WIDTH, below, 1)):
+        kept = inside[flag] > 0
+        packed = jnp.where(kept, rows[WIDTH], 0.0)
         for i in range(WIDTH):
-            start1[at + i] = jnp.where(
+            start0[at + i] = jnp.where(kept, rows[i], 0.0)
+            start1[at // WIDTH * (count + WIDTH) + i] = jnp.where(
                 is_right,
                 pltpu.roll(packed, (-i * WIDTH) % cells, 1),
                 jnp.where(is_left, pltpu.roll(packed, (half - (i + 1) * WIDTH) % cells, 1), 0.0),
@@ -284,10 +287,14 @@
             jnp.where(is_first, l0, l1) + jnp.where(is_last, r0, r1),
         )
 
+    to = lax.broadcasted_iota(jnp.int32, (2 * cells, 2 * cells), 1)
+    gap = (to - lax.broadcasted_iota(jnp.int32, (2 * cells, 2 * cells), 0)) & (2 * cells - 1)
+    shift = jnp.where((gap == 1) | (gap == 2 * cells - 1), 1.0, 0.0).astype(jnp.bfloat16)
+
     def first_row(x, ch):
         if x < WIDTH:
-            return above[x, ch]
-        return merged[x - WIDTH, ch] if x < WIDTH + count else below[x - WIDTH - count, ch]
+            return start0[x, ch]
+        return merged[x - WIDTH, ch] if x < WIDTH + count else start0[x - count, ch]
 
     for c in range(0, chan, SUB):
         ch = slice(c, c + SUB)
@@ -304,20 +311,35 @@
                     return first_row(x, ch), start1[x, ch]
                 return now[0][x, ch], now[1][x, ch]
 
-            up, mid = held(begin - 1), held(begin)
-            for x in range(begin, end):
-                down = held(x + 1)
-                across = turn(*mid)
-                part = lo if x < WIDTH else hi if x >= WIDTH + count else None
-                g0 = gain if part is None else gain * part
-                new = first_row(x, ch) * inv8 + g0 * (up[0] + down[0] + across[0])
-                if s == SWEEPS - 1:
-                    out[x - WIDTH, ch] = new
-                else:
-                    later[0][x, ch] = new
-                    g1 = gain_side if part is None else gain_side * part
-                    later[1][x, ch] = start1[x, ch] * inv8 + g1 * (up[1] + down[1] + across[1])
-                up, mid = mid, down
+            size = end - begin
+            parts = []
+            for x0 in range(begin, end, CHUNK):
+                x1 = min(x0 + CHUNK, end)
+                both = [held(x) for x in range(x0, x1)]
+                block = jnp.concatenate(
+                    [jnp.concatenate([v[k] for v in both], axis=0) for k in (0, 1)], axis=1
+                )
+                coarse = block.astype(jnp.bfloat16)
+                fine = (block - coarse.astype(F32)).astype(jnp.bfloat16)
+                across = jnp.dot(coarse, shift, preferred_element_type=F32) + jnp.dot(
+                    fine, shift, preferred_element_type=F32
+                )
+                for x in range(x0, x1):
+                    at = (x - x0) * SUB
+                    part = lo if x < WIDTH else hi if x >= WIDTH + count else None
+                    g0 = gain if part is None else gain * part
+                    up, down = held(x - 1), held(x + 1)
+                    new = first_row(x, ch) * inv8 + g0 * (
+                        up[0] + down[0] + across[at : at + SUB, :cells]
+                    )
+                    if s == SWEEPS - 1:
+                        out[x - WIDTH, ch] = new
+                    else:
+                        later[0][x, ch] = new
+                        g1 = gain_side if part is None else gain_side * part
+                        later[1][x, ch] = start1[x, ch] * inv8 + g1 * (
+                            up[1] + down[1] + across[at : at + SUB, cells:]
+                        )
         pltpu.make_async_copy(out.at[:, ch], result.at[:, ch], sem.at[c // SUB]).start()
 
     for c in range(0, chan, SUB):
@@ -325,26 +347,26 @@
         pltpu.make_async_copy(out.at[:, ch], result.at[:, ch], sem.at[c // SUB]).wait()
 
 
-def relax(inside, merged, above, below, above_side, below_side, left, right, coef):
+def relax(inside, merged, above, below, left, right, coef):
     count, chan, cells = merged.shape
     held = pltpu.VMEM((count + 2 * WIDTH, chan, cells), F32)
     return pl.pallas_call(
         relax_kernel,
         out_shape=jax.ShapeDtypeStruct(merged.shape, F32),
-        in_specs=[whole(pltpu.SMEM)] + [whole()] * 8,
+        in_specs=[whole(pltpu.SMEM)] + [whole()] * 6,
         out_specs=whole(pl.ANY),
         scratch_shapes=[pltpu.VMEM(merged.shape, F32)]
         + [held] * 5
+        + [pltpu.VMEM((2 * WIDTH, chan, cells), F32)]
         + [pltpu.SemaphoreType.DMA((chan // SUB,))],
         compiler_params=params(),
         name="relax",
-    )(inside, merged, above, below, above_side, below_side, left, right, coef)
+    )(inside, merged, above, below, left, right, coef)
 
 
 def shifted(block, axis, step):
     count = lax.axis_size(axis)
-    route = [(i, i + step) for i in range(count) if 0 <= i + step < count]
-    return lax.ppermute(block, axis, route)
+    return lax.ppermute(block, axis, [(i, (i + step) % count) for i in range(count)])
 
 
 def local(
@@ -368,14 +390,12 @@
         row_source, strip_from[0], slots, coupled, depart_cell[0], depart_frac[0]
     )
     received = lax.ppermute(picked, "panel", [(0, 1), (1, 0)])
-    merged, low, high, first, last = merge(strip_into[0], arrival, received)
+    merged, low, high = merge(strip_into[0], arrival, received)
     right = shifted(low, "gy", -1)
     left = shifted(high, "gy", 1)
+    first, last = edge_rows(merged, left, right)
     below = shifted(first, "gx", -1)
     above = shifted(last, "gx", 1)
-    first_side, last_side = corners(left, right)
-    below_side = shifted(first_side, "gx", -1)
-    above_side = shifted(last_side, "gx", 1)
     gx, gy = lax.axis_index("gx"), lax.axis_index("gy")
     inside = jnp.stack(
         [gx > 0, gx < lax.axis_size("gx") - 1, gy > 0, gy < lax.axis_size("gy") - 1]
@@ -385,8 +405,6 @@
         merged,
         above,
         below,
-        above_side,
-        below_side,
         left,
         right,
         helmholtz_coef.reshape(chan, 1),

time: 235 us -> 180 us (0.77)
  Pallas kernels: 68.8 us -> 29.4 us
  starting transfers between devices: 49.5 us -> 23.9 us
  waiting for transfers between devices: 114 us -> 122 us
    pallas_call x1, Pallas kernels: 36.5 us -> 2.19 us  [pack_blocks(): pl.pallas_call(pack_kernel, out_shape=jax.ShapeDtypeStruct((tiles, slots)...]
    all_to_all x1, starting transfers between devices: 29.9 us -> 16.1 us  [local(): lax.all_to_all(outgoing, ('gx', 'gy'), split_axis=0, concat_axis=0, tiled...]
    ppermute x6 -> x4, starting transfers between devices: 19.4 us -> 7.68 us  [shifted(): lax.ppermute(block, axis, [(i, (i + step) % count) for i in range(count)])]
    ppermute x6 -> x4, waiting for transfers between devices: 1.12 us -> 6.16 us  [shifted(): lax.ppermute(block, axis, [(i, (i + step) % count) for i in range(count)])]
    pallas_call x1, Pallas kernels: 14.1 us -> 9.11 us  [relax(): pl.pallas_call(relax_kernel, out_shape=jax.ShapeDtypeStruct(merged.shape,...]
    all_to_all x1, waiting for transfers between devices: 111 us -> 115 us  [local(): lax.all_to_all(outgoing, ('gx', 'gy'), split_axis=0, concat_axis=0, tiled...]
  transfers between devices with their start and end apart: 8 -> 6, of which waited for: 3 -> 4; matrix products, arithmetic and copies ran while one was open for 0% -> 0% of each run, Pallas kernels for 2% -> 2%
where the time goes in v4:
time: 180 us; the launch traced here: 178 us
  waiting for transfers between devices  122 us (68%)
  Pallas kernels  29.4 us (16%)
  starting transfers between devices  23.9 us (13%)
  local copies, waits for them, and re-layouts  2.2 us (1%)
    all_to_all x1, waiting for transfers between devices, local(): lax.all_to_all(outgoing, ('gx', 'gy'), split_axis=0, concat_axis=0, tiled...  115 us
    all_to_all x1, starting transfers between devices, local(): lax.all_to_all(outgoing, ('gx', 'gy'), split_axis=0, concat_axis=0, tiled...  16.1 us
    pallas_call x1, Pallas kernels, relax(): pl.pallas_call(relax_kernel, out_shape=jax.ShapeDtypeStruct(merged.shape,...  9.11 us
    pallas_call x1, Pallas kernels, arrive(): pl.pallas_call(arrive_kernel, out_shape=(jax.ShapeDtypeStruct(coupled.sha...  8.58 us
    ppermute x4, starting transfers between devices, shifted(): lax.ppermute(block, axis, [(i, (i + step) % count) for i in range(count)])  7.68 us
    ppermute x4, waiting for transfers between devices, shifted(): lax.ppermute(block, axis, [(i, (i + step) % count) for i in range(count)])  6.16 us
    pallas_call x1, Pallas kernels, merge(): pl.pallas_call(merge_kernel, out_shape=(jax.ShapeDtypeStruct(arrival.shap...  5.16 us
    pallas_call x1, Pallas kernels, couple(): pl.pallas_call(couple_kernel, out_shape=jax.ShapeDtypeStruct(tile.shape,...  4.33 us
  transfers between devices with their start and end apart: 6, of which 4 were waited for; matrix products, arithmetic and copies ran while one was open for 0% of the time, Pallas kernels for 2%

profile of v4, /device:TPU:2, one launch (start us, length us, event | category | flops | bytes accessed | tf_op | source)
XLA Modules:
  0.0 178.0 jit_solution(8871719525279996967)
XLA Ops:
  0.0 1.3 copy-done
  1.3 0.7 copy-done.6
  2.0 2.2 %pack_blocks.1 = f32[128,2,40,128]{3,2,1,0:T(8,128)} custom-call(s32[2,128]{1,0:T(2,128)S(1)} %bitcast.23, f32[64,40,128]{2,1,0:T(8,128)S(1)} %bitcast.16), custom_call_target="tpu_custom_call" | custom-call | tf_op jit(solution)/shard_map/pack_blocks/pallas_call | solution.py:62
  4.2 0.0 copy-start.8
  4.2 0.0 copy-start.1
  4.2 16.1 %all-to-all-start = ((f32[128,2,40,128]{3,2,1,0:T(8,128)}), f32[128,2,40,128]{3,2,1,0:T(8,128)}, u32[]{:S(2)}, u32[]{:S(2)}) async-start(f32[128,2,40,128]{3,2,1,0:T(8,128)} %pack_blocks.1), calls=%async_computation | async-start | bytes 10485760 | tf_op jit(solution)/shard_map/all_to_all | solution.py:386
  20.3 0.0 copy-done.8
  20.3 0.1 copy.10
  20.4 0.0 copy-done.1
  20.4 0.0 copy-start.3
  20.4 0.0 copy-start.4
  20.4 0.0 copy-start.7
  20.4 4.3 %couple.1.coupled = f32[64,40,128]{2,1,0:T(8,128)S(1)} custom-call(f32[64,40,128]{2,1,0:T(8,128)S(1)} %bitcast.17, f32[40,40]{1,0:T(8,128)S(1)} %bitcast.18), custom_call_target="tpu_custom_call" | custom-call | flops 157286400 | bytes 2621440 | tf_op jit(solution)/shard_map/couple/pallas_call | solution.py:84
  24.8 114.7 %all-to-all-done = f32[128,2,40,128]{3,2,1,0:T(8,128)} async-done(((f32[128,2,40,128]{3,2,1,0:T(8,128)}), f32[128,2,40,128]{3,2,1,0:T(8,128)}, u32[]{:S(2)}, u32[]{:S(2)}) %all-to-all-start) | async-done | bytes 5242912 | tf_op jit(solution)/shard_map/all_to_all | solution.py:386
  139.5 0.0 copy-done.3
  139.5 0.0 copy-start.5
  139.5 8.6 %arrive.1 = (f32[64,40,128]{2,1,0:T(8,128)S(1)}, f32[40,512]{1,0:T(8,128)S(1)}) custom-call(s32[1,64]{1,0:T(1,128)S(1)} %copy-done.7, s32[1,512]{1,0:T(1,128)S(1)} %bitcast.21, f32[256,40,128]{2,1,0:T(8,128)} %bitcast.9.slots, f32[64,40,128]{2,1,0:T(8,128)S(1)} %couple.1.coupled, s32[64,128]{1,0:T(8,128)S(1)} %bitcast.19, f32[64,128]{1,0:T(8,128)S(1)} %bitcast.20), custom_call_target="tpu_custom_call" | custom-call | tf_op jit(solution)/shard_map/arrive/pallas_call | solution.py:148
  148.1 0.1 collective-permute-start
  148.2 1.3 collective-permute-done.received
  149.5 5.2 %merge.1 = (f32[64,40,128]{2,1,0:T(8,128)S(1)}, f32[4,40,128]{2,1,0:T(8,128)S(1)}, f32[4,40,128]{2,1,0:T(8,128)S(1)}) custom-call(s32[1,512]{1,0:T(1,128)S(1)} %bitcast.22, f32[64,40,128]{2,1,0:T(8,128)S(1)} %get-tuple-element.12.arrival, f32[40,512]{1,0:T(8,128)S(1)} %collective-permute-done.received), custom_call_target="tpu_custom_call" | custom-call | tf_op jit(solution)/shard_map/merge/pallas_call | solution.py:195
  154.7 0.6 collective-permute-start.1
  155.2 2.7 %collective-permute-start.2 = (f32[4,40,128]{2,1,0:T(8,128)S(1)}, f32[4,40,128]{2,1,0:T(8,128)S(1)}, u32[]{:S(2)}, u32[]{:S(2)}) collective-permute-start(f32[4,40,128]{2,1,0:T(8,128)S(1)} %get-tuple-element.16), channel_id=1, source_target_pairs={{0,3},{1,0},{2,1},{3,2},{4,7},{5,4},{6,5},{7,6},{8,11},{9,8},{10,9... | collective-permute-start | bytes 245768 | tf_op jit(solution)/shard_map/ppermute | solution.py:369
  158.0 2.5 %collective-permute-done.1.left = f32[4,40,128]{2,1,0:T(8,128)S(1)} collective-permute-done((f32[4,40,128]{2,1,0:T(8,128)S(1)}, f32[4,40,128]{2,1,0:T(8,128)S(1)}, u32[]{:S(2)}, u32[]{:S(2)}) %collective-permute-start.1) | collective-permute-done | bytes 81952 | tf_op jit(solution)/shard_map/ppermute | solution.py:369
  160.5 0.0 collective-permute-done.2.right
  160.5 0.1 edge_rows.1
  160.5 0.5 collective-permute-start.3
  161.0 3.9 %collective-permute-start.4 = (f32[9,40,128]{2,1,0:T(8,128)S(1)}, f32[9,40,128]{2,1,0:T(8,128)S(1)}, u32[]{:S(2)}, u32[]{:S(2)}) collective-permute-start(f32[9,40,128]{2,1,0:T(8,128)S(1)} %get-tuple-element.18), channel_id=1, source_target_pairs={{0,124},{4,0},{8,4},{12,8},{16,12},{20,16},{24,20},{28,24},{32,28}... | collective-permute-start | bytes 552968 | tf_op jit(solution)/shard_map/ppermute | solution.py:369
  164.9 0.1 copy.11.coef
  165.0 0.1 add_convert_fusion.inside
  165.1 3.7 %collective-permute-done.3.above = f32[9,40,128]{2,1,0:T(8,128)S(1)} collective-permute-done((f32[9,40,128]{2,1,0:T(8,128)S(1)}, f32[9,40,128]{2,1,0:T(8,128)S(1)}, u32[]{:S(2)}, u32[]{:S(2)}) %collective-permute-start.3) | collective-permute-done | bytes 184352 | tf_op jit(solution)/shard_map/ppermute | solution.py:369
  168.8 0.0 collective-permute-done.4.below
  168.8 9.1 %relax.1 = f32[64,40,128]{2,1,0:T(8,128)} custom-call(s32[4]{0:T(128)S(1)} %add_convert_fusion.inside, f32[64,40,128]{2,1,0:T(8,128)S(1)} %get-tuple-element.14.merged, f32[9,40,128]{2,1,0:T(8,128)S(1)} %collective-permute-done.3.above, f32[9,40,128]{2,1,0:T(8,128)S(1)} %collective-permute-done.4.below, f32[4,40,128]{2,1,0:T(8,128)S(1)} %collective-permute-done.1.left, ...), custom_call_target="tpu_custom_call" | custom-call | tf_op jit(solution)/shard_map/relax/pallas_call | solution.py:353
  (9 shorter events, 0.0 us)
Async XLA Ops:
  0.0 1.3 copy-start
  1.3 0.7 copy-start.6
  4.2 16.1 %copy-start.8 = (f32[40,40]{1,0:T(8,128)S(1)}, f32[40,40]{1,0:T(8,128)}, u32[]{:S(2)}) copy-start(f32[40,40]{1,0:T(8,128)} %param.17) | copy-start | bytes 19204
  4.2 16.2 %copy-start.1 = (f32[1,64,40,128]{3,2,1,0:T(8,128)S(1)}, f32[1,64,40,128]{3,2,1,0:T(8,128)}, u32[]{:S(2)}) copy-start(f32[1,64,40,128]{3,2,1,0:T(8,128)} %param.9) | copy-start | bytes 3932164
  4.2 135.3 %all-to-all-start = ((f32[128,2,40,128]{3,2,1,0:T(8,128)}), f32[128,2,40,128]{3,2,1,0:T(8,128)}, u32[]{:S(2)}, u32[]{:S(2)}) async-start(f32[128,2,40,128]{3,2,1,0:T(8,128)} %pack_blocks.1), calls=%async_computation | async-start | bytes 10485760 | tf_op jit(solution)/shard_map/all_to_all | solution.py:386
  20.4 119.1 %copy-start.2 = (s32[1,64,128]{2,1,0:T(8,128)S(1)}, s32[1,64,128]{2,1,0:T(8,128)}, u32[]{:S(2)}) copy-start(s32[1,64,128]{2,1,0:T(8,128)} %param.11) | copy-start | bytes 98308
  20.4 119.1 %copy-start.3 = (f32[1,64,128]{2,1,0:T(8,128)S(1)}, f32[1,64,128]{2,1,0:T(8,128)}, u32[]{:S(2)}) copy-start(f32[1,64,128]{2,1,0:T(8,128)} %param.10) | copy-start | bytes 98308
  20.4 119.1 %copy-start.4 = (s32[1,1,512]{2,1,0:T(1,128)S(1)}, s32[1,1,512]{2,1,0:T(1,128)}, u32[]{:S(2)}) copy-start(s32[1,1,512]{2,1,0:T(1,128)} %param.14) | copy-start | bytes 6148
  20.4 119.1 %copy-start.7 = (s32[1,64]{1,0:T(1,128)S(1)}, s32[1,64]{1,0:T(1,128)}, u32[]{:S(2)}) copy-start(s32[1,64]{1,0:T(1,128)} %rows.1) | copy-start | bytes 772
  139.5 10.0 %copy-start.5 = (s32[1,1,512]{2,1,0:T(1,128)S(1)}, s32[1,1,512]{2,1,0:T(1,128)}, u32[]{:S(2)}) copy-start(s32[1,1,512]{2,1,0:T(1,128)} %param.15) | copy-start | bytes 6148
  148.1 1.4 collective-permute-start
  149.5 15.4 %copy-start.9 = (f32[40]{0:T(128)S(1)}, f32[40]{0:T(128)}, u32[]{:S(2)}) copy-start(f32[40]{0:T(128)} %param.16) | copy-start | bytes 484
  154.7 5.8 %collective-permute-start.1 = (f32[4,40,128]{2,1,0:T(8,128)S(1)}, f32[4,40,128]{2,1,0:T(8,128)S(1)}, u32[]{:S(2)}, u32[]{:S(2)}) collective-permute-start(f32[4,40,128]{2,1,0:T(8,128)S(1)} %get-tuple-element.15), channel_id=1, source_target_pairs={{0,1},{1,2},{2,3},{3,0},{4,5},{5,6},{6,7},{7,4},{8,9},{9,10},{10,1... | collective-permute-start | bytes 245768 | tf_op jit(solution)/shard_map/ppermute | solution.py:369
  155.2 5.2 %collective-permute-start.2 = (f32[4,40,128]{2,1,0:T(8,128)S(1)}, f32[4,40,128]{2,1,0:T(8,128)S(1)}, u32[]{:S(2)}, u32[]{:S(2)}) collective-permute-start(f32[4,40,128]{2,1,0:T(8,128)S(1)} %get-tuple-element.16), channel_id=1, source_target_pairs={{0,3},{1,0},{2,1},{3,2},{4,7},{5,4},{6,5},{7,6},{8,11},{9,8},{10,9... | collective-permute-start | bytes 245768 | tf_op jit(solution)/shard_map/ppermute | solution.py:369
  160.5 8.2 %collective-permute-start.3 = (f32[9,40,128]{2,1,0:T(8,128)S(1)}, f32[9,40,128]{2,1,0:T(8,128)S(1)}, u32[]{:S(2)}, u32[]{:S(2)}) collective-permute-start(f32[9,40,128]{2,1,0:T(8,128)S(1)} %get-tuple-element.17), channel_id=1, source_target_pairs={{0,4},{4,8},{8,12},{12,16},{16,20},{20,24},{24,28},{28,32},{32,36}... | collective-permute-start | bytes 552968 | tf_op jit(solution)/shard_map/ppermute | solution.py:369
  161.0 7.7 %collective-permute-start.4 = (f32[9,40,128]{2,1,0:T(8,128)S(1)}, f32[9,40,128]{2,1,0:T(8,128)S(1)}, u32[]{:S(2)}, u32[]{:S(2)}) collective-permute-start(f32[9,40,128]{2,1,0:T(8,128)S(1)} %get-tuple-element.18), channel_id=1, source_target_pairs={{0,124},{4,0},{8,4},{12,8},{16,12},{20,16},{24,20},{28,24},{32,28}... | collective-permute-start | bytes 552968 | tf_op jit(solution)/shard_map/ppermute | solution.py:369

commit v5 on v4

--- a/solution.py
+++ b/solution.py
@@ -28,13 +28,31 @@
     return pl.CostEstimate(flops=flops, bytes_accessed=moved, transcendentals=0)
 
 
-def split(place, cells):
-    return lax.shift_right_logical(place, cells.bit_length() - 1), place & (cells - 1)
-
-
-def pack_kernel(listed, tile, out, wanted, sem):
+def terms(value):
+    first = value.astype(jnp.bfloat16)
+    rest = value - first.astype(F32)
+    second = rest.astype(jnp.bfloat16)
+    third = (rest - second.astype(F32)).astype(jnp.bfloat16)
+    return first, second, third
+
+
+def ones_where(mask):
+    return jnp.where(mask, 1.0, 0.0).astype(jnp.bfloat16)
+
+
+def pack_kernel(listed, tile, out, wanted, held, sem, list_sem, part_sem):
     slots, tiles = wanted.shape
-    pltpu.sync_copy(listed, wanted)
+    step = tile.shape[0] // PARTS
+    table = pltpu.make_async_copy(listed, wanted, list_sem)
+    table.start()
+    parts = []
+    for part in range(PARTS):
+        here = pl.ds(part * step, step)
+        parts.append(pltpu.make_async_copy(tile.at[here], held.at[here], part_sem.at[part]))
+        parts[-1].start()
+    table.wait()
+    for copy in parts:
+        copy.wait()
 
     def send(d, sent):
         for k in range(slots):
@@ -43,7 +61,7 @@
 
             @pl.when(filled)
             def _():
-                pltpu.make_async_copy(tile.at[block], out.at[d, k], sem).start()
+                pltpu.make_async_copy(held.at[block], out.at[d, k], sem).start()
 
             sent = sent + jnp.where(filled, 1, 0)
         return sent
@@ -51,7 +69,7 @@
     sent = lax.fori_loop(0, tiles, send, 0, unroll=4)
 
     def wait(_, carry):
-        pltpu.make_async_copy(tile.at[0], out.at[0, 0], sem).wait()
+        pltpu.make_async_copy(held.at[0], out.at[0, 0], sem).wait()
         return carry
 
     lax.fori_loop(0, sent, wait, 0)
@@ -62,10 +80,16 @@
     return pl.pallas_call(
         pack_kernel,
         out_shape=jax.ShapeDtypeStruct((tiles, slots) + tile.shape[1:], F32),
-        in_specs=[whole(pltpu.HBM), whole()],
+        in_specs=[whole(pl.ANY), whole(pl.ANY)],
         out_specs=whole(pl.ANY),
-        scratch_shapes=[pltpu.SMEM(wanted.shape, jnp.int32), pltpu.SemaphoreType.DMA],
-        compiler_params=params(),
+        scratch_shapes=[
+            pltpu.SMEM(wanted.shape, jnp.int32),
+            pltpu.VMEM(tile.shape, F32),
+            pltpu.SemaphoreType.DMA,
+            pltpu.SemaphoreType.DMA,
+            pltpu.SemaphoreType.DMA((PARTS,)),
+        ],
+        compiler_params=pltpu.CompilerParams(vmem_limit_bytes=60 * 1024 * 1024),
         name="pack_blocks",
     )(wanted, tile)
 
@@ -92,9 +116,8 @@
     )(tile, mix_t)
 
 
-def arrive_kernel(rows, strip, slots, coupled, cell, frac, out, picked, fetched, sem):
+def arrive_kernel(rows, strip, slots, coupled, cell, frac, out, picked, fetched, offset, sem):
     count, chan, cells = out.shape
-
     step = count // PARTS
 
     def fetch(r, carry, part):
@@ -105,10 +128,11 @@
         lax.fori_loop(
             part * step, (part + 1) * step, functools.partial(fetch, part=part), 0, unroll=True
         )
-
-    def row(r, carry):
-        t = frac[pl.ds(r, 1), :]
-        m = jnp.broadcast_to(cell[pl.ds(r, 1), :], (SUB, cells))
+    offset[...] = strip[...] - lax.broadcasted_iota(jnp.int32, offset.shape, 0)
+
+    def row(r):
+        t = frac[r : r + 1, :]
+        m = jnp.broadcast_to(cell[r : r + 1, :], (SUB, cells))
         weights = (
             -t * (t - 1.0) * (t - 2.0) / 6.0,
             (t + 1.0) * (t - 1.0) * (t - 2.0) / 2.0,
@@ -124,24 +148,20 @@
                     block, m + tap, axis=1, mode="promise_in_bounds"
                 )
             out[r, c : c + SUB, :] = total
-        return carry
-
+
+    total = jnp.zeros((3 * chan, picked.shape[1]), F32)
     for part in range(PARTS):
         here = pl.ds(part * step, step)
         pltpu.make_async_copy(slots.at[here], fetched.at[here], sem.at[part]).wait()
-        lax.fori_loop(part * step, (part + 1) * step, row, 0, unroll=True)
-
-    lane = lax.broadcasted_iota(jnp.int32, (chan, cells), 1)
-    for part in range(picked.shape[1] // cells):
-
-        def pick(j, held):
-            place = strip[0, part * cells + j]
-            row, at = split(place, cells)
-            moved = pltpu.roll(out[row], (j - at) & (cells - 1), 1)
-            return jnp.where(lane == j, moved, held)
-
-        held = lax.fori_loop(0, cells, pick, jnp.zeros((chan, cells), F32), unroll=True)
-        picked[:, part * cells : (part + 1) * cells] = held
+        for r in range(part * step, (part + 1) * step, 2):
+            row(r)
+            row(r + 1)
+            pair = jnp.concatenate([out[r], out[r + 1]], axis=1)
+            wanted = ones_where(offset[...] == r * cells)
+            total = total + jnp.dot(
+                jnp.concatenate(terms(pair), axis=0), wanted, preferred_element_type=F32
+            )
+    picked[...] = total[:chan] + total[chan : 2 * chan] + total[2 * chan :]
 
 
 def arrive(rows, strip, slots, coupled, cell, frac):
@@ -151,30 +171,35 @@
             jax.ShapeDtypeStruct(coupled.shape, F32),
             jax.ShapeDtypeStruct((coupled.shape[1], strip.shape[1]), F32),
         ),
-        in_specs=[whole(pltpu.SMEM), whole(pltpu.SMEM), whole(pl.ANY), whole(), whole(), whole()],
+        in_specs=[whole(pltpu.SMEM), whole(), whole(pl.ANY), whole(), whole(), whole()],
         out_specs=(whole(), whole()),
-        scratch_shapes=[pltpu.VMEM(coupled.shape, F32), pltpu.SemaphoreType.DMA((PARTS,))],
+        scratch_shapes=[
+            pltpu.VMEM(coupled.shape, F32),
+            pltpu.VMEM((2 * coupled.shape[2], strip.shape[1]), jnp.int32),
+            pltpu.SemaphoreType.DMA((PARTS,)),
+        ],
         compiler_params=params(),
         name="arrive",
     )(rows, strip, slots, coupled, cell, frac)
 
 
-def merge_kernel(strip, arrival, received, out, low, high):
+def merge_kernel(strip, arrival, received, out, low, high, offset):
     count, chan, cells = out.shape
-    out[...] = arrival[...]
+    offset[...] = strip[...] - lax.broadcasted_iota(jnp.int32, offset.shape, 1)
+    size = received.shape[1]
+    values = jnp.concatenate(
+        [*terms(received[...]), jnp.ones((SUB, size), jnp.bfloat16)], axis=0
+    )
+    for r in range(0, count, 2):
+        placed = jnp.dot(
+            values, ones_where(offset[...] == r * cells), preferred_element_type=F32
+        )
+        value = placed[:chan] + placed[chan : 2 * chan] + placed[2 * chan : 3 * chan]
+        hit = jnp.broadcast_to(placed[3 * chan : 3 * chan + 1], value.shape) > 0.5
+        for k in range(2):
+            at = slice(k * cells, (k + 1) * cells)
+            out[r + k] = jnp.where(hit[:, at], value[:, at], arrival[r + k])
     lane = lax.broadcasted_iota(jnp.int32, (chan, cells), 1)
-    for part in range(received.shape[1] // cells):
-
-        def put(j, carry):
-            place = strip[0, part * cells + j]
-            row, at = split(place, cells)
-            moved = pltpu.roll(
-                received[:, part * cells : (part + 1) * cells], (at - j) & (cells - 1), 1
-            )
-            pltpu.store(out.at[row], moved, mask=lane == at)
-            return carry
-
-        lax.fori_loop(0, cells, put, 0, unroll=32)
     per = cells // WIDTH
     for g in range(count // per):
 
@@ -195,8 +220,9 @@
     return pl.pallas_call(
         merge_kernel,
         out_shape=(jax.ShapeDtypeStruct(arrival.shape, F32), edge, edge),
-        in_specs=[whole(pltpu.SMEM), whole(), whole()],
+        in_specs=[whole(), whole(), whole()],
         out_specs=(whole(),) * 3,
+        scratch_shapes=[pltpu.VMEM((strip.shape[0], 2 * cells), jnp.int32)],
         compiler_params=params(),
         name="merge",
     )(strip, arrival, received)
@@ -242,6 +268,8 @@
     b1,
     start1,
     start0,
+    scaled0,
+    scaled1,
     sem,
 ):
     count, chan, cells = merged.shape
@@ -273,19 +301,10 @@
         )
 
     lane8 = lax.broadcasted_iota(jnp.int32, (SUB, cells), 1)
-    is_first, is_last = lane8 == 0, lane8 == cells - 1
     side = jnp.where(
         lane8 < WIDTH, inside[3], jnp.where(lane8 >= cells - WIDTH, inside[2], 0)
     ).astype(F32)
     lo, hi = inside[0].astype(F32), inside[1].astype(F32)
-
-    def turn(row, beside):
-        l0, l1 = pltpu.roll(row, 1, 1), pltpu.roll(beside, 1, 1)
-        r0, r1 = pltpu.roll(row, cells - 1, 1), pltpu.roll(beside, cells - 1, 1)
-        return (
-            jnp.where(is_first, l1, l0) + jnp.where(is_last, r1, r0),
-            jnp.where(is_first, l0, l1) + jnp.where(is_last, r0, r1),
-        )
 
     to = lax.broadcasted_iota(jnp.int32, (2 * cells, 2 * cells), 1)
     gap = (to - lax.broadcasted_iota(jnp.int32, (2 * cells, 2 * cells), 0)) & (2 * cells - 1)
@@ -302,6 +321,10 @@
         gain = jnp.broadcast_to(h[ch] * inv[ch], (SUB, cells))
         gain_side = gain * side
 
+        for x in range(total):
+            scaled0[x, ch] = first_row(x, ch) * inv8
+            scaled1[x, ch] = start1[x, ch] * inv8
+
         for s in range(SWEEPS):
             now, later = ((a0, a1), (b0, b1))[:: 1 if s % 2 else -1]
             begin, end = s + 1, total - s - 1
@@ -311,11 +334,22 @@
                     return first_row(x, ch), start1[x, ch]
                 return now[0][x, ch], now[1][x, ch]
 
-            size = end - begin
-            parts = []
-            for x0 in range(begin, end, CHUNK):
-                x1 = min(x0 + CHUNK, end)
-                both = [held(x) for x in range(x0, x1)]
+            def store(x, across):
+                part = lo if x < WIDTH else hi if x >= WIDTH + count else None
+                up, down = held(x - 1), held(x + 1)
+                g0 = gain if part is None else gain * part
+                new = scaled0[x, ch] + g0 * (up[0] + down[0] + across[0])
+                if s == SWEEPS - 1:
+                    out[x - WIDTH, ch] = new
+                else:
+                    later[0][x, ch] = new
+                    g1 = gain_side if part is None else gain_side * part
+                    later[1][x, ch] = scaled1[x, ch] + g1 * (up[1] + down[1] + across[1])
+
+            x = begin
+            while x < end:
+                x1 = min(x + CHUNK, end)
+                both = [held(y) for y in range(x, x1)]
                 block = jnp.concatenate(
                     [jnp.concatenate([v[k] for v in both], axis=0) for k in (0, 1)], axis=1
                 )
@@ -324,22 +358,10 @@
                 across = jnp.dot(coarse, shift, preferred_element_type=F32) + jnp.dot(
                     fine, shift, preferred_element_type=F32
                 )
-                for x in range(x0, x1):
-                    at = (x - x0) * SUB
-                    part = lo if x < WIDTH else hi if x >= WIDTH + count else None
-                    g0 = gain if part is None else gain * part
-                    up, down = held(x - 1), held(x + 1)
-                    new = first_row(x, ch) * inv8 + g0 * (
-                        up[0] + down[0] + across[at : at + SUB, :cells]
-                    )
-                    if s == SWEEPS - 1:
-                        out[x - WIDTH, ch] = new
-                    else:
-                        later[0][x, ch] = new
-                        g1 = gain_side if part is None else gain_side * part
-                        later[1][x, ch] = start1[x, ch] * inv8 + g1 * (
-                            up[1] + down[1] + across[at : at + SUB, cells:]
-                        )
+                for y in range(x, x1):
+                    at = slice((y - x) * SUB, (y - x + 1) * SUB)
+                    store(y, (across[at, :cells], across[at, cells:]))
+                x = x1
         pltpu.make_async_copy(out.at[:, ch], result.at[:, ch], sem.at[c // SUB]).start()
 
     for c in range(0, chan, SUB):
@@ -358,6 +380,7 @@
         scratch_shapes=[pltpu.VMEM(merged.shape, F32)]
         + [held] * 5
         + [pltpu.VMEM((2 * WIDTH, chan, cells), F32)]
+        + [held] * 2
         + [pltpu.SemaphoreType.DMA((chan // SUB,))],
         compiler_params=params(),
         name="relax",
@@ -390,7 +413,7 @@
         row_source, strip_from[0], slots, coupled, depart_cell[0], depart_frac[0]
     )
     received = lax.ppermute(picked, "panel", [(0, 1), (1, 0)])
-    merged, low, high = merge(strip_into[0], arrival, received)
+    merged, low, high = merge(strip_into[0].T, arrival, received)
     right = shifted(low, "gy", -1)
     left = shifted(high, "gy", 1)
     first, last = edge_rows(merged, left, right)

time: 180 us -> 174 us (0.967)
  Pallas kernels: 29.4 us -> 23.7 us
    pallas_call x1, Pallas kernels: 5.16 us -> 1.67 us  [merge(): pl.pallas_call(merge_kernel, out_shape=(jax.ShapeDtypeStruct(arrival.shap...]
    pallas_call x1, Pallas kernels: 8.58 us -> 6.06 us  [arrive(): pl.pallas_call(arrive_kernel, out_shape=(jax.ShapeDtypeStruct(coupled.sha...]
  transfers between devices with their start and end apart: 6 -> 6, of which waited for: 4 -> 4; matrix products, arithmetic and copies ran while one was open for 0% -> 0% of each run, Pallas kernels for 2% -> 3%
where the time goes in v5:
time: 174 us; the launch traced here: 172 us
  waiting for transfers between devices  122 us (70%)
  Pallas kernels  23.7 us (14%)
  starting transfers between devices  23.7 us (14%)
  local copies, waits for them, and re-layouts  2.72 us (2%)
    all_to_all x1, waiting for transfers between devices, local(): lax.all_to_all(outgoing, ('gx', 'gy'), split_axis=0, concat_axis=0, tiled...  114 us
    all_to_all x1, starting transfers between devices, local(): lax.all_to_all(outgoing, ('gx', 'gy'), split_axis=0, concat_axis=0, tiled...  16.2 us
    pallas_call x1, Pallas kernels, relax(): pl.pallas_call(relax_kernel, out_shape=jax.ShapeDtypeStruct(merged.shape,...  8.95 us
    ppermute x4, starting transfers between devices, shifted(): lax.ppermute(block, axis, [(i, (i + step) % count) for i in range(count)])  7.5 us
    ppermute x4, waiting for transfers between devices, shifted(): lax.ppermute(block, axis, [(i, (i + step) % count) for i in range(count)])  6.14 us
    pallas_call x1, Pallas kernels, arrive(): pl.pallas_call(arrive_kernel, out_shape=(jax.ShapeDtypeStruct(coupled.sha...  6.06 us
    pallas_call x1, Pallas kernels, couple(): pl.pallas_call(couple_kernel, out_shape=jax.ShapeDtypeStruct(tile.shape,...  4.33 us
  transfers between devices with their start and end apart: 6, of which 4 were waited for; matrix products, arithmetic and copies ran while one was open for 0% of the time, Pallas kernels for 3%

profile of v5, /device:TPU:2, one launch (start us, length us, event | category | flops | bytes accessed | tf_op | source)
XLA Modules:
  0.0 172.1 jit_solution(9811421309333266903)
XLA Ops:
  0.0 2.6 %pack_blocks.1 = f32[128,2,40,128]{3,2,1,0:T(8,128)} custom-call(s32[2,128]{1,0:T(2,128)} %bitcast.23, f32[64,40,128]{2,1,0:T(8,128)} %bitcast.16), custom_call_target="tpu_custom_call" | custom-call | tf_op jit(solution)/shard_map/pack_blocks/pallas_call | solution.py:80
  2.6 0.0 copy-start.7
  2.6 0.0 copy-start
  2.6 16.2 %all-to-all-start = ((f32[128,2,40,128]{3,2,1,0:T(8,128)}), f32[128,2,40,128]{3,2,1,0:T(8,128)}, u32[]{:S(2)}, u32[]{:S(2)}) async-start(f32[128,2,40,128]{3,2,1,0:T(8,128)} %pack_blocks.1), calls=%async_computation | async-start | bytes 10485760 | tf_op jit(solution)/shard_map/all_to_all | solution.py:409
  18.9 0.0 copy-done.7
  18.9 0.1 copy.12
  19.0 0.0 copy-start.4
  19.0 0.0 copy-start.5
  19.0 0.0 copy-start.6
  19.0 4.3 %couple.1.coupled = f32[64,40,128]{2,1,0:T(8,128)S(1)} custom-call(f32[64,40,128]{2,1,0:T(8,128)S(1)} %bitcast.17, f32[40,40]{1,0:T(8,128)S(1)} %bitcast.18), custom_call_target="tpu_custom_call" | custom-call | flops 157286400 | bytes 2621440 | tf_op jit(solution)/shard_map/couple/pallas_call | solution.py:108
  23.3 114.3 %all-to-all-done = f32[128,2,40,128]{3,2,1,0:T(8,128)} async-done(((f32[128,2,40,128]{3,2,1,0:T(8,128)}), f32[128,2,40,128]{3,2,1,0:T(8,128)}, u32[]{:S(2)}, u32[]{:S(2)}) %all-to-all-start) | async-done | bytes 5242912 | tf_op jit(solution)/shard_map/all_to_all | solution.py:409
  137.7 0.0 copy-start.8
  137.7 6.1 %arrive.1 = (f32[64,40,128]{2,1,0:T(8,128)S(1)}, f32[40,512]{1,0:T(8,128)S(1)}) custom-call(s32[1,64]{1,0:T(1,128)S(1)} %copy-done.6, s32[1,512]{1,0:T(1,128)S(1)} %bitcast.21, f32[256,40,128]{2,1,0:T(8,128)} %bitcast.9.slots, f32[64,40,128]{2,1,0:T(8,128)S(1)} %couple.1.coupled, s32[64,128]{1,0:T(8,128)S(1)} %bitcast.19, f32[64,128]{1,0:T(8,128)S(1)} %bitcast.20), custom_call_target="tpu_custom_call" | custom-call | tf_op jit(solution)/shard_map/arrive/pallas_call | solution.py:168
  143.8 0.0 copy-start.1
  143.8 1.0 copy-done.1
  144.8 0.0 collective-permute-start
  144.8 0.1 copy.13.strip
  145.0 1.1 collective-permute-done.received
  146.1 1.3 copy-done.2
  147.4 1.7 merge.1
  149.1 0.7 collective-permute-start.1
  149.8 2.7 %collective-permute-start.2 = (f32[4,40,128]{2,1,0:T(8,128)S(1)}, f32[4,40,128]{2,1,0:T(8,128)S(1)}, u32[]{:S(2)}, u32[]{:S(2)}) collective-permute-start(f32[4,40,128]{2,1,0:T(8,128)S(1)} %get-tuple-element.16), channel_id=1, source_target_pairs={{0,3},{1,0},{2,1},{3,2},{4,7},{5,4},{6,5},{7,6},{8,11},{9,8},{10,9... | collective-permute-start | bytes 245768 | tf_op jit(solution)/shard_map/ppermute | solution.py:392
  152.4 2.5 %collective-permute-done.1.left = f32[4,40,128]{2,1,0:T(8,128)S(1)} collective-permute-done((f32[4,40,128]{2,1,0:T(8,128)S(1)}, f32[4,40,128]{2,1,0:T(8,128)S(1)}, u32[]{:S(2)}, u32[]{:S(2)}) %collective-permute-start.1) | collective-permute-done | bytes 81952 | tf_op jit(solution)/shard_map/ppermute | solution.py:392
  154.9 0.0 collective-permute-done.2.right
  154.9 0.1 edge_rows.1
  155.0 0.6 collective-permute-start.3
  155.5 3.6 %collective-permute-start.4 = (f32[9,40,128]{2,1,0:T(8,128)S(1)}, f32[9,40,128]{2,1,0:T(8,128)S(1)}, u32[]{:S(2)}, u32[]{:S(2)}) collective-permute-start(f32[9,40,128]{2,1,0:T(8,128)S(1)} %get-tuple-element.18), channel_id=1, source_target_pairs={{0,124},{4,0},{8,4},{12,8},{16,12},{20,16},{24,20},{28,24},{32,28}... | collective-permute-start | bytes 552968 | tf_op jit(solution)/shard_map/ppermute | solution.py:392
  159.2 0.1 copy.14.coef
  159.3 0.1 add_convert_fusion.inside
  159.3 3.7 %collective-permute-done.3.above = f32[9,40,128]{2,1,0:T(8,128)S(1)} collective-permute-done((f32[9,40,128]{2,1,0:T(8,128)S(1)}, f32[9,40,128]{2,1,0:T(8,128)S(1)}, u32[]{:S(2)}, u32[]{:S(2)}) %collective-permute-start.3) | collective-permute-done | bytes 184352 | tf_op jit(solution)/shard_map/ppermute | solution.py:392
  163.0 0.0 collective-permute-done.4.below
  163.0 9.0 %relax.1 = f32[64,40,128]{2,1,0:T(8,128)} custom-call(s32[4]{0:T(128)S(1)} %add_convert_fusion.inside, f32[64,40,128]{2,1,0:T(8,128)S(1)} %get-tuple-element.14.merged, f32[9,40,128]{2,1,0:T(8,128)S(1)} %collective-permute-done.3.above, f32[9,40,128]{2,1,0:T(8,128)S(1)} %collective-permute-done.4.below, f32[4,40,128]{2,1,0:T(8,128)S(1)} %collective-permute-done.1.left, ...), custom_call_target="tpu_custom_call" | custom-call | tf_op jit(solution)/shard_map/relax/pallas_call | solution.py:375
  (10 shorter events, 0.0 us)
Async XLA Ops:
  2.6 16.3 %copy-start.7 = (f32[40,40]{1,0:T(8,128)S(1)}, f32[40,40]{1,0:T(8,128)}, u32[]{:S(2)}) copy-start(f32[40,40]{1,0:T(8,128)} %param.17) | copy-start | bytes 19204
  2.6 16.3 %copy-start = (f32[1,64,40,128]{3,2,1,0:T(8,128)S(1)}, f32[1,64,40,128]{3,2,1,0:T(8,128)}, u32[]{:S(2)}) copy-start(f32[1,64,40,128]{3,2,1,0:T(8,128)} %param.9) | copy-start | bytes 3932164
  2.6 135.0 %all-to-all-start = ((f32[128,2,40,128]{3,2,1,0:T(8,128)}), f32[128,2,40,128]{3,2,1,0:T(8,128)}, u32[]{:S(2)}, u32[]{:S(2)}) async-start(f32[128,2,40,128]{3,2,1,0:T(8,128)} %pack_blocks.1), calls=%async_computation | async-start | bytes 10485760 | tf_op jit(solution)/shard_map/all_to_all | solution.py:409
  19.0 118.7 %copy-start.3 = (s32[1,64,128]{2,1,0:T(8,128)S(1)}, s32[1,64,128]{2,1,0:T(8,128)}, u32[]{:S(2)}) copy-start(s32[1,64,128]{2,1,0:T(8,128)} %param.11) | copy-start | bytes 98308
  19.0 118.7 %copy-start.4 = (f32[1,64,128]{2,1,0:T(8,128)S(1)}, f32[1,64,128]{2,1,0:T(8,128)}, u32[]{:S(2)}) copy-start(f32[1,64,128]{2,1,0:T(8,128)} %param.10) | copy-start | bytes 98308
  19.0 118.7 %copy-start.5 = (s32[1,1,512]{2,1,0:T(1,128)S(1)}, s32[1,1,512]{2,1,0:T(1,128)}, u32[]{:S(2)}) copy-start(s32[1,1,512]{2,1,0:T(1,128)} %param.14) | copy-start | bytes 6148
  19.0 118.7 %copy-start.6 = (s32[1,64]{1,0:T(1,128)S(1)}, s32[1,64]{1,0:T(1,128)}, u32[]{:S(2)}) copy-start(s32[1,64]{1,0:T(1,128)} %rows.1) | copy-start | bytes 772
  137.7 7.1 %copy-start.8 = (s32[1,1,512]{2,1,0:T(1,128)S(1)}, s32[1,1,512]{2,1,0:T(1,128)}, u32[]{:S(2)}) copy-start(s32[1,1,512]{2,1,0:T(1,128)} %param.15) | copy-start | bytes 6148
  143.8 1.1 copy-start.1
  144.8 1.3 collective-permute-start
  146.1 1.3 copy-start.2
  147.4 11.7 %copy-start.9 = (f32[40]{0:T(128)S(1)}, f32[40]{0:T(128)}, u32[]{:S(2)}) copy-start(f32[40]{0:T(128)} %param.16) | copy-start | bytes 484
  149.1 5.8 %collective-permute-start.1 = (f32[4,40,128]{2,1,0:T(8,128)S(1)}, f32[4,40,128]{2,1,0:T(8,128)S(1)}, u32[]{:S(2)}, u32[]{:S(2)}) collective-permute-start(f32[4,40,128]{2,1,0:T(8,128)S(1)} %get-tuple-element.15), channel_id=1, source_target_pairs={{0,1},{1,2},{2,3},{3,0},{4,5},{5,6},{6,7},{7,4},{8,9},{9,10},{10,1... | collective-permute-start | bytes 245768 | tf_op jit(solution)/shard_map/ppermute | solution.py:392
  149.8 5.1 %collective-permute-start.2 = (f32[4,40,128]{2,1,0:T(8,128)S(1)}, f32[4,40,128]{2,1,0:T(8,128)S(1)}, u32[]{:S(2)}, u32[]{:S(2)}) collective-permute-start(f32[4,40,128]{2,1,0:T(8,128)S(1)} %get-tuple-element.16), channel_id=1, source_target_pairs={{0,3},{1,0},{2,1},{3,2},{4,7},{5,4},{6,5},{7,6},{8,11},{9,8},{10,9... | collective-permute-start | bytes 245768 | tf_op jit(solution)/shard_map/ppermute | solution.py:392
  155.0 8.0 %collective-permute-start.3 = (f32[9,40,128]{2,1,0:T(8,128)S(1)}, f32[9,40,128]{2,1,0:T(8,128)S(1)}, u32[]{:S(2)}, u32[]{:S(2)}) collective-permute-start(f32[9,40,128]{2,1,0:T(8,128)S(1)} %get-tuple-element.17), channel_id=1, source_target_pairs={{0,4},{4,8},{8,12},{12,16},{16,20},{20,24},{24,28},{28,32},{32,36}... | collective-permute-start | bytes 552968 | tf_op jit(solution)/shard_map/ppermute | solution.py:392
  155.5 7.5 %collective-permute-start.4 = (f32[9,40,128]{2,1,0:T(8,128)S(1)}, f32[9,40,128]{2,1,0:T(8,128)S(1)}, u32[]{:S(2)}, u32[]{:S(2)}) collective-permute-start(f32[9,40,128]{2,1,0:T(8,128)S(1)} %get-tuple-element.18), channel_id=1, source_target_pairs={{0,124},{4,0},{8,4},{12,8},{16,12},{20,16},{24,20},{28,24},{32,28}... | collective-permute-start | bytes 552968 | tf_op jit(solution)/shard_map/ppermute | solution.py:392

commit v6 on v5

--- a/solution.py
+++ b/solution.py
@@ -13,15 +13,15 @@
 CHUNK = 16
 SUB = 8
 F32 = jnp.float32
-VMEM_LIMIT = 48 * 1024 * 1024
+MIB = 1024 * 1024
 
 
 def whole(space=pltpu.VMEM):
     return pl.BlockSpec(memory_space=space)
 
 
-def params():
-    return pltpu.CompilerParams(vmem_limit_bytes=VMEM_LIMIT)
+def params(mib):
+    return pltpu.CompilerParams(vmem_limit_bytes=mib * MIB)
 
 
 def cost(flops, moved):
@@ -89,12 +89,12 @@
             pltpu.SemaphoreType.DMA,
             pltpu.SemaphoreType.DMA((PARTS,)),
         ],
-        compiler_params=pltpu.CompilerParams(vmem_limit_bytes=60 * 1024 * 1024),
+        compiler_params=params(60),
         name="pack_blocks",
     )(wanted, tile)
 
 
-def couple_kernel(tile, mix_t, out):
+def prepare_kernel(tile, mix_t, strip, out, columns):
     mix = mix_t[...] * 0.5
 
     def row(r, carry):
@@ -102,18 +102,23 @@
         return carry
 
     lax.fori_loop(0, tile.shape[0], row, 0, unroll=4)
-
-
-def couple(tile, mix_t):
-    return pl.pallas_call(
-        couple_kernel,
-        out_shape=jax.ShapeDtypeStruct(tile.shape, F32),
-        in_specs=[whole(), whole()],
-        out_specs=whole(),
-        compiler_params=params(),
+    size, cells = columns.shape
+    columns[...] = jnp.broadcast_to(strip[...], (cells, size)).T
+
+
+def prepare(tile, mix_t, strip):
+    return pl.pallas_call(
+        prepare_kernel,
+        out_shape=(
+            jax.ShapeDtypeStruct(tile.shape, F32),
+            jax.ShapeDtypeStruct((strip.shape[1], tile.shape[2]), jnp.int32),
+        ),
+        in_specs=[whole()] * 3,
+        out_specs=(whole(), whole()),
+        compiler_params=params(16),
         cost_estimate=cost(2 * tile.size * tile.shape[1] * 6, 8 * tile.size),
-        name="couple",
-    )(tile, mix_t)
+        name="prepare",
+    )(tile, mix_t, strip)
 
 
 def arrive_kernel(rows, strip, slots, coupled, cell, frac, out, picked, fetched, offset, sem):
@@ -178,14 +183,18 @@
             pltpu.VMEM((2 * coupled.shape[2], strip.shape[1]), jnp.int32),
             pltpu.SemaphoreType.DMA((PARTS,)),
         ],
-        compiler_params=params(),
+        compiler_params=params(48),
         name="arrive",
     )(rows, strip, slots, coupled, cell, frac)
 
 
-def merge_kernel(strip, arrival, received, out, low, high, offset):
+def merge_kernel(columns, arrival, received, out, low, high, offset):
     count, chan, cells = out.shape
-    offset[...] = strip[...] - lax.broadcasted_iota(jnp.int32, offset.shape, 1)
+    for k in range(2):
+        at = slice(k * cells, (k + 1) * cells)
+        offset[:, at] = (
+            columns[...] - lax.broadcasted_iota(jnp.int32, columns.shape, 1) - k * cells
+        )
     size = received.shape[1]
     values = jnp.concatenate(
         [*terms(received[...]), jnp.ones((SUB, size), jnp.bfloat16)], axis=0
@@ -214,7 +223,7 @@
         low[g], high[g] = lax.fori_loop(0, per, edge, (empty, empty), unroll=True)
 
 
-def merge(strip, arrival, received):
+def merge(columns, arrival, received):
     count, chan, cells = arrival.shape
     edge = jax.ShapeDtypeStruct((count * WIDTH // cells, chan, cells), F32)
     return pl.pallas_call(
@@ -222,10 +231,10 @@
         out_shape=(jax.ShapeDtypeStruct(arrival.shape, F32), edge, edge),
         in_specs=[whole(), whole(), whole()],
         out_specs=(whole(),) * 3,
-        scratch_shapes=[pltpu.VMEM((strip.shape[0], 2 * cells), jnp.int32)],
-        compiler_params=params(),
+        scratch_shapes=[pltpu.VMEM((columns.shape[0], 2 * cells), jnp.int32)],
+        compiler_params=params(16),
         name="merge",
-    )(strip, arrival, received)
+    )(columns, arrival, received)
 
 
 def edge_rows_kernel(merged, left, right, first, last):
@@ -247,7 +256,7 @@
         out_shape=(rows, rows),
         in_specs=[whole(), whole(), whole()],
         out_specs=(whole(), whole()),
-        compiler_params=params(),
+        compiler_params=params(8),
         name="edge_rows",
     )(merged, left, right)
 
@@ -382,7 +391,7 @@
         + [pltpu.VMEM((2 * WIDTH, chan, cells), F32)]
         + [held] * 2
         + [pltpu.SemaphoreType.DMA((chan // SUB,))],
-        compiler_params=params(),
+        compiler_params=params(32),
         name="relax",
     )(inside, merged, above, below, left, right, coef)
 
@@ -407,13 +416,13 @@
     chan = tile.shape[1]
     outgoing = pack_blocks(send_block[0, 0].T, tile)
     arrived = lax.all_to_all(outgoing, ("gx", "gy"), split_axis=0, concat_axis=0, tiled=True)
-    coupled = couple(tile, vertical_mix.T)
+    coupled, columns = prepare(tile, vertical_mix.T, strip_into[0])
     slots = arrived.reshape((-1,) + tile.shape[1:])
     arrival, picked = arrive(
         row_source, strip_from[0], slots, coupled, depart_cell[0], depart_frac[0]
     )
     received = lax.ppermute(picked, "panel", [(0, 1), (1, 0)])
-    merged, low, high = merge(strip_into[0].T, arrival, received)
+    merged, low, high = merge(columns, arrival, received)
     right = shifted(low, "gy", -1)
     left = shifted(high, "gy", 1)
     first, last = edge_rows(merged, left, right)

time: 174 us -> 172 us (0.989)
  local copies, waits for them, and re-layouts: 2.72 us -> 0.21 us
    unnamed x21 -> x17, local copies, waits for them, and re-layouts: 2.48 us -> 0.12 us
where the time goes in v6:
time: 172 us; the launch traced here: 170 us
  waiting for transfers between devices  122 us (71%)
  Pallas kernels  23.8 us (14%)
  starting transfers between devices  23.7 us (14%)
    all_to_all x1, waiting for transfers between devices, local(): lax.all_to_all(outgoing, ('gx', 'gy'), split_axis=0, concat_axis=0, tiled...  115 us
    all_to_all x1, starting transfers between devices, local(): lax.all_to_all(outgoing, ('gx', 'gy'), split_axis=0, concat_axis=0, tiled...  16.1 us
    pallas_call x1, Pallas kernels, relax(): pl.pallas_call(relax_kernel, out_shape=jax.ShapeDtypeStruct(merged.shape,...  8.96 us
    ppermute x4, starting transfers between devices, shifted(): lax.ppermute(block, axis, [(i, (i + step) % count) for i in range(count)])  7.5 us
    ppermute x4, waiting for transfers between devices, shifted(): lax.ppermute(block, axis, [(i, (i + step) % count) for i in range(count)])  6.24 us
    pallas_call x1, Pallas kernels, arrive(): pl.pallas_call(arrive_kernel, out_shape=(jax.ShapeDtypeStruct(coupled.sha...  6.06 us
    pallas_call x1, Pallas kernels, prepare(): pl.pallas_call(prepare_kernel, out_shape=(jax.ShapeDtypeStruct(tile.shape...  4.35 us
  transfers between devices with their start and end apart: 6, of which 4 were waited for; matrix products, arithmetic and copies ran while one was open for 0% of the time, Pallas kernels for 3%

profile of v6, /device:TPU:2, one launch (start us, length us, event | category | flops | bytes accessed | tf_op | source)
XLA Modules:
  0.0 170.3 jit_solution(14721579285017312620)
XLA Ops:
  0.0 2.6 %pack_blocks.1 = f32[128,2,40,128]{3,2,1,0:T(8,128)} custom-call(s32[2,128]{1,0:T(2,128)} %bitcast.23, f32[64,40,128]{2,1,0:T(8,128)} %bitcast.16), custom_call_target="tpu_custom_call" | custom-call | tf_op jit(solution)/shard_map/pack_blocks/pallas_call | solution.py:80
  2.7 0.0 copy-start.6
  2.7 0.0 copy-start
  2.7 0.0 copy-start.4
  2.7 16.1 %all-to-all-start = ((f32[128,2,40,128]{3,2,1,0:T(8,128)}), f32[128,2,40,128]{3,2,1,0:T(8,128)}, u32[]{:S(2)}, u32[]{:S(2)}) async-start(f32[128,2,40,128]{3,2,1,0:T(8,128)} %pack_blocks.1), calls=%async_computation | async-start | bytes 10485760 | tf_op jit(solution)/shard_map/all_to_all | solution.py:418
  18.8 0.0 copy-done.6
  18.8 0.0 copy-start.1
  18.8 0.0 copy-start.2
  18.8 0.0 copy-start.3
  18.8 0.0 copy-start.5
  18.8 0.1 copy.10
  18.9 0.0 copy-done
  18.9 0.0 copy-done.4
  18.9 4.3 %prepare.1 = (f32[64,40,128]{2,1,0:T(8,128)S(1)}, s32[512,128]{1,0:T(8,128)S(1)}) custom-call(f32[64,40,128]{2,1,0:T(8,128)S(1)} %bitcast.17, f32[40,40]{1,0:T(8,128)S(1)} %bitcast.18, s32[1,512]{1,0:T(1,128)S(1)} %bitcast.22), custom_call_target="tpu_custom_call" | custom-call | flops 157286400 | bytes 2621440 | tf_op jit(solution)/shard_map/prepare/pallas_call | solution.py:110
  23.3 114.7 %all-to-all-done = f32[128,2,40,128]{3,2,1,0:T(8,128)} async-done(((f32[128,2,40,128]{3,2,1,0:T(8,128)}), f32[128,2,40,128]{3,2,1,0:T(8,128)}, u32[]{:S(2)}, u32[]{:S(2)}) %all-to-all-start) | async-done | bytes 5242912 | tf_op jit(solution)/shard_map/all_to_all | solution.py:418
  138.0 0.0 copy-done.5
  138.0 6.1 %arrive.1 = (f32[64,40,128]{2,1,0:T(8,128)S(1)}, f32[40,512]{1,0:T(8,128)S(1)}) custom-call(s32[1,64]{1,0:T(1,128)S(1)} %copy-done.5, s32[1,512]{1,0:T(1,128)S(1)} %bitcast.21, f32[256,40,128]{2,1,0:T(8,128)} %bitcast.10.slots, f32[64,40,128]{2,1,0:T(8,128)S(1)} %get-tuple-element.15.coupled, s32[64,128]{1,0:T(8,128)S(1)} %bitcast.19, f32[64,128]{1,0:T(8,128)S(1)} %bitcast.20), custom_call_target="tpu_custom_call" | custom-call | tf_op jit(solution)/shard_map/arrive/pallas_call | solution.py:173
  144.1 0.1 collective-permute-start
  144.2 1.3 collective-permute-done.received
  145.5 1.7 merge.1
  147.2 0.6 collective-permute-start.1
  147.8 2.7 %collective-permute-start.2 = (f32[4,40,128]{2,1,0:T(8,128)S(1)}, f32[4,40,128]{2,1,0:T(8,128)S(1)}, u32[]{:S(2)}, u32[]{:S(2)}) collective-permute-start(f32[4,40,128]{2,1,0:T(8,128)S(1)} %get-tuple-element.20), channel_id=1, source_target_pairs={{0,3},{1,0},{2,1},{3,2},{4,7},{5,4},{6,5},{7,6},{8,11},{9,8},{10,9... | collective-permute-start | bytes 245768 | tf_op jit(solution)/shard_map/ppermute | solution.py:401
  150.5 2.5 %collective-permute-done.1.left = f32[4,40,128]{2,1,0:T(8,128)S(1)} collective-permute-done((f32[4,40,128]{2,1,0:T(8,128)S(1)}, f32[4,40,128]{2,1,0:T(8,128)S(1)}, u32[]{:S(2)}, u32[]{:S(2)}) %collective-permute-start.1) | collective-permute-done | bytes 81952 | tf_op jit(solution)/shard_map/ppermute | solution.py:401
  153.0 0.0 collective-permute-done.2.right
  153.0 0.1 edge_rows.1
  153.1 0.3 collective-permute-start.3
  153.4 3.9 %collective-permute-start.4 = (f32[9,40,128]{2,1,0:T(8,128)S(1)}, f32[9,40,128]{2,1,0:T(8,128)S(1)}, u32[]{:S(2)}, u32[]{:S(2)}) collective-permute-start(f32[9,40,128]{2,1,0:T(8,128)S(1)} %get-tuple-element.22), channel_id=1, source_target_pairs={{0,124},{4,0},{8,4},{12,8},{16,12},{20,16},{24,20},{28,24},{32,28}... | collective-permute-start | bytes 552968 | tf_op jit(solution)/shard_map/ppermute | solution.py:401
  157.3 0.1 copy.11.coef
  157.4 0.1 add_convert_fusion.inside
  157.4 3.7 %collective-permute-done.3.above = f32[9,40,128]{2,1,0:T(8,128)S(1)} collective-permute-done((f32[9,40,128]{2,1,0:T(8,128)S(1)}, f32[9,40,128]{2,1,0:T(8,128)S(1)}, u32[]{:S(2)}, u32[]{:S(2)}) %collective-permute-start.3) | collective-permute-done | bytes 184352 | tf_op jit(solution)/shard_map/ppermute | solution.py:401
  161.2 0.0 collective-permute-done.4.below
  161.2 9.0 %relax.1 = f32[64,40,128]{2,1,0:T(8,128)} custom-call(s32[4]{0:T(128)S(1)} %add_convert_fusion.inside, f32[64,40,128]{2,1,0:T(8,128)S(1)} %get-tuple-element.18.merged, f32[9,40,128]{2,1,0:T(8,128)S(1)} %collective-permute-done.3.above, f32[9,40,128]{2,1,0:T(8,128)S(1)} %collective-permute-done.4.below, f32[4,40,128]{2,1,0:T(8,128)S(1)} %collective-permute-done.1.left, ...), custom_call_target="tpu_custom_call" | custom-call | tf_op jit(solution)/shard_map/relax/pallas_call | solution.py:384
  (5 shorter events, 0.0 us)
Async XLA Ops:
  2.7 16.1 %copy-start.6 = (f32[40,40]{1,0:T(8,128)S(1)}, f32[40,40]{1,0:T(8,128)}, u32[]{:S(2)}) copy-start(f32[40,40]{1,0:T(8,128)} %param.17) | copy-start | bytes 19204
  2.7 16.3 %copy-start = (f32[1,64,40,128]{3,2,1,0:T(8,128)S(1)}, f32[1,64,40,128]{3,2,1,0:T(8,128)}, u32[]{:S(2)}) copy-start(f32[1,64,40,128]{3,2,1,0:T(8,128)} %param.9) | copy-start | bytes 3932164
  2.7 16.2 %copy-start.4 = (s32[1,1,512]{2,1,0:T(1,128)S(1)}, s32[1,1,512]{2,1,0:T(1,128)}, u32[]{:S(2)}) copy-start(s32[1,1,512]{2,1,0:T(1,128)} %param.15) | copy-start | bytes 6148
  2.7 135.3 %all-to-all-start = ((f32[128,2,40,128]{3,2,1,0:T(8,128)}), f32[128,2,40,128]{3,2,1,0:T(8,128)}, u32[]{:S(2)}, u32[]{:S(2)}) async-start(f32[128,2,40,128]{3,2,1,0:T(8,128)} %pack_blocks.1), calls=%async_computation | async-start | bytes 10485760 | tf_op jit(solution)/shard_map/all_to_all | solution.py:418
  18.8 119.2 %copy-start.1 = (s32[1,64,128]{2,1,0:T(8,128)S(1)}, s32[1,64,128]{2,1,0:T(8,128)}, u32[]{:S(2)}) copy-start(s32[1,64,128]{2,1,0:T(8,128)} %param.11) | copy-start | bytes 98308
  18.8 119.2 %copy-start.2 = (f32[1,64,128]{2,1,0:T(8,128)S(1)}, f32[1,64,128]{2,1,0:T(8,128)}, u32[]{:S(2)}) copy-start(f32[1,64,128]{2,1,0:T(8,128)} %param.10) | copy-start | bytes 98308
  18.8 119.2 %copy-start.3 = (s32[1,1,512]{2,1,0:T(1,128)S(1)}, s32[1,1,512]{2,1,0:T(1,128)}, u32[]{:S(2)}) copy-start(s32[1,1,512]{2,1,0:T(1,128)} %param.14) | copy-start | bytes 6148
  18.8 119.2 %copy-start.5 = (s32[1,64]{1,0:T(1,128)S(1)}, s32[1,64]{1,0:T(1,128)}, u32[]{:S(2)}) copy-start(s32[1,64]{1,0:T(1,128)} %rows.1) | copy-start | bytes 772
  144.1 1.4 collective-permute-start
  145.5 11.8 %copy-start.7 = (f32[40]{0:T(128)S(1)}, f32[40]{0:T(128)}, u32[]{:S(2)}) copy-start(f32[40]{0:T(128)} %param.16) | copy-start | bytes 484
  147.2 5.8 %collective-permute-start.1 = (f32[4,40,128]{2,1,0:T(8,128)S(1)}, f32[4,40,128]{2,1,0:T(8,128)S(1)}, u32[]{:S(2)}, u32[]{:S(2)}) collective-permute-start(f32[4,40,128]{2,1,0:T(8,128)S(1)} %get-tuple-element.19), channel_id=1, source_target_pairs={{0,1},{1,2},{2,3},{3,0},{4,5},{5,6},{6,7},{7,4},{8,9},{9,10},{10,1... | collective-permute-start | bytes 245768 | tf_op jit(solution)/shard_map/ppermute | solution.py:401
  147.8 5.2 %collective-permute-start.2 = (f32[4,40,128]{2,1,0:T(8,128)S(1)}, f32[4,40,128]{2,1,0:T(8,128)S(1)}, u32[]{:S(2)}, u32[]{:S(2)}) collective-permute-start(f32[4,40,128]{2,1,0:T(8,128)S(1)} %get-tuple-element.20), channel_id=1, source_target_pairs={{0,3},{1,0},{2,1},{3,2},{4,7},{5,4},{6,5},{7,6},{8,11},{9,8},{10,9... | collective-permute-start | bytes 245768 | tf_op jit(solution)/shard_map/ppermute | solution.py:401
  153.1 8.1 %collective-permute-start.3 = (f32[9,40,128]{2,1,0:T(8,128)S(1)}, f32[9,40,128]{2,1,0:T(8,128)S(1)}, u32[]{:S(2)}, u32[]{:S(2)}) collective-permute-start(f32[9,40,128]{2,1,0:T(8,128)S(1)} %get-tuple-element.21), channel_id=1, source_target_pairs={{0,4},{4,8},{8,12},{12,16},{16,20},{20,24},{24,28},{28,32},{32,36}... | collective-permute-start | bytes 552968 | tf_op jit(solution)/shard_map/ppermute | solution.py:401
  153.4 7.8 %collective-permute-start.4 = (f32[9,40,128]{2,1,0:T(8,128)S(1)}, f32[9,40,128]{2,1,0:T(8,128)S(1)}, u32[]{:S(2)}, u32[]{:S(2)}) collective-permute-start(f32[9,40,128]{2,1,0:T(8,128)S(1)} %get-tuple-element.22), channel_id=1, source_target_pairs={{0,124},{4,0},{8,4},{12,8},{16,12},{20,16},{24,20},{28,24},{32,28}... | collective-permute-start | bytes 552968 | tf_op jit(solution)/shard_map/ppermute | solution.py:401

commit v7 on v6

--- a/solution.py
+++ b/solution.py
@@ -66,7 +66,7 @@
             sent = sent + jnp.where(filled, 1, 0)
         return sent
 
-    sent = lax.fori_loop(0, tiles, send, 0, unroll=4)
+    sent = lax.fori_loop(0, tiles, send, 0, unroll=16)
 
     def wait(_, carry):
         pltpu.make_async_copy(held.at[0], out.at[0, 0], sem).wait()
@@ -261,13 +261,45 @@
     )(merged, left, right)
 
 
+def unpack_kernel(inside, merged, left, right, coef, beside, ready0, ready1):
+    count, chan, cells = merged.shape
+    lane = lax.broadcasted_iota(jnp.int32, (chan, cells), 1)
+    is_right = lane < jnp.where(inside[3] > 0, WIDTH, 0)
+    is_left = lane >= jnp.where(inside[2] > 0, cells - WIDTH, cells)
+    inv = jnp.broadcast_to(1.0 / (1.0 + 4.0 * coef[...]), (chan, cells))
+    for r in range(count):
+        g, i = divmod(r, cells // WIDTH)
+        row = jnp.where(
+            is_right,
+            pltpu.roll(right[g], (-i * WIDTH) % cells, 1),
+            jnp.where(is_left, pltpu.roll(left[g], (-(i + 1) * WIDTH) % cells, 1), 0.0),
+        )
+        beside[r] = row
+        ready0[r] = merged[r] * inv
+        ready1[r] = row * inv
+
+
+def unpack(inside, merged, left, right, coef):
+    tile = jax.ShapeDtypeStruct(merged.shape, F32)
+    return pl.pallas_call(
+        unpack_kernel,
+        out_shape=(tile,) * 3,
+        in_specs=[whole(pltpu.SMEM)] + [whole()] * 4,
+        out_specs=(whole(),) * 3,
+        compiler_params=params(8),
+        cost_estimate=cost(8 * merged.size, 16 * merged.size),
+        name="unpack",
+    )(inside, merged, left, right, coef)
+
+
 def relax_kernel(
     inside,
     merged,
     above,
     below,
-    left,
-    right,
+    beside,
+    ready0,
+    ready1,
     coef,
     result,
     out,
@@ -288,7 +320,6 @@
     h = coef[...]
     inv = 1.0 / (1.0 + 4.0 * h)
     total = count + 2 * WIDTH
-    per = cells // WIDTH
     half = cells // 2
 
     for at, rows, flag in ((0, above, 0), (WIDTH, below, 1)):
@@ -301,13 +332,6 @@
                 pltpu.roll(packed, (-i * WIDTH) % cells, 1),
                 jnp.where(is_left, pltpu.roll(packed, (half - (i + 1) * WIDTH) % cells, 1), 0.0),
             )
-    for r in range(count):
-        g, i = divmod(r, per)
-        start1[WIDTH + r] = jnp.where(
-            is_right,
-            pltpu.roll(right[g], (-i * WIDTH) % cells, 1),
-            jnp.where(is_left, pltpu.roll(left[g], (-(i + 1) * WIDTH) % cells, 1), 0.0),
-        )
 
     lane8 = lax.broadcasted_iota(jnp.int32, (SUB, cells), 1)
     side = jnp.where(
@@ -319,6 +343,9 @@
     gap = (to - lax.broadcasted_iota(jnp.int32, (2 * cells, 2 * cells), 0)) & (2 * cells - 1)
     shift = jnp.where((gap == 1) | (gap == 2 * cells - 1), 1.0, 0.0).astype(jnp.bfloat16)
 
+    def side_row(x, ch):
+        return beside[x - WIDTH, ch] if WIDTH <= x < WIDTH + count else start1[x, ch]
+
     def first_row(x, ch):
         if x < WIDTH:
             return start0[x, ch]
@@ -330,7 +357,7 @@
         gain = jnp.broadcast_to(h[ch] * inv[ch], (SUB, cells))
         gain_side = gain * side
 
-        for x in range(total):
+        for x in (*range(WIDTH), *range(WIDTH + count, total)):
             scaled0[x, ch] = first_row(x, ch) * inv8
             scaled1[x, ch] = start1[x, ch] * inv8
 
@@ -340,20 +367,21 @@
 
             def held(x):
                 if s == 0:
-                    return first_row(x, ch), start1[x, ch]
+                    return first_row(x, ch), side_row(x, ch)
                 return now[0][x, ch], now[1][x, ch]
 
             def store(x, across):
                 part = lo if x < WIDTH else hi if x >= WIDTH + count else None
                 up, down = held(x - 1), held(x + 1)
                 g0 = gain if part is None else gain * part
-                new = scaled0[x, ch] + g0 * (up[0] + down[0] + across[0])
+                own = WIDTH <= x < WIDTH + count
+                new = (ready0[x - WIDTH, ch] if own else scaled0[x, ch]) + g0 * (up[0] + down[0] + across[0])
                 if s == SWEEPS - 1:
                     out[x - WIDTH, ch] = new
                 else:
                     later[0][x, ch] = new
                     g1 = gain_side if part is None else gain_side * part
-                    later[1][x, ch] = scaled1[x, ch] + g1 * (up[1] + down[1] + across[1])
+                    later[1][x, ch] = (ready1[x - WIDTH, ch] if own else scaled1[x, ch]) + g1 * (up[1] + down[1] + across[1])
 
             x = begin
             while x < end:
@@ -364,8 +392,9 @@
                 )
                 coarse = block.astype(jnp.bfloat16)
                 fine = (block - coarse.astype(F32)).astype(jnp.bfloat16)
-                across = jnp.dot(coarse, shift, preferred_element_type=F32) + jnp.dot(
-                    fine, shift, preferred_element_type=F32
+                ways = shift[:, :cells] if s == SWEEPS - 1 else shift
+                across = jnp.dot(coarse, ways, preferred_element_type=F32) + jnp.dot(
+                    fine, ways, preferred_element_type=F32
                 )
                 for y in range(x, x1):
                     at = slice((y - x) * SUB, (y - x + 1) * SUB)
@@ -378,13 +407,13 @@
         pltpu.make_async_copy(out.at[:, ch], result.at[:, ch], sem.at[c // SUB]).wait()
 
 
-def relax(inside, merged, above, below, left, right, coef):
+def relax(inside, merged, above, below, beside, ready0, ready1, coef):
     count, chan, cells = merged.shape
     held = pltpu.VMEM((count + 2 * WIDTH, chan, cells), F32)
     return pl.pallas_call(
         relax_kernel,
         out_shape=jax.ShapeDtypeStruct(merged.shape, F32),
-        in_specs=[whole(pltpu.SMEM)] + [whole()] * 6,
+        in_specs=[whole(pltpu.SMEM)] + [whole()] * 7,
         out_specs=whole(pl.ANY),
         scratch_shapes=[pltpu.VMEM(merged.shape, F32)]
         + [held] * 5
@@ -393,7 +422,7 @@
         + [pltpu.SemaphoreType.DMA((chan // SUB,))],
         compiler_params=params(32),
         name="relax",
-    )(inside, merged, above, below, left, right, coef)
+    )(inside, merged, above, below, beside, ready0, ready1, coef)
 
 
 def shifted(block, axis, step):
@@ -425,21 +454,24 @@
     merged, low, high = merge(columns, arrival, received)
     right = shifted(low, "gy", -1)
     left = shifted(high, "gy", 1)
-    first, last = edge_rows(merged, left, right)
-    below = shifted(first, "gx", -1)
-    above = shifted(last, "gx", 1)
     gx, gy = lax.axis_index("gx"), lax.axis_index("gy")
     inside = jnp.stack(
         [gx > 0, gx < lax.axis_size("gx") - 1, gy > 0, gy < lax.axis_size("gy") - 1]
     ).astype(jnp.int32)
+    coef = helmholtz_coef.reshape(chan, 1)
+    first, last = edge_rows(merged, left, right)
+    below = shifted(first, "gx", -1)
+    above = shifted(last, "gx", 1)
+    beside, ready0, ready1 = unpack(inside, merged, left, right, coef)
     balanced = relax(
         inside,
         merged,
         above,
         below,
-        left,
-        right,
-        helmholtz_coef.reshape(chan, 1),
+        beside,
+        ready0,
+        ready1,
+        coef,
     )
     return balanced[None]
 

time: 172 us -> 172 us (level)
  no operation moved by 1% of the time
where the time goes in v7:
time: 172 us; the launch traced here: 171 us
  waiting for transfers between devices  121 us (70%)
  Pallas kernels  25.2 us (15%)
  starting transfers between devices  23.8 us (14%)
    all_to_all x1, waiting for transfers between devices, local(): lax.all_to_all(outgoing, ('gx', 'gy'), split_axis=0, concat_axis=0, tiled...  115 us
    all_to_all x1, starting transfers between devices, local(): lax.all_to_all(outgoing, ('gx', 'gy'), split_axis=0, concat_axis=0, tiled...  16.2 us
    pallas_call x1, Pallas kernels, relax(): pl.pallas_call(relax_kernel, out_shape=jax.ShapeDtypeStruct(merged.shape,...  9.19 us
    ppermute x4, starting transfers between devices, shifted(): lax.ppermute(block, axis, [(i, (i + step) % count) for i in range(count)])  7.5 us
    pallas_call x1, Pallas kernels, arrive(): pl.pallas_call(arrive_kernel, out_shape=(jax.ShapeDtypeStruct(coupled.sha...  6.09 us
    ppermute x4, waiting for transfers between devices, shifted(): lax.ppermute(block, axis, [(i, (i + step) % count) for i in range(count)])  4.87 us
    pallas_call x1, Pallas kernels, prepare(): pl.pallas_call(prepare_kernel, out_shape=(jax.ShapeDtypeStruct(tile.shape...  4.35 us
  transfers between devices with their start and end apart: 6, of which 4 were waited for; matrix products, arithmetic and copies ran while one was open for 0% of the time, Pallas kernels for 3%

profile of v7, /device:TPU:2, one launch (start us, length us, event | category | flops | bytes accessed | tf_op | source)
XLA Modules:
  0.0 170.5 jit_solution(11080897363711558818)
XLA Ops:
  0.0 2.5 %pack_blocks.1 = f32[128,2,40,128]{3,2,1,0:T(8,128)} custom-call(s32[2,128]{1,0:T(2,128)} %bitcast.23, f32[64,40,128]{2,1,0:T(8,128)} %bitcast.16), custom_call_target="tpu_custom_call" | custom-call | tf_op jit(solution)/shard_map/pack_blocks/pallas_call | solution.py:80
  2.5 0.0 copy-start.6
  2.6 0.0 copy-start
  2.6 0.0 copy-start.4
  2.6 16.2 %all-to-all-start = ((f32[128,2,40,128]{3,2,1,0:T(8,128)}), f32[128,2,40,128]{3,2,1,0:T(8,128)}, u32[]{:S(2)}, u32[]{:S(2)}) async-start(f32[128,2,40,128]{3,2,1,0:T(8,128)} %pack_blocks.1), calls=%async_computation | async-start | bytes 10485760 | tf_op jit(solution)/shard_map/all_to_all | solution.py:447
  18.8 0.0 copy-start.1
  18.8 0.0 copy-start.2
  18.8 0.0 copy-start.3
  18.8 0.0 copy-start.5
  18.8 0.1 copy.10
  18.9 0.0 copy-done.4
  18.9 4.3 %prepare.1 = (f32[64,40,128]{2,1,0:T(8,128)S(1)}, s32[512,128]{1,0:T(8,128)S(1)}) custom-call(f32[64,40,128]{2,1,0:T(8,128)S(1)} %bitcast.17, f32[40,40]{1,0:T(8,128)S(1)} %bitcast.18, s32[1,512]{1,0:T(1,128)S(1)} %bitcast.22), custom_call_target="tpu_custom_call" | custom-call | flops 157286400 | bytes 2621440 | tf_op jit(solution)/shard_map/prepare/pallas_call | solution.py:110
  23.2 114.8 %all-to-all-done = f32[128,2,40,128]{3,2,1,0:T(8,128)} async-done(((f32[128,2,40,128]{3,2,1,0:T(8,128)}), f32[128,2,40,128]{3,2,1,0:T(8,128)}, u32[]{:S(2)}, u32[]{:S(2)}) %all-to-all-start) | async-done | bytes 5242912 | tf_op jit(solution)/shard_map/all_to_all | solution.py:447
  138.0 0.0 copy-done.1
  138.1 0.0 copy-done.3
  138.1 6.1 %arrive.1 = (f32[64,40,128]{2,1,0:T(8,128)S(1)}, f32[40,512]{1,0:T(8,128)S(1)}) custom-call(s32[1,64]{1,0:T(1,128)S(1)} %copy-done.5, s32[1,512]{1,0:T(1,128)S(1)} %bitcast.21, f32[256,40,128]{2,1,0:T(8,128)} %bitcast.10.slots, f32[64,40,128]{2,1,0:T(8,128)S(1)} %get-tuple-element.18.coupled, s32[64,128]{1,0:T(8,128)S(1)} %bitcast.19, f32[64,128]{1,0:T(8,128)S(1)} %bitcast.20), custom_call_target="tpu_custom_call" | custom-call | tf_op jit(solution)/shard_map/arrive/pallas_call | solution.py:173
  144.2 0.1 collective-permute-start
  144.3 1.3 collective-permute-done.received
  145.5 1.7 %merge.1 = (f32[64,40,128]{2,1,0:T(8,128)S(1)}, f32[4,40,128]{2,1,0:T(8,128)S(1)}, f32[4,40,128]{2,1,0:T(8,128)S(1)}) custom-call(s32[512,128]{1,0:T(8,128)S(1)} %get-tuple-element.17.columns, f32[64,40,128]{2,1,0:T(8,128)S(1)} %get-tuple-element.19.arrival, f32[40,512]{1,0:T(8,128)S(1)} %collective-permute-done.received), custom_call_target="tpu_custom_call" | custom-call | tf_op jit(solution)/shard_map/merge/pallas_call | solution.py:229
  147.2 0.5 collective-permute-start.1
  147.8 2.8 %collective-permute-start.2 = (f32[4,40,128]{2,1,0:T(8,128)S(1)}, f32[4,40,128]{2,1,0:T(8,128)S(1)}, u32[]{:S(2)}, u32[]{:S(2)}) collective-permute-start(f32[4,40,128]{2,1,0:T(8,128)S(1)} %get-tuple-element.23), channel_id=1, source_target_pairs={{0,3},{1,0},{2,1},{3,2},{4,7},{5,4},{6,5},{7,6},{8,11},{9,8},{10,9... | collective-permute-start | bytes 245768 | tf_op jit(solution)/shard_map/ppermute | solution.py:430
  150.6 2.5 %collective-permute-done.1.left = f32[4,40,128]{2,1,0:T(8,128)S(1)} collective-permute-done((f32[4,40,128]{2,1,0:T(8,128)S(1)}, f32[4,40,128]{2,1,0:T(8,128)S(1)}, u32[]{:S(2)}, u32[]{:S(2)}) %collective-permute-start.1) | collective-permute-done | bytes 81952 | tf_op jit(solution)/shard_map/ppermute | solution.py:430
  153.0 0.0 collective-permute-done.2.right
  153.1 0.1 edge_rows.1
  153.1 0.2 collective-permute-start.3
  153.3 4.0 %collective-permute-start.4 = (f32[9,40,128]{2,1,0:T(8,128)S(1)}, f32[9,40,128]{2,1,0:T(8,128)S(1)}, u32[]{:S(2)}, u32[]{:S(2)}) collective-permute-start(f32[9,40,128]{2,1,0:T(8,128)S(1)} %get-tuple-element.25), channel_id=1, source_target_pairs={{0,124},{4,0},{8,4},{12,8},{16,12},{20,16},{24,20},{28,24},{32,28}... | collective-permute-start | bytes 552968 | tf_op jit(solution)/shard_map/ppermute | solution.py:430
  157.3 0.1 copy.11.coef
  157.4 0.1 add_convert_fusion.inside
  157.5 1.3 unpack.1
  158.8 2.4 %collective-permute-done.3.above = f32[9,40,128]{2,1,0:T(8,128)S(1)} collective-permute-done((f32[9,40,128]{2,1,0:T(8,128)S(1)}, f32[9,40,128]{2,1,0:T(8,128)S(1)}, u32[]{:S(2)}, u32[]{:S(2)}) %collective-permute-start.3) | collective-permute-done | bytes 184352 | tf_op jit(solution)/shard_map/ppermute | solution.py:430
  161.2 0.0 collective-permute-done.4.below
  161.2 9.2 %relax.1 = f32[64,40,128]{2,1,0:T(8,128)} custom-call(s32[4]{0:T(128)S(1)} %add_convert_fusion.inside, f32[64,40,128]{2,1,0:T(8,128)S(1)} %get-tuple-element.21.merged, f32[9,40,128]{2,1,0:T(8,128)S(1)} %collective-permute-done.3.above, f32[9,40,128]{2,1,0:T(8,128)S(1)} %collective-permute-done.4.below, f32[64,40,128]{2,1,0:T(8,128)S(1)} %get-tuple-element.26.beside, ...), custom_call_target="tpu_custom_call" | custom-call | tf_op jit(solution)/shard_map/relax/pallas_call | solution.py:413
  (6 shorter events, 0.0 us)
Async XLA Ops:
  2.5 16.2 %copy-start.6 = (f32[40,40]{1,0:T(8,128)S(1)}, f32[40,40]{1,0:T(8,128)}, u32[]{:S(2)}) copy-start(f32[40,40]{1,0:T(8,128)} %param.17) | copy-start | bytes 19204
  2.6 16.3 %copy-start = (f32[1,64,40,128]{3,2,1,0:T(8,128)S(1)}, f32[1,64,40,128]{3,2,1,0:T(8,128)}, u32[]{:S(2)}) copy-start(f32[1,64,40,128]{3,2,1,0:T(8,128)} %param.9) | copy-start | bytes 3932164
  2.6 16.3 %copy-start.4 = (s32[1,1,512]{2,1,0:T(1,128)S(1)}, s32[1,1,512]{2,1,0:T(1,128)}, u32[]{:S(2)}) copy-start(s32[1,1,512]{2,1,0:T(1,128)} %param.15) | copy-start | bytes 6148
  2.6 135.5 %all-to-all-start = ((f32[128,2,40,128]{3,2,1,0:T(8,128)}), f32[128,2,40,128]{3,2,1,0:T(8,128)}, u32[]{:S(2)}, u32[]{:S(2)}) async-start(f32[128,2,40,128]{3,2,1,0:T(8,128)} %pack_blocks.1), calls=%async_computation | async-start | bytes 10485760 | tf_op jit(solution)/shard_map/all_to_all | solution.py:447
  18.8 119.3 %copy-start.1 = (s32[1,64,128]{2,1,0:T(8,128)S(1)}, s32[1,64,128]{2,1,0:T(8,128)}, u32[]{:S(2)}) copy-start(s32[1,64,128]{2,1,0:T(8,128)} %param.11) | copy-start | bytes 98308
  18.8 119.3 %copy-start.2 = (f32[1,64,128]{2,1,0:T(8,128)S(1)}, f32[1,64,128]{2,1,0:T(8,128)}, u32[]{:S(2)}) copy-start(f32[1,64,128]{2,1,0:T(8,128)} %param.10) | copy-start | bytes 98308
  18.8 119.3 %copy-start.3 = (s32[1,1,512]{2,1,0:T(1,128)S(1)}, s32[1,1,512]{2,1,0:T(1,128)}, u32[]{:S(2)}) copy-start(s32[1,1,512]{2,1,0:T(1,128)} %param.14) | copy-start | bytes 6148
  18.8 119.3 %copy-start.5 = (s32[1,64]{1,0:T(1,128)S(1)}, s32[1,64]{1,0:T(1,128)}, u32[]{:S(2)}) copy-start(s32[1,64]{1,0:T(1,128)} %rows.1) | copy-start | bytes 772
  144.2 1.4 collective-permute-start
  145.5 11.8 %copy-start.7 = (f32[40]{0:T(128)S(1)}, f32[40]{0:T(128)}, u32[]{:S(2)}) copy-start(f32[40]{0:T(128)} %param.16) | copy-start | bytes 484
  147.2 5.8 %collective-permute-start.1 = (f32[4,40,128]{2,1,0:T(8,128)S(1)}, f32[4,40,128]{2,1,0:T(8,128)S(1)}, u32[]{:S(2)}, u32[]{:S(2)}) collective-permute-start(f32[4,40,128]{2,1,0:T(8,128)S(1)} %get-tuple-element.22), channel_id=1, source_target_pairs={{0,1},{1,2},{2,3},{3,0},{4,5},{5,6},{6,7},{7,4},{8,9},{9,10},{10,1... | collective-permute-start | bytes 245768 | tf_op jit(solution)/shard_map/ppermute | solution.py:430
  147.8 5.3 %collective-permute-start.2 = (f32[4,40,128]{2,1,0:T(8,128)S(1)}, f32[4,40,128]{2,1,0:T(8,128)S(1)}, u32[]{:S(2)}, u32[]{:S(2)}) collective-permute-start(f32[4,40,128]{2,1,0:T(8,128)S(1)} %get-tuple-element.23), channel_id=1, source_target_pairs={{0,3},{1,0},{2,1},{3,2},{4,7},{5,4},{6,5},{7,6},{8,11},{9,8},{10,9... | collective-permute-start | bytes 245768 | tf_op jit(solution)/shard_map/ppermute | solution.py:430
  153.1 8.0 %collective-permute-start.3 = (f32[9,40,128]{2,1,0:T(8,128)S(1)}, f32[9,40,128]{2,1,0:T(8,128)S(1)}, u32[]{:S(2)}, u32[]{:S(2)}) collective-permute-start(f32[9,40,128]{2,1,0:T(8,128)S(1)} %get-tuple-element.24), channel_id=1, source_target_pairs={{0,4},{4,8},{8,12},{12,16},{16,20},{20,24},{24,28},{28,32},{32,36}... | collective-permute-start | bytes 552968 | tf_op jit(solution)/shard_map/ppermute | solution.py:430
  153.3 7.9 %collective-permute-start.4 = (f32[9,40,128]{2,1,0:T(8,128)S(1)}, f32[9,40,128]{2,1,0:T(8,128)S(1)}, u32[]{:S(2)}, u32[]{:S(2)}) collective-permute-start(f32[9,40,128]{2,1,0:T(8,128)S(1)} %get-tuple-element.25), channel_id=1, source_target_pairs={{0,124},{4,0},{8,4},{12,8},{16,12},{20,16},{24,20},{28,24},{32,28}... | collective-permute-start | bytes 552968 | tf_op jit(solution)/shard_map/ppermute | solution.py:430
